TPU v7x, 128 devices: a whole 4x4x4 slice. The times are simulated.
128 devices in a mesh: lists: 32 (over x, z, core), sub: 4 (over y).
Axes of the slice: x: 4, y: 4, z: 4, core: 2. Of those that a mesh axis runs over, the one named last changes fastest.
Arguments:
- embeddings: bfloat16 [262144, 1024], P(('lists', 'sub')), may hold values from -6 to 6
- owner_of_row: int32 [262144, 1], P(('lists', 'sub')), may hold values from 0 to 31; in each aligned block of 2048 rows (0 to 2047, 2048 to 4095, ...) at most 128 rows name the same one
- list_in_owner: int32 [262144], P(('lists', 'sub')), may hold values from 0 to 2047
- opq_matrix: bfloat16 [1024, 1024], replicated, may hold values from -0.1875 to 0.1875
- centroids: bfloat16 [65536, 1024], P('lists', 'sub'), may hold values from -5 to 5
- codebook: bfloat16 [64, 16, 256], P('sub'), may hold values from -5 to 5
- code_targets: int32 [64, 524288], P('sub', 'lists'), may hold values from 0 to 255
Outputs:
- quant_error: float32 [64, 524288], P('sub', 'lists')
- new_codebook: float32 [64, 16, 256], P('sub')
Inputs may be any that keep to these rules, and one draw needn't show every extreme that they name: `owner_of_row`: no more than 128 of the 2048 rows of one device name the same owner; some device sends exactly 128 rows to one owner.
All inputs are finite; a program needn't handle non-finite values.
Results may differ from a plain program's by a relative error of at most 0.0039.
Values may be sent and summed in bfloat16 or wider, within the bound.
No kernel may reach another device: no remote copies, remote signals or barrier semaphores. Data moves between devices by JAX's collectives and lax.ppermute only.
A program may use at most 128 MiB of HBM per device.

v0:
```python
import jax
import jax.numpy as jnp
from jax import lax
from jax.sharding import PartitionSpec as P


def per_device(
    embeddings, owner_of_row, list_in_owner, opq_matrix, centroids, codebook, code_targets
):
    rows = embeddings.shape[0]
    width = embeddings.shape[1]
    owners = lax.axis_size("lists")
    groups = lax.axis_size("sub")
    capacity = max(2, 2 * rows // owners)
    rotated = jnp.dot(embeddings, opq_matrix, preferred_element_type=jnp.float32).astype(
        jnp.bfloat16
    )
    owner = owner_of_row[:, 0]
    onehot = (owner[:, None] == jnp.arange(owners, dtype=jnp.int32)[None, :]).astype(jnp.int32)
    rank = jnp.sum((jnp.cumsum(onehot, axis=0) - onehot) * onehot, axis=1)
    target = owner * capacity + rank
    send_rows = jnp.zeros((owners * capacity, width), jnp.bfloat16).at[target].set(rotated)
    send_ids = jnp.full((owners * capacity,), -1, jnp.int32).at[target].set(list_in_owner)
    send_rows = send_rows.reshape(1, owners, capacity, width)
    send_ids = jnp.broadcast_to(
        send_ids.reshape(1, owners, capacity, 1), (1, owners, capacity, groups)
    )
    moved_rows, moved_ids = (
        lax.all_to_all(send_rows, "lists", split_axis=1, concat_axis=1, tiled=True),
        lax.all_to_all(send_ids, "lists", split_axis=1, concat_axis=1, tiled=True),
    )
    got_rows, got_ids = (
        lax.all_to_all(moved_rows, "sub", split_axis=3, concat_axis=0, tiled=True),
        lax.all_to_all(moved_ids, "sub", split_axis=3, concat_axis=0, tiled=True),
    )
    total_slots = groups * owners * capacity
    slab = got_rows.reshape(total_slots, width // groups)
    list_ids = got_ids.reshape(total_slots)
    live = list_ids >= 0
    picked = centroids[jnp.maximum(list_ids, 0)]
    resid = jnp.where(
        live[:, None], slab.astype(jnp.float32) - picked.astype(jnp.float32), 0.0
    ).astype(jnp.bfloat16)
    local_subs = codebook.shape[0]
    sub_dims = codebook.shape[1]
    code_count = codebook.shape[2]
    code_f = codebook.astype(jnp.float32)
    code_sq = jnp.sum(code_f * code_f, axis=1)
    code_iota = jnp.arange(code_count, dtype=jnp.int32)
    block = min(2048, total_slots)
    blocks = total_slots // block
    resid_blocks = resid.reshape(blocks, block, local_subs, sub_dims)
    code_blocks = code_targets.reshape(local_subs, blocks, block).transpose(1, 0, 2)
    live_blocks = live.reshape(blocks, block)

    def step(carry, items):
        sums, counts = carry
        part, targets, alive = items
        part_f = part.astype(jnp.float32)
        row_sq = jnp.sum(part_f * part_f, axis=2).T
        dots = jnp.einsum("nmd,mdk->mnk", part, codebook, preferred_element_type=jnp.float32)
        dist = row_sq[:, :, None] - 2.0 * dots + code_sq[:, None, :]
        error = jnp.where(alive[None, :], jnp.min(dist, axis=2), 0.0)
        hot = ((targets[:, :, None] == code_iota[None, None, :]) & alive[None, :, None]).astype(
            jnp.bfloat16
        )
        sums = sums + jnp.einsum("mnk,nmd->mdk", hot, part, preferred_element_type=jnp.float32)
        counts = counts + jnp.sum(hot.astype(jnp.float32), axis=1)
        return ((sums, counts), error)

    start = (
        jnp.zeros((local_subs, sub_dims, code_count), jnp.float32),
        jnp.zeros((local_subs, code_count), jnp.float32),
    )
    (sums, counts), errors = lax.scan(step, start, (resid_blocks, code_blocks, live_blocks))
    quant_error = errors.transpose(1, 0, 2).reshape(local_subs, total_slots)
    totals, tallies = lax.psum((sums, counts), "lists")
    new_codebook = (code_f + totals) / (1.0 + tallies[:, None, :])
    return (quant_error, new_codebook)


def solution(mesh):
    placed = (
        P(("lists", "sub"), None),
        P(("lists", "sub"), None),
        P(("lists", "sub")),
        P(),
        P("lists", "sub"),
        P("sub", None, None),
        P("sub", "lists"),
    )
    return jax.shard_map(
        per_device,
        mesh=mesh,
        in_specs=placed,
        out_specs=(P("sub", "lists"), P("sub", None, None)),
        check_vma=False,
    )
```

profile of v0, /device:TPU:1, one launch (start us, length us, event | category | flops | bytes accessed | tf_op | source)
XLA Modules:
  0.0 843.4 jit_solution(3716110875985533250)
XLA Ops:
  28.3 9.4 %all-to-all-start = ((s32[1,32,128,4]{2,3,0,1:T(4,128)}), s32[1,32,128,4]{2,3,0,1:T(4,128)S(1)}, u32[]{:S(2)}, u32[]{:S(2)}) async-start(s32[1,32,128,4]{2,3,0,1:T(4,128)} %broadcast_in_dim.65), calls=%async_computation | async-start | bytes 131072 | tf_op jit(solution)/shard_map/all_to_all | solution.py:30
  46.7 15.6 %scatter_custom_fusion.1 = bf16[4096,1024]{1,0:T(8,128)(2,1)} fusion(s32[2048]{0:T(1024)S(1)} %bitcast.111, f32[2048,1024]{1,0:T(8,128)} %fusion.29, bf16[]{:T(256)} %constant.16.clone.1), kind=kCustom, calls=%fused_computation.28 | custom fusion | flops 2097152 | bytes 16777218 | tf_op jit(solution)/shard_map/scatter | solution.py:22
  70.4 107.9 %all-to-all-done.2 = bf16[1,32,128,1024]{3,2,0,1:T(8,128)(2,1)} async-done(((bf16[1,32,128,1024]{3,2,0,1:T(8,128)(2,1)}), bf16[1,32,128,1024]{3,2,0,1:T(8,128)(2,1)}, u32[]{:S(2)}, u32[]{:S(2)}) %all-to-all-start.2) | async-done | bytes 8388640 | tf_op jit(solution)/shard_map/all_to_all | solution.py:29
  183.0 12.5 %copy.36 = bf16[1,32,128,1024]{2,1,0,3:T(8,128)(2,1)} copy(bf16[1,32,128,1024]{3,2,0,1:T(8,128)(2,1)} %all-to-all-done.2) | data formatting | bytes 16777216 | tf_op jit(solution)/shard_map/all_to_all | solution.py:29
  202.1 64.8 %gather_fusion = bf16[16384,256]{1,0:T(8,128)(2,1)} fusion(bf16[2048,256]{1,0:T(8,128)(2,1)S(1)} %copy-done.2, s32[16384]{0:T(1024)S(1)} %broadcast_clamp_fusion), kind=kCustom, calls=%fused_computation | custom fusion | bytes 16842752 | tf_op jit(solution)/shard_map/gather | solution.py:40
  267.0 12.2 %copy.39 = f32[16384,256]{0,1:T(8,128)} copy(bf16[16384,256]{1,0:T(8,128)(2,1)} %gather_fusion) | data formatting | bytes 25165824 | tf_op jit(solution)/shard_map/convert_element_type | solution.py:42
  279.2 18.6 %copy.47 = f32[32,8,8,2048]{3,2,1,0:T(8,128)} copy(f32[32,8,8,2048]{3,1,2,0:T(8,128)} %bitcast.93) | data formatting | bytes 33554432
  297.8 9.8 %copy.37 = bf16[1,32,128,1024]{2,3,1,0:T(8,128)(2,1)} copy(bf16[1,32,128,1024]{2,1,0,3:T(8,128)(2,1)} %all-to-all-done.3) | data formatting | bytes 16777216 | tf_op jit(solution)/shard_map/all_to_all | solution.py:33
  307.6 11.4 %convert_bitcast_fusion = f32[4,1,32,128,256]{3,4,0,2,1:T(8,128)} fusion(bf16[1,32,128,4,256]{2,4,3,1,0:T(8,128)(2,1)} %bitcast.94), kind=kLoop, calls=%fused_computation.26 | loop fusion | flops 4194304 | bytes 25165824 | tf_op jit(solution)/shard_map/convert_element_type | solution.py:42
  319.0 17.9 %copy.38 = f32[4,1,32,128,256]{3,2,0,4,1:T(8,128)} copy(f32[4,1,32,128,256]{3,4,0,2,1:T(8,128)} %convert_bitcast_fusion) | data formatting | bytes 33554432 | tf_op jit(solution)/shard_map/convert_element_type | solution.py:42
  336.9 18.0 %reshape.121 = f32[8,2048,16,16]{1,0,3,2:T(8,128)} reshape(f32[4,1,32,128,256]{3,2,0,4,1:T(8,128)} %copy.38) | data formatting | bytes 33554432 | tf_op jit(solution)/shard_map/convert_element_type | solution.py:42
  354.9 15.3 %select_convert_fusion = bf16[8,2048,16,16]{1,0,3,2:T(8,128)(2,1)} fusion(f32[8,2048,16,16]{1,0,3,2:T(8,128)} %reshape.121, f32[8,2048,16,16]{1,0,3,2:T(8,128)} %bitcast.92, pred[8,2048]{1,0:T(8,128)(4,1)S(1)} %ge.20), kind=kLoop, calls=%fused_computation.27 | loop fusion | flops 12582912 | bytes 41959424 | tf_op jit(solution)/shard_map/convert_element_type | solution.py:43
  370.2 11.2 %copy.40 = bf16[8,2048,16,16]{1,3,2,0:T(8,128)(2,1)} copy(bf16[8,2048,16,16]{1,0,3,2:T(8,128)(2,1)} %select_convert_fusion) | data formatting | bytes 16777216
  381.4 219.1 %while.15 = (s32[]{:T(128)}, f32[16,16,256]{2,1,0:T(8,128)}, f32[16,256]{1,0:T(8,128)S(1)}, f32[8,16,2048]{2,1,0:T(8,128)}, bf16[8,2048,16,16]{1,3,2,0:T(8,128)(...) while((s32[]{:T(128)}, f32[16,16,256]{2,1,0:T(8,128)}, ...), condition=%wide.region_10.11_spmd.clone, body=%wide.region_6.10_spmd.clone.sunk | while | flops 630820864 | bytes 5336708 | solution.py:75
  391.1 10.0 %fusion.43 = f32[16,16,256]{2,1,0:T(8,128)} fusion(s32[16,2048]{1,0:T(8,128)S(1)} %bitcast.97, pred[2048]{0:T(1024)(128)(4,1)S(1)} %dynamic-slice_reduce_fusion.2, bf16[8,2048,16,16]{1,3,2,0:T(8,128)(2,1)} %get-tuple-element.226, s32[]{:T(128)} %get-tuple-element.211, f32[16,16,256]{2,1,0:T(8,128)} %get-tuple-element.212, pred[]{:T(512)S(6)} %compare.3), kind=kOutput, calls=%fused_computation.13.clone.1 | convolution fusion | flops 285343744 | bytes 1706497 | tf_op jit(solution)/shard_map/while/body/eval_jaxpr/mnk,nmd->mdk/dot_general | solution.py:67
  418.3 10.1 %fusion.43 = f32[16,16,256]{2,1,0:T(8,128)} fusion(s32[16,2048]{1,0:T(8,128)S(1)} %bitcast.97, pred[2048]{0:T(1024)(128)(4,1)S(1)} %dynamic-slice_reduce_fusion.2, bf16[8,2048,16,16]{1,3,2,0:T(8,128)(2,1)} %get-tuple-element.226, s32[]{:T(128)} %get-tuple-element.211, f32[16,16,256]{2,1,0:T(8,128)} %get-tuple-element.212, pred[]{:T(512)S(6)} %compare.3), kind=kOutput, calls=%fused_computation.13.clone.1 | convolution fusion | flops 285343744 | bytes 1706497 | tf_op jit(solution)/shard_map/while/body/eval_jaxpr/mnk,nmd->mdk/dot_general | solution.py:67
  445.7 10.1 %fusion.43 = f32[16,16,256]{2,1,0:T(8,128)} fusion(s32[16,2048]{1,0:T(8,128)S(1)} %bitcast.97, pred[2048]{0:T(1024)(128)(4,1)S(1)} %dynamic-slice_reduce_fusion.2, bf16[8,2048,16,16]{1,3,2,0:T(8,128)(2,1)} %get-tuple-element.226, s32[]{:T(128)} %get-tuple-element.211, f32[16,16,256]{2,1,0:T(8,128)} %get-tuple-element.212, pred[]{:T(512)S(6)} %compare.3), kind=kOutput, calls=%fused_computation.13.clone.1 | convolution fusion | flops 285343744 | bytes 1706497 | tf_op jit(solution)/shard_map/while/body/eval_jaxpr/mnk,nmd->mdk/dot_general | solution.py:67
  473.1 10.1 %fusion.43 = f32[16,16,256]{2,1,0:T(8,128)} fusion(s32[16,2048]{1,0:T(8,128)S(1)} %bitcast.97, pred[2048]{0:T(1024)(128)(4,1)S(1)} %dynamic-slice_reduce_fusion.2, bf16[8,2048,16,16]{1,3,2,0:T(8,128)(2,1)} %get-tuple-element.226, s32[]{:T(128)} %get-tuple-element.211, f32[16,16,256]{2,1,0:T(8,128)} %get-tuple-element.212, pred[]{:T(512)S(6)} %compare.3), kind=kOutput, calls=%fused_computation.13.clone.1 | convolution fusion | flops 285343744 | bytes 1706497 | tf_op jit(solution)/shard_map/while/body/eval_jaxpr/mnk,nmd->mdk/dot_general | solution.py:67
  500.4 10.1 %fusion.43 = f32[16,16,256]{2,1,0:T(8,128)} fusion(s32[16,2048]{1,0:T(8,128)S(1)} %bitcast.97, pred[2048]{0:T(1024)(128)(4,1)S(1)} %dynamic-slice_reduce_fusion.2, bf16[8,2048,16,16]{1,3,2,0:T(8,128)(2,1)} %get-tuple-element.226, s32[]{:T(128)} %get-tuple-element.211, f32[16,16,256]{2,1,0:T(8,128)} %get-tuple-element.212, pred[]{:T(512)S(6)} %compare.3), kind=kOutput, calls=%fused_computation.13.clone.1 | convolution fusion | flops 285343744 | bytes 1706497 | tf_op jit(solution)/shard_map/while/body/eval_jaxpr/mnk,nmd->mdk/dot_general | solution.py:67
  527.8 10.1 %fusion.43 = f32[16,16,256]{2,1,0:T(8,128)} fusion(s32[16,2048]{1,0:T(8,128)S(1)} %bitcast.97, pred[2048]{0:T(1024)(128)(4,1)S(1)} %dynamic-slice_reduce_fusion.2, bf16[8,2048,16,16]{1,3,2,0:T(8,128)(2,1)} %get-tuple-element.226, s32[]{:T(128)} %get-tuple-element.211, f32[16,16,256]{2,1,0:T(8,128)} %get-tuple-element.212, pred[]{:T(512)S(6)} %compare.3), kind=kOutput, calls=%fused_computation.13.clone.1 | convolution fusion | flops 285343744 | bytes 1706497 | tf_op jit(solution)/shard_map/while/body/eval_jaxpr/mnk,nmd->mdk/dot_general | solution.py:67
  555.2 10.1 %fusion.43 = f32[16,16,256]{2,1,0:T(8,128)} fusion(s32[16,2048]{1,0:T(8,128)S(1)} %bitcast.97, pred[2048]{0:T(1024)(128)(4,1)S(1)} %dynamic-slice_reduce_fusion.2, bf16[8,2048,16,16]{1,3,2,0:T(8,128)(2,1)} %get-tuple-element.226, s32[]{:T(128)} %get-tuple-element.211, f32[16,16,256]{2,1,0:T(8,128)} %get-tuple-element.212, pred[]{:T(512)S(6)} %compare.3), kind=kOutput, calls=%fused_computation.13.clone.1 | convolution fusion | flops 285343744 | bytes 1706497 | tf_op jit(solution)/shard_map/while/body/eval_jaxpr/mnk,nmd->mdk/dot_general | solution.py:67
  582.6 10.1 %fusion.43 = f32[16,16,256]{2,1,0:T(8,128)} fusion(s32[16,2048]{1,0:T(8,128)S(1)} %bitcast.97, pred[2048]{0:T(1024)(128)(4,1)S(1)} %dynamic-slice_reduce_fusion.2, bf16[8,2048,16,16]{1,3,2,0:T(8,128)(2,1)} %get-tuple-element.226, s32[]{:T(128)} %get-tuple-element.211, f32[16,16,256]{2,1,0:T(8,128)} %get-tuple-element.212, pred[]{:T(512)S(6)} %compare.3), kind=kOutput, calls=%fused_computation.13.clone.1 | convolution fusion | flops 285343744 | bytes 1706497 | tf_op jit(solution)/shard_map/while/body/eval_jaxpr/mnk,nmd->mdk/dot_general | solution.py:67
  600.5 130.7 %psum.15 = f32[16,256]{1,0:T(8,128)S(1)} all-reduce(f32[16,256]{1,0:T(8,128)S(1)} %get-tuple-element.58), channel_id=1, replica_groups=mesh['lists'=32,'sub'=4] {'lists'}, use_global_device_ids=true, to_apply=%region_12.13 | all-reduce | flops 4096 | bytes 32768 | tf_op jit(solution)/shard_map/psum | solution.py:77
  733.5 101.1 %all-reduce.2.cloned.1.call-done = f32[16,16,256]{2,1,0:T(8,128)} async-done(((f32[16,16,256]{2,1,0:T(8,128)}), f32[16,16,256]{2,1,0:T(8,128)}) %all-reduce.2.cloned.1.call-update) | async-done | bytes 262160 | tf_op jit(solution)/shard_map/psum | solution.py:77
  (106 shorter events, 190.8 us)
Async XLA Ops:
  7.2 30.5 %copy-start = (bf16[1024,1024]{1,0:T(8,128)(2,1)S(1)}, bf16[1024,1024]{1,0:T(8,128)(2,1)}, u32[]{:S(2)}) copy-start(bf16[1024,1024]{1,0:T(8,128)(2,1)} %param.12) | copy-start | bytes 6291460
  28.3 34.0 %all-to-all-start = ((s32[1,32,128,4]{2,3,0,1:T(4,128)}), s32[1,32,128,4]{2,3,0,1:T(4,128)S(1)}, u32[]{:S(2)}, u32[]{:S(2)}) async-start(s32[1,32,128,4]{2,3,0,1:T(4,128)} %broadcast_in_dim.65), calls=%async_computation | async-start | bytes 131072 | tf_op jit(solution)/shard_map/all_to_all | solution.py:30
  62.3 116.0 %all-to-all-start.2 = ((bf16[1,32,128,1024]{3,2,0,1:T(8,128)(2,1)}), bf16[1,32,128,1024]{3,2,0,1:T(8,128)(2,1)}, u32[]{:S(2)}, u32[]{:S(2)}) async-start(bf16[1,32,128,1024]{3,2,0,1:T(8,128)(2,1)} %bitcast.95), calls=%async_computation.2 | async-start | bytes 16777216 | tf_op jit(solution)/shard_map/all_to_all | solution.py:29
  178.3 17.2 %all-to-all-start.1 = ((s32[1,32,128,4]{2,1,0,3:T(8,128)}), s32[1,32,128,4]{2,1,0,3:T(8,128)S(1)}, u32[]{:S(2)}, u32[]{:S(2)}) async-start(s32[1,32,128,4]{2,1,0,3:T(8,128)} %copy.34), calls=%async_computation.1 | async-start | bytes 131072 | tf_op jit(solution)/shard_map/all_to_all | solution.py:34
  195.5 5.9 copy-start.3
  195.5 6.5 copy-start.4
  195.5 6.6 copy-start.2
  195.5 102.4 %all-to-all-start.3 = ((bf16[1,32,128,1024]{2,1,0,3:T(8,128)(2,1)}), bf16[1,32,128,1024]{2,1,0,3:T(8,128)(2,1)}, u32[]{:S(2)}, u32[]{:S(2)}) async-start(bf16[1,32,128,1024]{2,1,0,3:T(8,128)(2,1)} %copy.36), calls=%async_computation.3 | async-start | bytes 16777216 | tf_op jit(solution)/shard_map/all_to_all | solution.py:33
  201.2 633.4 %all-reduce.2.cloned.1.call-start = ((), (), s32[]{:S(2)}) async-start(), calls=%async_computation.4 | async-start | bytes 524288 | tf_op jit(solution)/shard_map/psum | solution.py:77
  600.5 235.8 %copy-start.1 = (bf16[1024,1024]{1,0:T(8,128)(2,1)S(1)}, bf16[1024,1024]{1,0:T(8,128)(2,1)}, u32[]{:S(2)}) copy-start(bf16[1024,1024]{1,0:T(8,128)(2,1)} %param.12) | copy-start | bytes 6291460
Sparse Core Ops, SparseCore 0:
  731.3 103.1 all-reduce.1
where the time goes:
time: 854 us; the launch traced here: 843 us
  waiting for transfers between devices  209 us (24%)
  local copies, waits for them, and re-layouts  179 us (21%)
  matrix products  145 us (17%)
  other arithmetic  136 us (16%)
  blocking collectives  131 us (15%)
  starting transfers between devices  27.3 us (3%)
  between operations  14.5 us (2%)
    psum x1, blocking collectives, per_device(): totals, tallies = lax.psum((sums, counts), 'lists')  131 us
    all_to_all x1, waiting for transfers between devices, per_device(): lax.all_to_all(send_rows, 'lists', split_axis=1, concat_axis=1, tiled=True)  108 us
    psum x1, waiting for transfers between devices, per_device(): totals, tallies = lax.psum((sums, counts), 'lists')  101 us
    dot_general x8, matrix products, step(): jnp.einsum('mnk,nmd->mdk', hot, part, preferred_element_type=jnp.float32)  80.9 us
    gather x1, local copies, waits for them, and re-layouts, per_device(): picked = centroids[jnp.maximum(list_ids, 0)]  64.8 us
    reduce_sum x8, other arithmetic, step(): counts = counts + jnp.sum(hot.astype(jnp.float32), axis=1)  61.9 us
    dot_general x8, matrix products, step(): jnp.einsum('nmd,mdk->mnk', part, codebook, preferred_element_type=jnp.flo...  55.6 us
    convert_element_type x2, local copies, waits for them, and re-layouts, per_device(): slab.astype(jnp.float32) - picked.astype(jnp.float32)  35.9 us
  transfers between devices with their start and end apart: 5, of which 2 were waited for; matrix products, arithmetic and copies ran while one was open for 16% of the time, Pallas kernels for 0%

commit v1 on v0

v1 whole, which is shorter than its diff:
```python
import functools

import jax
import jax.numpy as jnp
from jax import lax
from jax.experimental import pallas as pl
from jax.experimental.pallas import tpu as pltpu
from jax.sharding import PartitionSpec as P

BF = jnp.bfloat16
F32 = jnp.float32
I32 = jnp.int32
I16 = jnp.int16
OWNERS = 32
GROUPS = 4
CAP = 128
ROWS = 2048
WIDTH = 1024
SOURCES = OWNERS * GROUPS
SLOTS = SOURCES * CAP
LISTS = 2048
CODES = 256
MIB = 2**20


def nn(a, b):
    return jnp.dot(a, b, preferred_element_type=F32)


def nt(a, b):
    return lax.dot_general(a, b, (((1,), (1,)), ((), ())), preferred_element_type=F32)


def params(mib=48):
    return pltpu.CompilerParams(
        vmem_limit_bytes=mib * MIB, dimension_semantics=("arbitrary",)
    )


def cost(flops, bytes_accessed):
    return pl.CostEstimate(
        flops=int(flops), bytes_accessed=int(bytes_accessed), transcendentals=0
    )


def rank_kernel(owner_ref, list_ref, slot_ref, ids_ref):
    owner = owner_ref[...]
    lists = list_ref[...]
    owner_hot = (owner == lax.broadcasted_iota(I32, (OWNERS, ROWS), 0)).astype(F32)
    before = (
        lax.broadcasted_iota(I32, (128, 128), 0) < lax.broadcasted_iota(I32, (128, 128), 1)
    ).astype(F32).astype(BF)
    blocks = ROWS // 128
    stacked = jnp.concatenate(
        [owner_hot[:, b * 128 : (b + 1) * 128] for b in range(blocks)], axis=0
    ).astype(BF)
    inside = nn(stacked, before)
    ranks = []
    carry = jnp.zeros((OWNERS, 1), F32)
    for b in range(blocks):
        hot = owner_hot[:, b * 128 : (b + 1) * 128]
        earlier = inside[b * OWNERS : (b + 1) * OWNERS] + carry
        ranks.append(jnp.sum(hot * earlier, axis=0, keepdims=True))
        carry = carry + jnp.sum(hot, axis=1, keepdims=True)
    rank = jnp.concatenate(ranks, axis=1).astype(I32)
    slot_ref[...] = owner * CAP + rank
    rank_hot = (rank == lax.broadcasted_iota(I32, (CAP, ROWS), 0)).astype(F32).astype(BF)
    high = (lists // 128).astype(F32)
    low = (lists % 128).astype(F32)
    left = jnp.concatenate([owner_hot * high, owner_hot * low, owner_hot], axis=0).astype(BF)
    found = nt(left, rank_hot)
    number = found[:OWNERS] * 128.0 + found[OWNERS : 2 * OWNERS]
    live = found[2 * OWNERS :]
    ids_ref[...] = (number + live - 1.0).astype(I32)


def rank_rows(owner, lists):
    return pl.pallas_call(
        rank_kernel,
        out_shape=[
            jax.ShapeDtypeStruct((1, ROWS), I32),
            jax.ShapeDtypeStruct((OWNERS, CAP), I32),
        ],
        compiler_params=pltpu.CompilerParams(vmem_limit_bytes=32 * MIB),
        cost_estimate=cost(1e9, 100000),
    )(owner, lists)


def route_kernel(step_owners, slot_ref, rows_ref, r0, r1, r2, r3, out_ref, rot_ref):
    step = pl.program_id(0)

    @pl.when(step == 0)
    def _():
        for g, r in enumerate((r0, r1, r2, r3)):
            rot_ref[:, g * 128 : (g + 1) * 128] = nn(rows_ref[...], r[...]).astype(BF)

    count = step_owners * CAP
    place = slot_ref[...] - step * count
    hot = (place == lax.broadcasted_iota(I32, (count, ROWS), 0)).astype(F32).astype(BF)
    sent = nn(hot, rot_ref[...]).astype(BF)
    for g in range(GROUPS):
        part = sent[:, g * 128 : (g + 1) * 128]
        out_ref[g] = part.reshape(step_owners, CAP, 128)


def route(half, slot, embeddings, matrix):
    step_owners = 4
    columns = [
        pl.BlockSpec((WIDTH, 128), functools.partial(lambda col, i: (0, col), 2 * g + half))
        for g in range(GROUPS)
    ]
    return pl.pallas_call(
        functools.partial(route_kernel, step_owners),
        grid=(OWNERS // step_owners,),
        in_specs=[
            pl.BlockSpec((1, ROWS), lambda i: (0, 0)),
            pl.BlockSpec((ROWS, WIDTH), lambda i: (0, 0)),
            *columns,
        ],
        out_specs=pl.BlockSpec((GROUPS, step_owners, CAP, 128), lambda i: (0, i, 0, 0)),
        out_shape=jax.ShapeDtypeStruct((GROUPS, OWNERS, CAP, 128), BF),
        scratch_shapes=[pltpu.VMEM((ROWS, GROUPS * 128), BF)],
        compiler_params=params(),
        cost_estimate=cost(11e9, 10 * MIB),
    )(slot, embeddings, matrix, matrix, matrix, matrix)


def pick_kernel(step_sources, ids_ref, centroid_ref, target_ref, out_ref, count_ref, acc_ref):
    step = pl.program_id(0)

    @pl.when(step == 0)
    def _():
        acc_ref[...] = jnp.zeros_like(acc_ref)

    slots = step_sources * CAP
    one = jnp.ones((), BF)
    zero = jnp.zeros((), BF)
    lane = lax.broadcasted_iota(I32, (CAP, 128), 1).astype(I16)
    for j in range(step_sources):
        ids = ids_ref[j : j + 1, :].astype(F32)
        column = jnp.broadcast_to(ids, (128, CAP)).T.astype(I32).astype(I16)
        hot = jnp.concatenate(
            [
                jnp.where(column == lane + jnp.int16(128 * b), one, zero)
                for b in range(LISTS // 128)
            ],
            axis=1,
        )
        out_ref[j] = nn(hot, centroid_ref[...]).astype(BF)

    live = jnp.concatenate([ids_ref[j : j + 1, :] for j in range(step_sources)], axis=1) >= 0
    target = jnp.where(live, target_ref[...], -1)
    high = jnp.where(live, target // 16, -1).astype(I16)
    low = (target % 16).astype(I16)
    digit = lax.broadcasted_iota(I32, (16, slots), 0).astype(I16)
    left = []
    right = []
    for m in range(16):
        left.append(jnp.where(high[m : m + 1] == digit, one, zero))
        right.append(jnp.where(low[m : m + 1] == digit, one, zero))
    acc_ref[...] += nt(jnp.concatenate(left, axis=0), jnp.concatenate(right, axis=0))

    @pl.when(step == pl.num_programs(0) - 1)
    def _():
        for m in range(16):
            block = acc_ref[m * 16 : (m + 1) * 16, m * 16 : (m + 1) * 16]
            count_ref[m] = block


def pick(ids, centroids, targets):
    step_sources = 8
    slots = step_sources * CAP
    return pl.pallas_call(
        functools.partial(pick_kernel, step_sources),
        grid=(SOURCES // step_sources,),
        in_specs=[
            pl.BlockSpec((step_sources, CAP), lambda i: (i, 0)),
            pl.BlockSpec((LISTS, 256), lambda i: (0, 0)),
            pl.BlockSpec((16, slots), lambda i: (0, i)),
        ],
        out_specs=[
            pl.BlockSpec((step_sources, CAP, 256), lambda i: (i, 0, 0)),
            pl.BlockSpec((16, 16, 16), lambda i: (0, 0, 0)),
        ],
        out_shape=[
            jax.ShapeDtypeStruct((SOURCES, CAP, 256), BF),
            jax.ShapeDtypeStruct((16, 16, 16), F32),
        ],
        scratch_shapes=[pltpu.VMEM((256, 256), F32)],
        compiler_params=params(),
        cost_estimate=cost(20e9, 12 * MIB),
    )(ids, centroids, targets)


def book_kernel(code_ref, out_ref):
    codes = code_ref[...].astype(F32).T
    lane = lax.broadcasted_iota(I32, (CODES, 128), 1)
    for m in range(8):
        mine = jnp.where(lane // 16 == m, codes, 0.0)
        square = jnp.sum(mine * mine, axis=1, keepdims=True)
        high = square.astype(BF).astype(F32)
        middle = (square - high).astype(BF).astype(F32)
        low = square - high - middle
        tail = jnp.where(
            lane == 0, high, jnp.where(lane == 1, middle, jnp.where(lane == 2, low, 0.0))
        )
        out_ref[m * CODES : (m + 1) * CODES, :128] = (-2.0 * mine).astype(BF)
        out_ref[m * CODES : (m + 1) * CODES, 128:] = tail.astype(BF)


def make_book(codebook):
    return pl.pallas_call(
        book_kernel,
        grid=(2,),
        in_specs=[pl.BlockSpec((128, CODES), lambda i: (i, 0))],
        out_specs=pl.BlockSpec((8 * CODES, 256), lambda i: (i, 0)),
        out_shape=jax.ShapeDtypeStruct((16 * CODES, 256), BF),
        compiler_params=params(),
        cost_estimate=cost(1e9, 3 * MIB),
    )(codebook.reshape(256, CODES))


def residual(rows_ref, pick_ref, slots):
    rows = rows_ref[...].reshape(slots, 128).astype(F32)
    centre = pick_ref[...].reshape(slots, 128).astype(F32)
    return (rows - centre).astype(BF)


def sums_kernel(slots, rows_ref, pick_ref, target_ref, out_ref, acc_ref):
    step = pl.program_id(0)

    @pl.when(step == 0)
    def _():
        acc_ref[...] = jnp.zeros_like(acc_ref)

    flipped = residual(rows_ref, pick_ref, slots).astype(F32).T.astype(BF)
    target = target_ref[...]
    high = (target // 64).astype(I16)
    low = (target % 64).astype(I16)
    digit = lax.broadcasted_iota(I32, (64, slots), 0).astype(I16)
    one = jnp.ones((), BF)
    zero = jnp.zeros((), BF)
    for t in range(2):
        left = []
        right = []
        for m in range(4 * t, 4 * t + 4):
            mine = flipped[m * 16 : (m + 1) * 16]
            row = jnp.broadcast_to(high[m : m + 1], (16, slots))
            for h in range(4):
                left.append(jnp.where(row == jnp.int16(h), mine, zero))
            right.append(jnp.where(low[m : m + 1] == digit, one, zero))
        acc_ref[t] += nt(jnp.concatenate(left, axis=0), jnp.concatenate(right, axis=0))

    @pl.when(step == pl.num_programs(0) - 1)
    def _():
        for m in range(8):
            part = acc_ref[m // 4][:, (m % 4) * 64 : (m % 4 + 1) * 64]
            base = (m % 4) * 64
            out_ref[m] = jnp.concatenate(
                [part[base + h * 16 : base + (h + 1) * 16] for h in range(4)], axis=1
            )


def code_sums(half, rows, picked, targets):
    step_sources = 16
    slots = step_sources * CAP
    return pl.pallas_call(
        functools.partial(sums_kernel, slots),
        grid=(SOURCES // step_sources,),
        in_specs=[
            pl.BlockSpec((step_sources, CAP, 128), lambda i: (i, 0, 0)),
            pl.BlockSpec((step_sources, CAP, 128), lambda i: (i, 0, half)),
            pl.BlockSpec((8, slots), lambda i: (half, i)),
        ],
        out_specs=pl.BlockSpec((8, 16, CODES), lambda i: (0, 0, 0)),
        out_shape=jax.ShapeDtypeStruct((8, 16, CODES), F32),
        scratch_shapes=[pltpu.VMEM((2, 256, 256), F32)],
        compiler_params=params(),
        cost_estimate=cost(4e9, 9 * MIB),
    )(rows, picked, targets)


def errors_kernel(slots, rows_ref, pick_ref, ids_ref, book_ref, out_ref):
    resid = residual(rows_ref, pick_ref, slots)
    wide = jnp.concatenate([resid, jnp.ones((slots, 128), BF)], axis=1)
    square = resid.astype(F32) * resid.astype(F32)
    high = square.astype(BF)
    low = (square - high.astype(F32)).astype(BF)
    member = (
        (lax.broadcasted_iota(I32, (16, 256), 1) % 128) // 16
        == lax.broadcasted_iota(I32, (16, 256), 0)
    ).astype(F32).astype(BF)
    row_sq = nt(member, jnp.concatenate([high, low], axis=1))
    sources = slots // CAP
    live = jnp.concatenate([ids_ref[j : j + 1, :] for j in range(sources)], axis=1) >= 0
    for m in range(8):
        dist = nt(book_ref[m * CODES : (m + 1) * CODES], wide)
        least = jnp.min(dist, axis=0, keepdims=True)
        out_ref[m : m + 1, :] = jnp.where(live, row_sq[m : m + 1] + least, 0.0)


def errors(half, rows, picked, ids, book):
    step_sources = 16
    slots = step_sources * CAP
    return pl.pallas_call(
        functools.partial(errors_kernel, slots),
        grid=(SOURCES // step_sources,),
        in_specs=[
            pl.BlockSpec((step_sources, CAP, 128), lambda i: (i, 0, 0)),
            pl.BlockSpec((step_sources, CAP, 128), lambda i: (i, 0, half)),
            pl.BlockSpec((step_sources, CAP), lambda i: (i, 0)),
            pl.BlockSpec((8 * CODES, 256), lambda i: (half, 0)),
        ],
        out_specs=pl.BlockSpec((8, slots), lambda i: (0, i)),
        out_shape=jax.ShapeDtypeStruct((8, SLOTS), F32),
        compiler_params=params(),
        cost_estimate=cost(18e9, 9 * MIB),
    )(rows, picked, ids, book)


def exchange(x, axes):
    return lax.all_to_all(x, axes, split_axis=0, concat_axis=0, tiled=True)


def per_device(
    embeddings, owner_of_row, list_in_owner, opq_matrix, centroids, codebook, code_targets
):
    every = ("sub", "lists")
    slot, ids = rank_rows(owner_of_row.reshape(1, ROWS), list_in_owner.reshape(1, ROWS))
    send_ids = jnp.broadcast_to(ids[None, :, None, :], (GROUPS, OWNERS, 1, CAP))
    got_ids = exchange(send_ids.reshape(SOURCES, 1, CAP), every).reshape(SOURCES, CAP)
    first = route(0, slot, embeddings, opq_matrix).reshape(SOURCES, CAP, 128)
    rows0 = exchange(first, every)
    second = route(1, slot, embeddings, opq_matrix).reshape(SOURCES, CAP, 128)
    book = make_book(codebook)
    picked, counts = pick(got_ids, centroids, code_targets)
    rows1 = exchange(second, every)
    sums0 = code_sums(0, rows0, picked, code_targets)
    errors0 = errors(0, rows0, picked, got_ids, book)
    sums1 = code_sums(1, rows1, picked, code_targets)
    sums = jnp.concatenate([sums0, sums1], axis=0)
    pieces = jnp.concatenate(
        [
            sums.reshape(16, 16, 2, 128).transpose(0, 2, 1, 3).reshape(OWNERS, 16, 128),
            jnp.broadcast_to(counts.reshape(OWNERS, 1, 128), (OWNERS, 8, 128)),
        ],
        axis=1,
    )
    got = jnp.sum(exchange(pieces, "lists"), axis=0)
    errors1 = errors(1, rows1, picked, got_ids, book)
    me = lax.axis_index("lists")
    code_piece = lax.dynamic_slice(codebook, (me // 2, 0, (me % 2) * 128), (1, 16, 128))[0]
    new_piece = (code_piece.astype(F32) + got[:16]) / (1.0 + got[16:17])
    spread = exchange(jnp.broadcast_to(new_piece[None], (OWNERS, 16, 128)), "lists")
    new_codebook = (
        spread.reshape(16, 2, 16, 128).transpose(0, 2, 1, 3).reshape(16, 16, CODES)
    )
    quant_error = jnp.concatenate([errors0, errors1], axis=0)
    return quant_error, new_codebook


def solution(mesh):
    placed = (
        P(("lists", "sub"), None),
        P(("lists", "sub"), None),
        P(("lists", "sub")),
        P(),
        P("lists", "sub"),
        P("sub", None, None),
        P("sub", "lists"),
    )
    return jax.shard_map(
        per_device,
        mesh=mesh,
        in_specs=placed,
        out_specs=(P("sub", "lists"), P("sub", None, None)),
        check_vma=False,
    )
```

time: 854 us -> 236 us (0.28); the launches traced: 843 us -> 235 us
  local copies, waits for them, and re-layouts: 179 us -> 6.76 us
  waiting for transfers between devices: 209 us -> 59.9 us
  matrix products: 145 us -> 0 us
  other arithmetic: 136 us -> 1.9 us
  blocking collectives: 131 us -> 0 us
  Pallas kernels: 0 us -> 127 us
  between operations: 14.5 us -> 0.88 us
  starting transfers between devices: 27.3 us -> 39.5 us
    dot_general x17 -> x0, matrix products: 145 us -> none  [the longest x8 80.9 us: step(): jnp.einsum('mnk,nmd->mdk', hot, part, preferred_element_type=jnp.float32)]
    psum x1 -> x0, blocking collectives: 131 us -> none  [per_device(): totals, tallies = lax.psum((sums, counts), 'lists')]
    pallas_call x0 -> x9, Pallas kernels: none -> 127 us  [the longest x2 45.9 us: errors(): pl.pallas_call(functools.partial(errors_kernel, slots), grid=(SOURCES //...]
    psum x1 -> x0, waiting for transfers between devices: 101 us -> none  [per_device(): totals, tallies = lax.psum((sums, counts), 'lists')]
    reduce_sum x18 -> x1, other arithmetic: 76 us -> 0.04 us  [per_device(): got = jnp.sum(exchange(pieces, 'lists'), axis=0)]
    gather x1 -> x0, local copies, waits for them, and re-layouts: 64.8 us -> none  [per_device(): picked = centroids[jnp.maximum(list_ids, 0)]]
    convert_element_type x3 -> x0, local copies, waits for them, and re-layouts: 48.1 us -> none  [the longest x2 35.9 us: per_device(): slab.astype(jnp.float32) - picked.astype(jnp.float32)]
    all_to_all x4 -> x5, waiting for transfers between devices: 108 us -> 59.9 us  [exchange(): return lax.all_to_all(x, axes, split_axis=0, concat_axis=0, tiled=True)]
  transfers between devices with their start and end apart: 5 -> 5, of which waited for: 2 -> 3; matrix products, arithmetic and copies ran while one was open for 16% -> 0% of each run, Pallas kernels for 0% -> 50%
where the time goes in v1:
time: 236 us; the launch traced here: 235 us
  Pallas kernels  127 us (54%)
  waiting for transfers between devices  59.9 us (25%)
  starting transfers between devices  39.5 us (17%)
  local copies, waits for them, and re-layouts  6.76 us (3%)
    all_to_all x5, waiting for transfers between devices, exchange(): return lax.all_to_all(x, axes, split_axis=0, concat_axis=0, tiled=True)  59.9 us
    pallas_call x2, Pallas kernels, errors(): pl.pallas_call(functools.partial(errors_kernel, slots), grid=(SOURCES //...  45.9 us
    all_to_all x5, starting transfers between devices, exchange(): return lax.all_to_all(x, axes, split_axis=0, concat_axis=0, tiled=True)  39.5 us
    pallas_call x2, Pallas kernels, route(): pl.pallas_call(functools.partial(route_kernel, step_owners), grid=(OWNERS...  35.6 us
    pallas_call x1, Pallas kernels, pick(): pl.pallas_call(functools.partial(pick_kernel, step_sources), grid=(SOURCE...  25.3 us
    pallas_call x2, Pallas kernels, code_sums(): pl.pallas_call(functools.partial(sums_kernel, slots), grid=(SOURCES // st...  18.1 us
  transfers between devices with their start and end apart: 5, of which 3 were waited for; matrix products, arithmetic and copies ran while one was open for 0% of the time, Pallas kernels for 50%

profile of v1, /device:TPU:1, one launch (start us, length us, event | category | flops | bytes accessed | tf_op | source)
XLA Modules:
  0.0 235.4 jit_solution(15328107159554464092)
XLA Ops:
  0.6 0.7 copy-done.5
  1.3 0.7 copy-done.6
  3.2 11.5 %all-to-all-start.1 = ((s32[128,1,128]{2,1,0:T(1,128)}), s32[128,1,128]{2,1,0:T(1,128)S(1)}, u32[]{:S(2)}, u32[]{:S(2)}) async-start(s32[128,1,128]{2,1,0:T(1,128)} %bitcast.3), calls=%async_computation.1 | async-start | bytes 131072 | tf_op jit(solution)/shard_map/all_to_all | solution.py:322
  14.7 1.6 copy-done.1
  16.3 17.8 %shard_map.91 = bf16[4,32,128,128]{3,2,1,0:T(8,128)(2,1)} custom-call(s32[1,2048]{1,0:T(1,128)S(1)} %get-tuple-element.6.slot_ref, bf16[2048,1024]{1,0:T(8,128)(2,1)} %rows_ref.3, bf16[1024,1024]{1,0:T(8,128)(2,1)S(1)} %copy-done.1, bf16[1024,1024]{1,0:T(8,128)(2,1)S(1)} %copy-done.1, bf16[1024,1024]{1,0:T(8,128)(2,1)S(1)} %copy-done.1, ...), custom_call_target="tpu_custom_call" | custom-call | flops 11000000512 | bytes 10485760 | tf_op jit(solution)/shard_map/pallas_call | solution.py:112
  34.1 10.2 %all-to-all-start.2 = ((bf16[128,128,128]{2,1,0:T(8,128)(2,1)}), bf16[128,128,128]{2,1,0:T(8,128)(2,1)}, u32[]{:S(2)}, u32[]{:S(2)}) async-start(bf16[128,128,128]{2,1,0:T(8,128)(2,1)} %bitcast.27), calls=%async_computation.2 | async-start | bytes 8388608 | tf_op jit(solution)/shard_map/all_to_all | solution.py:322
  44.3 17.8 %shard_map.87 = bf16[4,32,128,128]{3,2,1,0:T(8,128)(2,1)} custom-call(s32[1,2048]{1,0:T(1,128)S(1)} %get-tuple-element.6.slot_ref, bf16[2048,1024]{1,0:T(8,128)(2,1)} %rows_ref.3, bf16[1024,1024]{1,0:T(8,128)(2,1)S(1)} %copy-done.2, bf16[1024,1024]{1,0:T(8,128)(2,1)S(1)} %copy-done.2, bf16[1024,1024]{1,0:T(8,128)(2,1)S(1)} %copy-done.2, ...), custom_call_target="tpu_custom_call" | custom-call | flops 11000000512 | bytes 10485760 | tf_op jit(solution)/shard_map/pallas_call | solution.py:112
  62.1 34.8 %all-to-all-done.2.rows_ref = bf16[128,128,128]{2,1,0:T(8,128)(2,1)} async-done(((bf16[128,128,128]{2,1,0:T(8,128)(2,1)}), bf16[128,128,128]{2,1,0:T(8,128)(2,1)}, u32[]{:S(2)}, u32[]{:S(2)}) %all-to-all-start.2) | async-done | bytes 4194336 | tf_op jit(solution)/shard_map/all_to_all | solution.py:322
  96.9 5.7 %all-to-all-start = ((bf16[128,128,128]{2,1,0:T(8,128)(2,1)}), bf16[128,128,128]{2,1,0:T(8,128)(2,1)}, u32[]{:S(2)}, u32[]{:S(2)}) async-start(bf16[128,128,128]{2,1,0:T(8,128)(2,1)} %bitcast.26), calls=%async_computation | async-start | bytes 8388608 | tf_op jit(solution)/shard_map/all_to_all | solution.py:322
  102.7 1.1 shard_map.89.book_ref
  103.8 25.3 %shard_map.88 = (bf16[128,128,256]{2,1,0:T(8,128)(2,1)}, f32[16,16,16]{2,1,0:T(8,128)S(1)}) custom-call(s32[128,128]{1,0:T(8,128)S(1)} %bitcast.20, bf16[2048,256]{1,0:T(8,128)(2,1)S(1)} %copy-done.3, s32[16,16384]{1,0:T(8,128)S(1)} %copy-done.4), custom_call_target="tpu_custom_call" | custom-call | flops 20000000000 | bytes 12582912 | tf_op jit(solution)/shard_map/pallas_call | solution.py:173
  129.2 9.1 %shard_map.94 = f32[8,16,256]{2,1,0:T(8,128)S(1)} custom-call(bf16[128,128,128]{2,1,0:T(8,128)(2,1)} %all-to-all-done.2.rows_ref, bf16[128,128,256]{2,1,0:T(8,128)(2,1)} %get-tuple-element.8.pick_ref, s32[16,16384]{1,0:T(8,128)S(1)} %copy-done.4), custom_call_target="tpu_custom_call" | custom-call | flops 4000000000 | bytes 9437184 | tf_op jit(solution)/shard_map/pallas_call | solution.py:267
  138.3 17.1 %all-to-all-done.rows_ref = bf16[128,128,128]{2,1,0:T(8,128)(2,1)} async-done(((bf16[128,128,128]{2,1,0:T(8,128)(2,1)}), bf16[128,128,128]{2,1,0:T(8,128)(2,1)}, u32[]{:S(2)}, u32[]{:S(2)}) %all-to-all-start) | async-done | bytes 4194336 | tf_op jit(solution)/shard_map/all_to_all | solution.py:322
  155.4 9.0 %shard_map.93 = f32[8,16,256]{2,1,0:T(8,128)S(1)} custom-call(bf16[128,128,128]{2,1,0:T(8,128)(2,1)} %all-to-all-done.rows_ref, bf16[128,128,256]{2,1,0:T(8,128)(2,1)} %get-tuple-element.8.pick_ref, s32[16,16384]{1,0:T(8,128)S(1)} %copy-done.4), custom_call_target="tpu_custom_call" | custom-call | flops 4000000000 | bytes 9437184 | tf_op jit(solution)/shard_map/pallas_call | solution.py:267
  164.5 0.8 pad_maximum_fusion.1
  165.3 4.6 %all-to-all-start.3 = ((f32[32,24,128]{2,1,0:T(8,128)}), f32[32,24,128]{2,1,0:T(8,128)S(1)}, u32[]{:S(2)}, u32[]{:S(2)}) async-start(f32[32,24,128]{2,1,0:T(8,128)} %pad_maximum_fusion.1), calls=%async_computation.3 | async-start | bytes 786432 | tf_op jit(solution)/shard_map/all_to_all | solution.py:322
  169.8 1.6 copy-done.8
  171.4 23.0 %shard_map.92 = f32[8,16384]{1,0:T(8,128)S(1)} custom-call(bf16[128,128,128]{2,1,0:T(8,128)(2,1)} %all-to-all-done.2.rows_ref, bf16[128,128,256]{2,1,0:T(8,128)(2,1)} %get-tuple-element.8.pick_ref, s32[128,128]{1,0:T(8,128)S(1)} %bitcast.21, bf16[4096,256]{1,0:T(8,128)(2,1)S(1)} %copy-done.8), custom_call_target="tpu_custom_call" | custom-call | flops 17999998976 | bytes 9437184 | tf_op jit(solution)/shard_map/pallas_call | solution.py:305
  194.4 23.0 %shard_map.90 = f32[8,16384]{1,0:T(8,128)S(1)} custom-call(bf16[128,128,128]{2,1,0:T(8,128)(2,1)} %all-to-all-done.rows_ref, bf16[128,128,256]{2,1,0:T(8,128)(2,1)} %get-tuple-element.8.pick_ref, s32[128,128]{1,0:T(8,128)S(1)} %bitcast.22, bf16[4096,256]{1,0:T(8,128)(2,1)S(1)} %copy-done.8), custom_call_target="tpu_custom_call" | custom-call | flops 17999998976 | bytes 9437184 | tf_op jit(solution)/shard_map/pallas_call | solution.py:305
  217.5 0.7 broadcast_in_dim.25
  218.2 7.5 %all-to-all-start.4 = ((f32[32,16,128]{2,1,0:T(8,128)}), f32[32,16,128]{2,1,0:T(8,128)S(1)}, u32[]{:S(2)}, u32[]{:S(2)}) async-start(f32[32,16,128]{2,1,0:T(8,128)} %broadcast_in_dim.25), calls=%async_computation.4 | async-start | bytes 524288 | tf_op jit(solution)/shard_map/all_to_all | solution.py:322
  225.7 1.0 pad_maximum_fusion
  226.7 7.9 %all-to-all-done.4 = f32[32,16,128]{2,1,0:T(8,128)S(1)} async-done(((f32[32,16,128]{2,1,0:T(8,128)}), f32[32,16,128]{2,1,0:T(8,128)S(1)}, u32[]{:S(2)}, u32[]{:S(2)}) %all-to-all-start.4) | async-done | bytes 262176 | tf_op jit(solution)/shard_map/all_to_all | solution.py:322
  234.7 0.7 copy.13
  (25 shorter events, 1.4 us)
Async XLA Ops:
  0.6 0.7 copy-start.5
  1.3 0.7 copy-start.6
  3.2 30.9 %all-to-all-start.1 = ((s32[128,1,128]{2,1,0:T(1,128)}), s32[128,1,128]{2,1,0:T(1,128)S(1)}, u32[]{:S(2)}, u32[]{:S(2)}) async-start(s32[128,1,128]{2,1,0:T(1,128)} %bitcast.3), calls=%async_computation.1 | async-start | bytes 131072 | tf_op jit(solution)/shard_map/all_to_all | solution.py:322
  14.7 1.6 copy-start.1
  34.1 10.2 %copy-start.2 = (bf16[1024,1024]{1,0:T(8,128)(2,1)S(1)}, bf16[1024,1024]{1,0:T(8,128)(2,1)}, u32[]{:S(2)}) copy-start(bf16[1024,1024]{1,0:T(8,128)(2,1)} %r3.3) | copy-start | bytes 6291460
  34.1 62.8 %all-to-all-start.2 = ((bf16[128,128,128]{2,1,0:T(8,128)(2,1)}), bf16[128,128,128]{2,1,0:T(8,128)(2,1)}, u32[]{:S(2)}, u32[]{:S(2)}) async-start(bf16[128,128,128]{2,1,0:T(8,128)(2,1)} %bitcast.27), calls=%async_computation.2 | async-start | bytes 8388608 | tf_op jit(solution)/shard_map/all_to_all | solution.py:322
  96.9 5.8 %copy-start = (bf16[16,16,256]{2,1,0:T(8,128)(2,1)S(1)}, bf16[16,16,256]{2,1,0:T(8,128)(2,1)}, u32[]{:S(2)}) copy-start(bf16[16,16,256]{2,1,0:T(8,128)(2,1)} %param.12) | copy-start | bytes 393220
  96.9 6.9 %copy-start.3 = (bf16[2048,256]{1,0:T(8,128)(2,1)S(1)}, bf16[2048,256]{1,0:T(8,128)(2,1)}, u32[]{:S(2)}) copy-start(bf16[2048,256]{1,0:T(8,128)(2,1)} %centroid_ref.1) | copy-start | bytes 3145732
  96.9 6.9 %copy-start.4 = (s32[16,16384]{1,0:T(8,128)S(1)}, s32[16,16384]{1,0:T(8,128)}, u32[]{:S(2)}) copy-start(s32[16,16384]{1,0:T(8,128)} %target_ref.5) | copy-start | bytes 3145732
  96.9 58.5 %all-to-all-start = ((bf16[128,128,128]{2,1,0:T(8,128)(2,1)}), bf16[128,128,128]{2,1,0:T(8,128)(2,1)}, u32[]{:S(2)}, u32[]{:S(2)}) async-start(bf16[128,128,128]{2,1,0:T(8,128)(2,1)} %bitcast.26), calls=%async_computation | async-start | bytes 8388608 | tf_op jit(solution)/shard_map/all_to_all | solution.py:322
  103.8 25.3 %copy-start.7 = (bf16[4096,256]{1,0:T(8,128)(2,1)}, bf16[4096,256]{1,0:T(8,128)(2,1)S(1)}, u32[]{:S(2)}) copy-start(bf16[4096,256]{1,0:T(8,128)(2,1)S(1)} %shard_map.89.book_ref) | copy-start | bytes 6291460
  165.3 52.1 %all-to-all-start.3 = ((f32[32,24,128]{2,1,0:T(8,128)}), f32[32,24,128]{2,1,0:T(8,128)S(1)}, u32[]{:S(2)}, u32[]{:S(2)}) async-start(f32[32,24,128]{2,1,0:T(8,128)} %pad_maximum_fusion.1), calls=%async_computation.3 | async-start | bytes 786432 | tf_op jit(solution)/shard_map/all_to_all | solution.py:322
  169.8 1.6 copy-start.8
  218.2 16.5 %all-to-all-start.4 = ((f32[32,16,128]{2,1,0:T(8,128)}), f32[32,16,128]{2,1,0:T(8,128)S(1)}, u32[]{:S(2)}, u32[]{:S(2)}) async-start(f32[32,16,128]{2,1,0:T(8,128)} %broadcast_in_dim.25), calls=%async_computation.4 | async-start | bytes 524288 | tf_op jit(solution)/shard_map/all_to_all | solution.py:322

commit v2 on v1

v2 whole, which is shorter than its diff:
```python
import functools

import jax
import jax.numpy as jnp
from jax import lax
from jax.experimental import pallas as pl
from jax.experimental.pallas import tpu as pltpu
from jax.sharding import PartitionSpec as P

BF = jnp.bfloat16
F32 = jnp.float32
I32 = jnp.int32
I16 = jnp.int16
OWNERS = 32
GROUPS = 4
CAP = 128
ROWS = 2048
WIDTH = 1024
SOURCES = OWNERS * GROUPS
SLOTS = SOURCES * CAP
LISTS = 2048
CODES = 256
MIB = 2**20


def nn(a, b):
    return jnp.dot(a, b, preferred_element_type=F32)


def nt(a, b):
    return lax.dot_general(a, b, (((1,), (1,)), ((), ())), preferred_element_type=F32)


def params(mib):
    return pltpu.CompilerParams(
        vmem_limit_bytes=mib * MIB, dimension_semantics=("arbitrary",)
    )


def cost(flops, bytes_accessed):
    return pl.CostEstimate(
        flops=int(flops), bytes_accessed=int(bytes_accessed), transcendentals=0
    )


def rank_kernel(owner_ref, list_ref, place_ref, start_ref, ids_ref):
    owner = owner_ref[...]
    lists = list_ref[...]
    owner_hot = (owner == lax.broadcasted_iota(I32, (OWNERS, ROWS), 0)).astype(F32)
    before = (
        lax.broadcasted_iota(I32, (128, 128), 0) < lax.broadcasted_iota(I32, (128, 128), 1)
    ).astype(F32).astype(BF)
    blocks = ROWS // 128
    stacked = jnp.concatenate(
        [owner_hot[:, b * 128 : (b + 1) * 128] for b in range(blocks)], axis=0
    ).astype(BF)
    inside = nn(stacked, before)
    ranks = []
    carry = jnp.zeros((OWNERS, 1), F32)
    for b in range(blocks):
        hot = owner_hot[:, b * 128 : (b + 1) * 128]
        earlier = inside[b * OWNERS : (b + 1) * OWNERS] + carry
        ranks.append(jnp.sum(hot * earlier, axis=0, keepdims=True))
        carry = carry + jnp.sum(hot, axis=1, keepdims=True)
    rank = jnp.concatenate(ranks, axis=1)
    pages = ((carry.astype(I32) + 15) // 16).astype(F32).astype(BF)
    first = nn(before[:OWNERS, :OWNERS].astype(F32).T.astype(BF), jnp.broadcast_to(pages, (OWNERS, 128)))
    begin = jnp.sum(owner_hot * first[:, :1], axis=0, keepdims=True) * 16.0
    place_ref[...] = (begin + rank).astype(I32)
    start_ref[...] = first.astype(I32)
    rank_hot = (rank.astype(I32) == lax.broadcasted_iota(I32, (CAP, ROWS), 0)).astype(F32).astype(BF)
    high = (lists // 128).astype(F32)
    low = (lists % 128).astype(F32)
    left = jnp.concatenate([owner_hot * high, owner_hot * low, owner_hot], axis=0).astype(BF)
    found = nt(left, rank_hot)
    number = found[:OWNERS] * 128.0 + found[OWNERS : 2 * OWNERS]
    live = found[2 * OWNERS :]
    ids_ref[...] = (number + live - 1.0).astype(I32)


def rank_rows(owner, lists):
    return pl.pallas_call(
        rank_kernel,
        out_shape=[
            jax.ShapeDtypeStruct((1, ROWS), I32),
            jax.ShapeDtypeStruct((OWNERS, 128), I32),
            jax.ShapeDtypeStruct((OWNERS, CAP), I32),
        ],
        compiler_params=pltpu.CompilerParams(vmem_limit_bytes=56 * MIB),
        cost_estimate=cost(1e9, 100000),
    )(owner, lists)


ORDERED = ROWS + 16 * OWNERS
ID_ROWS = 16
HALF = CAP // 2
HALF_SLOTS = SOURCES * HALF


def order_rows(step, rot_steps, row_steps, place_ref, rows_ref, columns, rot_ref, run_ref):
    rot_rows = ROWS // rot_steps
    run_rows = ORDERED // row_steps

    @pl.when(step < rot_steps)
    def _():
        matrix = jnp.concatenate([r[...] for r in columns], axis=1)
        at = pl.multiple_of(step * rot_rows, rot_rows)
        rot_ref[pl.ds(at, rot_rows), :] = nn(rows_ref[...], matrix).astype(BF)

    @pl.when(step == 0)
    def _():
        run_ref[ORDERED:, :] = jnp.zeros((CAP, GROUPS * 128), BF)

    @pl.when(step == rot_steps)
    def _():
        one = jnp.ones((), BF)
        zero = jnp.zeros((), BF)
        digit = lax.broadcasted_iota(I32, (run_rows, ROWS), 0).astype(I16)
        for k in range(row_steps):
            place = (place_ref[...] - k * run_rows).astype(I16)
            hot = jnp.where(place == digit, one, zero)
            run_ref[k * run_rows : (k + 1) * run_rows, :] = nn(hot, rot_ref[...]).astype(BF)


def first_route_kernel(rot_steps, row_steps, step_owners, start_ref, place_ref, ids_ref, rows_ref,
                       r0, r1, r2, r3, low_ref, high_ref, rot_ref, run_ref):
    step = pl.program_id(0)
    order_rows(step, rot_steps, row_steps, place_ref, rows_ref, (r0, r1, r2, r3), rot_ref, run_ref)

    @pl.when(step >= rot_steps)
    def _():
        line = lax.broadcasted_iota(I32, (ID_ROWS, CAP), 0)
        for j in range(step_owners):
            owner = (step - rot_steps) * step_owners + j
            begin = pl.multiple_of(start_ref[owner, 0] * 16, 16)
            run = run_ref[pl.ds(begin, CAP), :]
            ids = ids_ref[pl.ds(owner, 1), :]
            high = jnp.where(ids < 0, -1, ids // 128)
            low = ids % 128
            tail = jnp.where(line == 0, high, jnp.where(line == 1, low, 0))
            tail = tail.astype(F32).astype(BF)
            for g in range(GROUPS):
                low_ref[g, j, :HALF, :] = run[:HALF, g * 128 : (g + 1) * 128]
                low_ref[g, j, HALF:, :] = tail
                high_ref[g, j] = run[HALF:, g * 128 : (g + 1) * 128]


def second_route_kernel(rot_steps, row_steps, step_owners, start_ref, place_ref, rest_ref, rows_ref,
                        r0, r1, r2, r3, both_ref, high_ref, rot_ref, run_ref):
    step = pl.program_id(0)
    order_rows(step, rot_steps, row_steps, place_ref, rows_ref, (r0, r1, r2, r3), rot_ref, run_ref)

    @pl.when(step >= rot_steps)
    def _():
        for j in range(step_owners):
            owner = (step - rot_steps) * step_owners + j
            begin = pl.multiple_of(start_ref[owner, 0] * 16, 16)
            run = run_ref[pl.ds(begin, CAP), :]
            for g in range(GROUPS):
                both_ref[g, j, :HALF, :] = rest_ref[g, j]
                both_ref[g, j, HALF:, :] = run[:HALF, g * 128 : (g + 1) * 128]
                high_ref[g, j] = run[HALF:, g * 128 : (g + 1) * 128]


def route(half, start, place, extra, embeddings, matrix):
    step_owners = 8
    rot_steps = 2
    row_steps = 5
    depths = (HALF + ID_ROWS, HALF) if half == 0 else (CAP, HALF)
    columns = [
        pl.BlockSpec((WIDTH, 128), functools.partial(lambda col, i: (0, col), 2 * g + half))
        for g in range(GROUPS)
    ]

    def by_owner(i):
        return (0, jnp.maximum(i - rot_steps, 0), 0, 0)

    if half == 0:
        extra_spec = pl.BlockSpec((OWNERS, CAP), lambda i: (0, 0))
    else:
        extra_spec = pl.BlockSpec((GROUPS, step_owners, HALF, 128), by_owner)
    kernel = first_route_kernel if half == 0 else second_route_kernel
    return pl.pallas_call(
        functools.partial(kernel, rot_steps, row_steps, step_owners),
        grid=(rot_steps + OWNERS // step_owners,),
        in_specs=[
            pl.BlockSpec(memory_space=pltpu.SMEM),
            pl.BlockSpec((1, ROWS), lambda i: (0, 0)),
            extra_spec,
            pl.BlockSpec((ROWS // rot_steps, WIDTH), lambda i: (jnp.minimum(i, rot_steps - 1), 0)),
            *columns,
        ],
        out_specs=[pl.BlockSpec((GROUPS, step_owners, d, 128), by_owner) for d in depths],
        out_shape=[jax.ShapeDtypeStruct((GROUPS, OWNERS, d, 128), BF) for d in depths],
        scratch_shapes=[
            pltpu.VMEM((ROWS, GROUPS * 128), BF),
            pltpu.VMEM((ORDERED + CAP, GROUPS * 128), BF),
        ],
        compiler_params=params(56),
        cost_estimate=cost(8e9, 10 * MIB),
    )(start, place, extra, embeddings, matrix, matrix, matrix, matrix)


def pick_kernel(step_sources, tail_ref, centroid_ref, target_ref, out_ref, lower_ref, upper_ref, count_ref, acc_ref):
    step = pl.program_id(0)

    @pl.when(step == 0)
    def _():
        acc_ref[...] = jnp.zeros_like(acc_ref)

    slots = step_sources * CAP
    one = jnp.ones((), BF)
    zero = jnp.zeros((), BF)
    lane = lax.broadcasted_iota(I32, (CAP, 128), 1).astype(I16)
    numbers = []
    hots = []
    for j in range(step_sources):
        tail = tail_ref[j].astype(F32)
        number = tail[0:1, :] * 128.0 + tail[1:2, :]
        numbers.append(number)
        column = jnp.broadcast_to(number, (128, CAP)).T.astype(I32).astype(I16)
        hots.append(
            jnp.concatenate(
                [
                    jnp.where(column == lane + jnp.int16(128 * b), one, zero)
                    for b in range(LISTS // 128)
                ],
                axis=1,
            )
        )
    found = nn(jnp.concatenate(hots, axis=0), centroid_ref[...]).astype(BF)
    out_ref[...] = found.reshape(step_sources, CAP, 256)
    side = lax.broadcasted_iota(I32, (1, CAP), 1) < HALF
    lower = []
    upper = []
    for j in range(0, step_sources, 2):
        even, odd = numbers[j], numbers[j + 1]
        lower.append(jnp.where(side, even, pltpu.roll(odd, HALF, 1)))
        upper.append(jnp.where(side, pltpu.roll(even, HALF, 1), odd))
    lower_ref[...] = jnp.concatenate(lower, axis=1)
    upper_ref[...] = jnp.concatenate(upper, axis=1)

    live = jnp.concatenate(numbers, axis=1) >= 0
    target = jnp.where(live, target_ref[...], -1)
    high = jnp.where(live, target // 16, -1).astype(I16)
    low = (target % 16).astype(I16)
    digit = lax.broadcasted_iota(I32, (16, slots), 0).astype(I16)
    left = []
    right = []
    for m in range(16):
        left.append(jnp.where(high[m : m + 1] == digit, one, zero))
        right.append(jnp.where(low[m : m + 1] == digit, one, zero))
    acc_ref[...] += nt(jnp.concatenate(left, axis=0), jnp.concatenate(right, axis=0))

    @pl.when(step == pl.num_programs(0) - 1)
    def _():
        for m in range(16):
            block = acc_ref[m * 16 : (m + 1) * 16, m * 16 : (m + 1) * 16]
            count_ref[m] = block


def pick(rows0, centroids, targets):
    step_sources = 16
    slots = step_sources * CAP
    return pl.pallas_call(
        functools.partial(pick_kernel, step_sources),
        grid=(SOURCES // step_sources,),
        in_specs=[
            pl.BlockSpec((step_sources, ID_ROWS, CAP), lambda i: (i, HALF // ID_ROWS, 0)),
            pl.BlockSpec((LISTS, 256), lambda i: (0, 0)),
            pl.BlockSpec((16, slots), lambda i: (0, i)),
        ],
        out_specs=[
            pl.BlockSpec((step_sources, CAP, 256), lambda i: (i, 0, 0)),
            pl.BlockSpec((1, slots // 2), lambda i: (0, i)),
            pl.BlockSpec((1, slots // 2), lambda i: (0, i)),
            pl.BlockSpec((16, 16, 16), lambda i: (0, 0, 0)),
        ],
        out_shape=[
            jax.ShapeDtypeStruct((SOURCES, CAP, 256), BF),
            jax.ShapeDtypeStruct((1, HALF_SLOTS), F32),
            jax.ShapeDtypeStruct((1, HALF_SLOTS), F32),
            jax.ShapeDtypeStruct((16, 16, 16), F32),
        ],
        scratch_shapes=[pltpu.VMEM((256, 256), F32)],
        compiler_params=params(56),
        cost_estimate=cost(20e9, 12 * MIB),
    )(rows0, centroids, targets)


def book_kernel(code_ref, out_ref):
    codes = code_ref[...].astype(F32).T
    lane = lax.broadcasted_iota(I32, (CODES, 128), 1)
    for m in range(8):
        mine = jnp.where(lane // 16 == m, codes, 0.0)
        square = jnp.sum(mine * mine, axis=1, keepdims=True)
        high = square.astype(BF).astype(F32)
        middle = (square - high).astype(BF).astype(F32)
        low = square - high - middle
        tail = jnp.where(
            lane == 0, high, jnp.where(lane == 1, middle, jnp.where(lane == 2, low, 0.0))
        )
        out_ref[m * CODES : (m + 1) * CODES, :128] = (-2.0 * mine).astype(BF)
        out_ref[m * CODES : (m + 1) * CODES, 128:] = tail.astype(BF)


def make_book(codebook):
    return pl.pallas_call(
        book_kernel,
        grid=(2,),
        in_specs=[pl.BlockSpec((128, CODES), lambda i: (i, 0))],
        out_specs=pl.BlockSpec((8 * CODES, 256), lambda i: (i, 0)),
        out_shape=jax.ShapeDtypeStruct((16 * CODES, 256), BF),
        compiler_params=params(56),
        cost_estimate=cost(1e9, 3 * MIB),
    )(codebook.reshape(256, CODES))


def residual(rows_ref, pick_ref, slots):
    rows = rows_ref[...].reshape(slots, 128).astype(F32)
    centre = pick_ref[...].reshape(slots, 128).astype(F32)
    return (rows - centre).astype(BF)


def add_sums(slots, flipped, live, target, acc_ref):
    high = jnp.where(live, target // 64, -1).astype(I16)
    low = (target % 64).astype(I16)
    digit = lax.broadcasted_iota(I32, (64, slots), 0).astype(I16)
    one = jnp.ones((), BF)
    zero = jnp.zeros((), BF)
    for t in range(2):
        left = []
        right = []
        for m in range(4 * t, 4 * t + 4):
            mine = flipped[m * 16 : (m + 1) * 16]
            row = jnp.broadcast_to(high[m : m + 1], (16, slots))
            for h in range(4):
                left.append(jnp.where(row == jnp.int16(h), mine, zero))
            right.append(jnp.where(low[m : m + 1] == digit, one, zero))
        acc_ref[t] += nt(jnp.concatenate(left, axis=0), jnp.concatenate(right, axis=0))


def sum_of(acc_ref, m):
    base = (m % 4) * 64
    part = acc_ref[m // 4][:, base : base + 64]
    return jnp.concatenate([part[base + h * 16 : base + (h + 1) * 16] for h in range(4)], axis=1)


def least_errors(slots, resid, flipped, live, book_ref):
    wide = jnp.concatenate([resid, jnp.ones((slots, 128), BF)], axis=1)
    lines = []
    for m in range(8):
        mine = flipped[m * 16 : (m + 1) * 16]
        row_sq = jnp.sum(mine * mine, axis=0, keepdims=True)
        dist = nt(book_ref[m * CODES : (m + 1) * CODES], wide)
        least = jnp.min(dist, axis=0, keepdims=True)
        lines.append(jnp.where(live, row_sq + least, 0.0))
    return lines


def quarter_kernel(slots, rows_ref, pick_ref, ids_ref, target_ref, book_ref, error_ref, sum_ref, acc_ref):
    step = pl.program_id(0)

    @pl.when(step == 0)
    def _():
        acc_ref[...] = jnp.zeros_like(acc_ref)

    resid = residual(rows_ref, pick_ref, slots)
    flipped = resid.astype(F32).T
    live = ids_ref[...] >= 0
    add_sums(slots, flipped.astype(BF), live, target_ref[0], acc_ref)
    for m, line in enumerate(least_errors(slots, resid, flipped, live, book_ref)):
        error_ref[m : m + 1, :] = line

    @pl.when(step == pl.num_programs(0) - 1)
    def _():
        for m in range(8):
            sum_ref[m] = sum_of(acc_ref, m)


def quarter_specs(step_sources, half, side, place, begin=0):
    slots = step_sources * HALF
    return [
        pl.BlockSpec((step_sources, HALF, 128), lambda i: (i + begin, place, 0)),
        pl.BlockSpec((step_sources, HALF, 128), lambda i: (i + begin, side, half)),
        pl.BlockSpec((1, slots), lambda i: (0, i + begin)),
        pl.BlockSpec((1, 8, slots), lambda i: (side, half, i + begin)),
        pl.BlockSpec((8 * CODES, 256), lambda i: (half, 0)),
    ]


def quarter(half, side, place, rows, picked, ids, targets, book):
    step_sources = 32
    slots = step_sources * HALF
    return pl.pallas_call(
        functools.partial(quarter_kernel, slots),
        grid=(SOURCES // step_sources,),
        in_specs=quarter_specs(step_sources, half, side, place),
        out_specs=[
            pl.BlockSpec((8, slots), lambda i: (0, i)),
            pl.BlockSpec((8, 16, CODES), lambda i: (0, 0, 0)),
        ],
        out_shape=[
            jax.ShapeDtypeStruct((8, HALF_SLOTS), F32),
            jax.ShapeDtypeStruct((8, 16, CODES), F32),
        ],
        scratch_shapes=[pltpu.VMEM((2, 256, 256), F32)],
        compiler_params=params(56),
        cost_estimate=cost(11e9, 5 * MIB),
    )(rows, picked, ids, targets, book)


def last_sums_kernel(slots, rows_ref, pick_ref, ids_ref, target_ref, s00, s01, s10, count_ref, out_ref, acc_ref):
    step = pl.program_id(0)

    @pl.when(step == 0)
    def _():
        acc_ref[...] = jnp.zeros_like(acc_ref)
        out_ref[:, 16:, :] = jnp.zeros((OWNERS, 8, 128), F32)

    resid = residual(rows_ref, pick_ref, slots)
    flipped = resid.astype(F32).T.astype(BF)
    add_sums(slots, flipped, ids_ref[...] >= 0, target_ref[0], acc_ref)

    @pl.when(step == pl.num_programs(0) - 1)
    def _():
        for m in range(16):
            total = s00[m] + s01[m] if m < 8 else s10[m - 8] + sum_of(acc_ref, m - 8)
            for h in range(2):
                out_ref[2 * m + h, :8, :] = total[8 * h : 8 * h + 8, :128]
                out_ref[2 * m + h, 8:16, :] = total[8 * h : 8 * h + 8, 128:]
                out_ref[2 * m + h, 16:18, :] = count_ref[m]


def last_sums(rows, picked, ids, targets, s00, s01, s10, counts):
    step_sources = 32
    slots = step_sources * HALF
    whole = [pl.BlockSpec((8, 16, CODES), lambda i: (0, 0, 0))] * 3
    return pl.pallas_call(
        functools.partial(last_sums_kernel, slots),
        grid=(SOURCES // step_sources,),
        in_specs=[
            *quarter_specs(step_sources, 1, 1, 0)[:4],
            *whole,
            pl.BlockSpec((16, 2, 128), lambda i: (0, 0, 0)),
        ],
        out_specs=pl.BlockSpec((OWNERS, 24, 128), lambda i: (0, 0, 0)),
        out_shape=jax.ShapeDtypeStruct((OWNERS, 24, 128), F32),
        scratch_shapes=[pltpu.VMEM((2, 256, 256), F32)],
        compiler_params=params(56),
        cost_estimate=cost(2e9, 5 * MIB),
    )(rows, picked, ids, targets, s00, s01, s10, counts)


def last_errors_kernel(slots, rows_ref, pick_ref, ids_ref, target_ref, book_ref, e00, e01, e10, *rest):
    del target_ref
    out_ref = rest[-1]
    resid = residual(rows_ref, pick_ref, slots)
    flipped = resid.astype(F32).T
    last = least_errors(slots, resid, flipped, ids_ref[...] >= 0, book_ref)
    e11 = jnp.concatenate(last, axis=0)
    side = lax.broadcasted_iota(I32, (8, CAP), 1) < HALF
    for at, (lower, upper) in enumerate(((e00[...], e01[...]), (e10[...], e11))):
        for b in range(slots // CAP):
            low = lower[:, b * CAP : (b + 1) * CAP]
            up = upper[:, b * CAP : (b + 1) * CAP]
            even = jnp.where(side, low, pltpu.roll(up, HALF, 1))
            odd = jnp.where(side, pltpu.roll(low, HALF, 1), up)
            out_ref[8 * at : 8 * at + 8, 2 * b * CAP : (2 * b + 1) * CAP] = even
            out_ref[8 * at : 8 * at + 8, (2 * b + 1) * CAP : (2 * b + 2) * CAP] = odd


def last_errors(begin, end, rows, picked, ids, targets, book, e00, e01, e10, before):
    step_sources = 16
    slots = step_sources * HALF
    block = [pl.BlockSpec((8, slots), lambda i: (0, i + begin))] * 3
    earlier = [] if before is None else [before]
    return pl.pallas_call(
        functools.partial(last_errors_kernel, slots),
        grid=(end - begin,),
        in_specs=[
            *quarter_specs(step_sources, 1, 1, 0, begin),
            *block,
            *[pl.BlockSpec(memory_space=pl.ANY) for _ in earlier],
        ],
        out_specs=pl.BlockSpec((16, 2 * slots), lambda i: (0, i + begin)),
        out_shape=jax.ShapeDtypeStruct((16, SLOTS), F32),
        input_output_aliases={} if before is None else {8: 0},
        compiler_params=params(56),
        cost_estimate=cost(1.1e9 * (end - begin), (end - begin) * MIB),
    )(rows, picked, ids, targets, book, e00, e01, e10, *earlier)


def piece_kernel(got_ref, code_ref, out_ref):
    total = jnp.sum(got_ref[...], axis=0)
    codes = code_ref[...]
    low = (codes[:, :128] + total[:8]) / (1.0 + total[16:17])
    high = (codes[:, 128:] + total[8:16]) / (1.0 + total[17:18])
    piece = jnp.concatenate([low, high], axis=1)
    out_ref[...] = jnp.broadcast_to(piece[None], (OWNERS, 8, CODES))


def new_piece(got, codes):
    return pl.pallas_call(
        piece_kernel,
        out_shape=jax.ShapeDtypeStruct((OWNERS, 8, CODES), F32),
        compiler_params=pltpu.CompilerParams(vmem_limit_bytes=56 * MIB),
        cost_estimate=cost(1e6, MIB),
    )(got, codes)


def exchange(x, axes):
    return lax.all_to_all(x, axes, split_axis=0, concat_axis=0, tiled=True)


def per_device(
    embeddings, owner_of_row, list_in_owner, opq_matrix, centroids, codebook, code_targets
):
    every = ("sub", "lists")
    place, start, ids = rank_rows(owner_of_row.reshape(1, ROWS), list_in_owner.reshape(1, ROWS))
    send_a, rest = route(0, start, place, ids, embeddings, opq_matrix)
    rows_a = exchange(send_a.reshape(SOURCES, HALF + ID_ROWS, 128), every)
    send_b, send_c = route(1, start, place, rest, embeddings, opq_matrix)
    book = make_book(codebook)
    targets = code_targets.reshape(16, SOURCES, 2, HALF).transpose(2, 0, 1, 3)
    targets = targets.reshape(2, 16, HALF_SLOTS)
    me = lax.axis_index("lists")
    codes = codebook.astype(F32).reshape(OWNERS, 8, CODES)
    codes = lax.dynamic_slice(codes, (me, 0, 0), (1, 8, CODES))[0]
    send_b, book, targets, codes = lax.optimization_barrier((send_b, book, targets, codes))
    rows_b = exchange(send_b.reshape(SOURCES, CAP, 128), every)
    picked, lower, upper, counts = pick(rows_a, centroids, code_targets)
    counts = counts.reshape(16, 2, 128)
    e00, s00 = quarter(0, 0, 0, rows_a, picked, lower, targets, book)
    send_c, e00, counts = lax.optimization_barrier((send_c, e00, counts))
    rows_c = exchange(send_c.reshape(SOURCES, HALF, 128), every)
    e01, s01 = quarter(0, 1, 0, rows_b, picked, upper, targets, book)
    e10, s10 = quarter(1, 0, 1, rows_b, picked, lower, targets, book)
    rows_c, s01, s10 = lax.optimization_barrier((rows_c, s01, s10))
    pieces = last_sums(rows_c, picked, upper, targets, s00, s01, s10, counts)
    quant_error = last_errors(0, 2, rows_c, picked, upper, targets, book, e00, e01, e10, None)
    got = exchange(pieces, "lists")
    piece, quant_error = lax.optimization_barrier((new_piece(got, codes), quant_error))
    spread = exchange(piece, "lists")
    quant_error = last_errors(
        2, 8, rows_c, picked, upper, targets, book, e00, e01, e10, quant_error
    )
    return quant_error, spread.reshape(16, 16, CODES)


def solution(mesh):
    placed = (
        P(("lists", "sub"), None),
        P(("lists", "sub"), None),
        P(("lists", "sub")),
        P(),
        P("lists", "sub"),
        P("sub", None, None),
        P("sub", "lists"),
    )
    return jax.shard_map(
        per_device,
        mesh=mesh,
        in_specs=placed,
        out_specs=(P("sub", "lists"), P("sub", None, None)),
        check_vma=False,
    )
```

time: 236 us -> 199 us (0.84)
  waiting for transfers between devices: 59.9 us -> 29.6 us
  starting transfers between devices: 39.5 us -> 32.7 us
  local copies, waits for them, and re-layouts: 6.76 us -> 10.8 us
  Pallas kernels: 127 us -> 123 us
    all_to_all x5, waiting for transfers between devices: 59.9 us -> 29.6 us  [exchange(): return lax.all_to_all(x, axes, split_axis=0, concat_axis=0, tiled=True)]
    all_to_all x5, starting transfers between devices: 39.5 us -> 32.7 us  [exchange(): return lax.all_to_all(x, axes, split_axis=0, concat_axis=0, tiled=True)]
    pallas_call x6 -> x9, Pallas kernels: 99.6 us -> 94.1 us  [the longest x3 43.5 us: quarter(): pl.pallas_call(functools.partial(quarter_kernel, slots), grid=(SOURCES //...]
    reshape x1 -> x3, local copies, waits for them, and re-layouts: 0.72 us -> 6.14 us  [the longest x1 2.89 us: per_device(): targets = code_targets.reshape(16, SOURCES, 2, HALF).transpose(2, 0, 1, 3)]
  transfers between devices with their start and end apart: 5 -> 5, of which waited for: 3 -> 4; matrix products, arithmetic and copies ran while one was open for 0% -> 5% of each run, Pallas kernels for 50% -> 51%
where the time goes in v2:
time: 199 us; the launch traced here: 198 us
  Pallas kernels  123 us (62%)
  starting transfers between devices  32.7 us (16%)
  waiting for transfers between devices  29.6 us (15%)
  local copies, waits for them, and re-layouts  10.8 us (5%)
    pallas_call x3, Pallas kernels, quarter(): pl.pallas_call(functools.partial(quarter_kernel, slots), grid=(SOURCES //...  43.5 us
    all_to_all x5, starting transfers between devices, exchange(): return lax.all_to_all(x, axes, split_axis=0, concat_axis=0, tiled=True)  32.7 us
    all_to_all x5, waiting for transfers between devices, exchange(): return lax.all_to_all(x, axes, split_axis=0, concat_axis=0, tiled=True)  29.6 us
    pallas_call x2, Pallas kernels, route(): pl.pallas_call(functools.partial(kernel, rot_steps, row_steps, step_owner...  27.1 us
    pallas_call x1, Pallas kernels, pick(): pl.pallas_call(functools.partial(pick_kernel, step_sources), grid=(SOURCE...  24.3 us
    pallas_call x2, Pallas kernels, last_errors(): pl.pallas_call(functools.partial(last_errors_kernel, slots), grid=(end -...  15.8 us
    pallas_call x1, Pallas kernels, last_sums(): pl.pallas_call(functools.partial(last_sums_kernel, slots), grid=(SOURCES...  5.89 us
  transfers between devices with their start and end apart: 5, of which 4 were waited for; matrix products, arithmetic and copies ran while one was open for 5% of the time, Pallas kernels for 51%

profile of v2, /device:TPU:1, one launch (start us, length us, event | category | flops | bytes accessed | tf_op | source)
XLA Modules:
  0.0 198.3 jit_solution(9822155170434660810)
XLA Ops:
  0.6 1.8 shard_map.86
  2.5 13.0 %shard_map.87 = (bf16[4,32,80,128]{3,2,1,0:T(8,128)(2,1)}, bf16[4,32,64,128]{3,2,1,0:T(8,128)(2,1)}) custom-call(s32[32,128]{1,0:T(8,128)} %get-tuple-element.31.start_ref, s32[1,2048]{1,0:T(1,128)} %get-tuple-element.32.place_ref, s32[32,128]{1,0:T(8,128)} %get-tuple-element.33.ids_ref, bf16[2048,1024]{1,0:T(8,128)(2,1)} %rows_ref.3, ...), custom_call_target="tpu_custom_call" | custom-call | flops 8000000000 | bytes 10485760 | tf_op jit(solution)/shard_map/pallas_call | solution.py:183
  15.4 11.9 %all-to-all-start = ((bf16[128,80,128]{2,1,0:T(8,128)(2,1)}), bf16[128,80,128]{2,1,0:T(8,128)(2,1)}, u32[]{:S(2)}, u32[]{:S(2)}) async-start(bf16[128,80,128]{2,1,0:T(8,128)(2,1)} %bitcast.16), calls=%async_computation | async-start | bytes 5242880 | tf_op jit(solution)/shard_map/all_to_all | solution.py:513
  27.4 2.9 %reshape.44 = s32[16,128,2,64]{3,2,1,0:T(2,128)} reshape(s32[16,16384]{1,0:T(8,128)S(1)} %copy-done.2) | data formatting | bytes 2097152 | tf_op jit(solution)/shard_map/reshape | solution.py:525
  30.3 1.8 copy.11
  32.1 1.6 reshape.45.target_ref
  33.7 2.9 %shard_map.90.book_ref = bf16[4096,256]{1,0:T(8,128)(2,1)} custom-call(bf16[256,256]{1,0:T(8,128)(2,1)} %bitcast.19), custom_call_target="tpu_custom_call" | custom-call | flops 1000000000 | bytes 3145728 | tf_op jit(solution)/shard_map/pallas_call | solution.py:308
  37.9 14.2 %shard_map.88 = (bf16[4,32,128,128]{3,2,1,0:T(8,128)(2,1)}, bf16[4,32,64,128]{3,2,1,0:T(8,128)(2,1)}) custom-call(s32[32,128]{1,0:T(8,128)} %get-tuple-element.31.start_ref, s32[1,2048]{1,0:T(1,128)} %get-tuple-element.32.place_ref, bf16[4,32,64,128]{3,2,1,0:T(8,128)(2,1)} %get-tuple-element.34.rest_ref, bf16[2048,1024]{1,0:T(8,128)(2,1)} %rows_ref.3, ...), custom_call_target="tpu_custom_call" | custom-call | flops 8000000000 | bytes 10485760 | tf_op jit(solution)/shard_map/pallas_call | solution.py:183
  52.1 10.7 %all-to-all-done.tail_ref.rows_ref = bf16[128,80,128]{2,1,0:T(8,128)(2,1)} async-done(((bf16[128,80,128]{2,1,0:T(8,128)(2,1)}), bf16[128,80,128]{2,1,0:T(8,128)(2,1)}, u32[]{:S(2)}, u32[]{:S(2)}) %all-to-all-start) | async-done | bytes 2621472 | tf_op jit(solution)/shard_map/all_to_all | solution.py:513
  62.8 6.1 %all-to-all-start.2 = ((bf16[128,128,128]{2,1,0:T(8,128)(2,1)}), bf16[128,128,128]{2,1,0:T(8,128)(2,1)}, u32[]{:S(2)}, u32[]{:S(2)}) async-start(bf16[128,128,128]{2,1,0:T(8,128)(2,1)} %bitcast.15), calls=%async_computation.2 | async-start | bytes 8388608 | tf_op jit(solution)/shard_map/all_to_all | solution.py:513
  68.9 24.3 %shard_map.89 = (bf16[128,128,256]{2,1,0:T(8,128)(2,1)}, f32[1,8192]{1,0:T(1,128)}, f32[1,8192]{1,0:T(1,128)}, f32[16,16,16]{2,1,0:T(8,128)}) custom-call(bf16[128,80,128]{2,1,0:T(8,128)(2,1)} %all-to-all-done.tail_ref.rows_ref, bf16[2048,256]{1,0:T(8,128)(2,1)} %centroid_ref.1, s32[16,16384]{1,0:T(8,128)} %target_ref.1), custom_call_target="tpu_custom_call" | custom-call | flops 20000000000 | bytes 12582912 | tf_op jit(solution)/shard_map/pallas_call | solution.py:265
  93.2 1.6 reshape.48.count_ref
  94.8 14.5 %shard_map.91 = (f32[8,8192]{1,0:T(8,128)}, f32[8,16,256]{2,1,0:T(8,128)}) custom-call(bf16[128,80,128]{2,1,0:T(8,128)(2,1)} %all-to-all-done.tail_ref.rows_ref, bf16[128,128,256]{2,1,0:T(8,128)(2,1)} %get-tuple-element.37.pick_ref, f32[1,8192]{1,0:T(1,128)} %get-tuple-element.38.ids_ref, s32[2,16,8192]{2,1,0:T(8,128)} %reshape.45.target_ref, ...), custom_call_target="tpu_custom_call" | custom-call | flops 11000000512 | bytes 5242880 | tf_op jit(solution)/shard_map/pallas_call | solution.py:395
  109.3 12.3 %all-to-all-done.2.rows_ref = bf16[128,128,128]{2,1,0:T(8,128)(2,1)} async-done(((bf16[128,128,128]{2,1,0:T(8,128)(2,1)}), bf16[128,128,128]{2,1,0:T(8,128)(2,1)}, u32[]{:S(2)}, u32[]{:S(2)}) %all-to-all-start.2) | async-done | bytes 4194336 | tf_op jit(solution)/shard_map/all_to_all | solution.py:513
  121.6 4.5 %all-to-all-start.1 = ((bf16[128,64,128]{2,1,0:T(8,128)(2,1)}), bf16[128,64,128]{2,1,0:T(8,128)(2,1)S(1)}, u32[]{:S(2)}, u32[]{:S(2)}) async-start(bf16[128,64,128]{2,1,0:T(8,128)(2,1)} %bitcast.17), calls=%async_computation.1 | async-start | bytes 4194304 | tf_op jit(solution)/shard_map/all_to_all | solution.py:513
  126.1 14.5 %shard_map.93 = (f32[8,8192]{1,0:T(8,128)}, f32[8,16,256]{2,1,0:T(8,128)}) custom-call(bf16[128,128,128]{2,1,0:T(8,128)(2,1)} %all-to-all-done.2.rows_ref, bf16[128,128,256]{2,1,0:T(8,128)(2,1)} %get-tuple-element.37.pick_ref, f32[1,8192]{1,0:T(1,128)} %get-tuple-element.38.ids_ref, s32[2,16,8192]{2,1,0:T(8,128)} %reshape.45.target_ref, ...), custom_call_target="tpu_custom_call" | custom-call | flops 11000000512 | bytes 5242880 | tf_op jit(solution)/shard_map/pallas_call | solution.py:395
  140.7 14.5 %shard_map.92 = (f32[8,8192]{1,0:T(8,128)}, f32[8,16,256]{2,1,0:T(8,128)}) custom-call(bf16[128,128,128]{2,1,0:T(8,128)(2,1)} %all-to-all-done.2.rows_ref, bf16[128,128,256]{2,1,0:T(8,128)(2,1)} %get-tuple-element.37.pick_ref, f32[1,8192]{1,0:T(1,128)} %get-tuple-element.46.ids_ref, s32[2,16,8192]{2,1,0:T(8,128)} %reshape.45.target_ref, ...), custom_call_target="tpu_custom_call" | custom-call | flops 11000000512 | bytes 5242880 | tf_op jit(solution)/shard_map/pallas_call | solution.py:395
  157.9 5.9 %shard_map.94 = f32[32,24,128]{2,1,0:T(8,128)} custom-call(bf16[128,64,128]{2,1,0:T(8,128)(2,1)} %copy-done, bf16[128,128,256]{2,1,0:T(8,128)(2,1)} %get-tuple-element.37.pick_ref, f32[1,8192]{1,0:T(1,128)} %get-tuple-element.46.ids_ref, s32[2,16,8192]{2,1,0:T(8,128)} %reshape.45.target_ref, f32[8,16,256]{2,1,0:T(8,128)} %get-tuple-element.53.s00, ...), custom_call_target="tpu_custom_call" | custom-call | flops 2000000000 | bytes 5242880 | tf_op jit(solution)/shard_map/pallas_call | solution.py:439
  163.8 6.6 %all-to-all-start.3 = ((f32[32,24,128]{2,1,0:T(8,128)}), f32[32,24,128]{2,1,0:T(8,128)S(1)}, u32[]{:S(2)}, u32[]{:S(2)}) async-start(f32[32,24,128]{2,1,0:T(8,128)} %shard_map.94), calls=%async_computation.3 | async-start | bytes 786432 | tf_op jit(solution)/shard_map/all_to_all | solution.py:513
  170.4 5.0 %shard_map.96.rest_0_ = f32[16,16384]{1,0:T(8,128)} custom-call(bf16[128,64,128]{2,1,0:T(8,128)(2,1)} %copy-done, bf16[128,128,256]{2,1,0:T(8,128)(2,1)} %get-tuple-element.37.pick_ref, f32[1,8192]{1,0:T(1,128)} %get-tuple-element.46.ids_ref, s32[2,16,8192]{2,1,0:T(8,128)} %reshape.45.target_ref, bf16[4096,256]{1,0:T(8,128)(2,1)} %shard_map.90.book_ref, ...), custom_call_target="tpu_custom_call" | custom-call | flops 2200000000 | bytes 2097152 | tf_op jit(solution)/shard_map/pallas_call | solution.py:478
  175.4 5.3 %all-to-all-done.3.got_ref = f32[32,24,128]{2,1,0:T(8,128)S(1)} async-done(((f32[32,24,128]{2,1,0:T(8,128)}), f32[32,24,128]{2,1,0:T(8,128)S(1)}, u32[]{:S(2)}, u32[]{:S(2)}) %all-to-all-start.3) | async-done | bytes 393248 | tf_op jit(solution)/shard_map/all_to_all | solution.py:513
  181.4 1.8 shard_map.95
  183.2 3.7 %all-to-all-start.4 = ((f32[32,8,256]{2,1,0:T(8,128)}), f32[32,8,256]{2,1,0:T(8,128)S(1)}, u32[]{:S(2)}, u32[]{:S(2)}) async-start(f32[32,8,256]{2,1,0:T(8,128)} %shard_map.95), calls=%async_computation.4 | async-start | bytes 524288 | tf_op jit(solution)/shard_map/all_to_all | solution.py:513
  186.8 10.8 %shard_map.97 = f32[16,16384]{1,0:T(8,128)} custom-call(bf16[128,64,128]{2,1,0:T(8,128)(2,1)} %copy-done, bf16[128,128,256]{2,1,0:T(8,128)(2,1)} %get-tuple-element.37.pick_ref, f32[1,8192]{1,0:T(1,128)} %get-tuple-element.46.ids_ref, s32[2,16,8192]{2,1,0:T(8,128)} %reshape.45.target_ref, ...), custom_call_target="tpu_custom_call", output_to_operand_aliasing={{}: (8, {})} | custom-call | flops 6600000000 | bytes 6291456 | tf_op jit(solution)/shard_map/pallas_call | solution.py:478
  (10 shorter events, 5.4 us)
Async XLA Ops:
  15.4 11.9 %copy-start.2 = (s32[16,16384]{1,0:T(8,128)S(1)}, s32[16,16384]{1,0:T(8,128)}, u32[]{:S(2)}) copy-start(s32[16,16384]{1,0:T(8,128)} %target_ref.1) | copy-start | bytes 3145732
  15.4 47.3 %all-to-all-start = ((bf16[128,80,128]{2,1,0:T(8,128)(2,1)}), bf16[128,80,128]{2,1,0:T(8,128)(2,1)}, u32[]{:S(2)}, u32[]{:S(2)}) async-start(bf16[128,80,128]{2,1,0:T(8,128)(2,1)} %bitcast.16), calls=%async_computation | async-start | bytes 5242880 | tf_op jit(solution)/shard_map/all_to_all | solution.py:513
  62.8 58.8 %all-to-all-start.2 = ((bf16[128,128,128]{2,1,0:T(8,128)(2,1)}), bf16[128,128,128]{2,1,0:T(8,128)(2,1)}, u32[]{:S(2)}, u32[]{:S(2)}) async-start(bf16[128,128,128]{2,1,0:T(8,128)(2,1)} %bitcast.15), calls=%async_computation.2 | async-start | bytes 8388608 | tf_op jit(solution)/shard_map/all_to_all | solution.py:513
  121.6 34.9 %all-to-all-start.1 = ((bf16[128,64,128]{2,1,0:T(8,128)(2,1)}), bf16[128,64,128]{2,1,0:T(8,128)(2,1)S(1)}, u32[]{:S(2)}, u32[]{:S(2)}) async-start(bf16[128,64,128]{2,1,0:T(8,128)(2,1)} %bitcast.17), calls=%async_computation.1 | async-start | bytes 4194304 | tf_op jit(solution)/shard_map/all_to_all | solution.py:513
  156.5 1.4 copy-start
  163.8 16.9 %all-to-all-start.3 = ((f32[32,24,128]{2,1,0:T(8,128)}), f32[32,24,128]{2,1,0:T(8,128)S(1)}, u32[]{:S(2)}, u32[]{:S(2)}) async-start(f32[32,24,128]{2,1,0:T(8,128)} %shard_map.94), calls=%async_computation.3 | async-start | bytes 786432 | tf_op jit(solution)/shard_map/all_to_all | solution.py:513
  180.7 0.7 copy-start.1
  183.2 14.5 %all-to-all-start.4 = ((f32[32,8,256]{2,1,0:T(8,128)}), f32[32,8,256]{2,1,0:T(8,128)S(1)}, u32[]{:S(2)}, u32[]{:S(2)}) async-start(f32[32,8,256]{2,1,0:T(8,128)} %shard_map.95), calls=%async_computation.4 | async-start | bytes 524288 | tf_op jit(solution)/shard_map/all_to_all | solution.py:513

commit v3 on v2

--- a/solution.py
+++ b/solution.py
@@ -43,18 +43,22 @@
     )
 
 
-def rank_kernel(owner_ref, list_ref, place_ref, start_ref, ids_ref):
-    owner = owner_ref[...]
-    lists = list_ref[...]
+ORDERED = ROWS + 16 * OWNERS
+ID_ROWS = 8
+HALF = CAP // 2
+HALF_SLOTS = SOURCES * HALF
+
+
+def rank_rows(owner, lists):
     owner_hot = (owner == lax.broadcasted_iota(I32, (OWNERS, ROWS), 0)).astype(F32)
     before = (
         lax.broadcasted_iota(I32, (128, 128), 0) < lax.broadcasted_iota(I32, (128, 128), 1)
-    ).astype(F32).astype(BF)
+    ).astype(F32)
     blocks = ROWS // 128
     stacked = jnp.concatenate(
         [owner_hot[:, b * 128 : (b + 1) * 128] for b in range(blocks)], axis=0
     ).astype(BF)
-    inside = nn(stacked, before)
+    inside = nn(stacked, before.astype(BF))
     ranks = []
     carry = jnp.zeros((OWNERS, 1), F32)
     for b in range(blocks):
@@ -64,52 +68,134 @@
         carry = carry + jnp.sum(hot, axis=1, keepdims=True)
     rank = jnp.concatenate(ranks, axis=1)
     pages = ((carry.astype(I32) + 15) // 16).astype(F32).astype(BF)
-    first = nn(before[:OWNERS, :OWNERS].astype(F32).T.astype(BF), jnp.broadcast_to(pages, (OWNERS, 128)))
+    after = before[:OWNERS, :OWNERS].T.astype(BF)
+    first = nn(after, jnp.broadcast_to(pages, (OWNERS, 128)))
     begin = jnp.sum(owner_hot * first[:, :1], axis=0, keepdims=True) * 16.0
-    place_ref[...] = (begin + rank).astype(I32)
-    start_ref[...] = first.astype(I32)
-    rank_hot = (rank.astype(I32) == lax.broadcasted_iota(I32, (CAP, ROWS), 0)).astype(F32).astype(BF)
+    place = (begin + rank).astype(I32)
+    rank = rank.astype(I32)
+    rank_hot = (rank == lax.broadcasted_iota(I32, (CAP, ROWS), 0)).astype(F32).astype(BF)
     high = (lists // 128).astype(F32)
     low = (lists % 128).astype(F32)
     left = jnp.concatenate([owner_hot * high, owner_hot * low, owner_hot], axis=0).astype(BF)
     found = nt(left, rank_hot)
     number = found[:OWNERS] * 128.0 + found[OWNERS : 2 * OWNERS]
-    live = found[2 * OWNERS :]
-    ids_ref[...] = (number + live - 1.0).astype(I32)
-
-
-def rank_rows(owner, lists):
+    ids = (number + found[2 * OWNERS :] - 1.0).astype(I32)
+    return rank, place, first.astype(I32), ids
+
+
+def matrix_columns(half):
+    return [
+        pl.BlockSpec((WIDTH, 128), functools.partial(lambda col, i: (0, col), 2 * g + half))
+        for g in range(GROUPS)
+    ]
+
+
+def first_route_kernel(parts, step_owners, owner_ref, list_ref, rows_hbm, r0, r1, r2, r3,
+                       low_ref, rot_hbm, place_ref, start_ref,
+                       slot_ref, ids_ref, rows_ref, rot_ref, in_sem, out_sem):
+    step = pl.program_id(0)
+    part_rows = ROWS // parts
+    count = step_owners * HALF
+
+    def kept():
+        return pltpu.make_async_copy(rot_ref, rot_hbm, out_sem)
+
+    @pl.when(step == 0)
+    def _():
+        copies = []
+        for k in range(parts):
+            part = pl.ds(k * part_rows, part_rows)
+            copies.append(
+                pltpu.make_async_copy(rows_hbm.at[part], rows_ref.at[part], in_sem.at[k])
+            )
+            copies[k].start()
+        owner = owner_ref[...]
+        rank, place, first, ids = rank_rows(owner, list_ref[...])
+        place_ref[...] = place
+        start_ref[...] = first
+        ids_ref[...] = ids
+        slot_ref[...] = jnp.where(rank < HALF, owner * HALF + rank, -1)
+        matrix = jnp.concatenate([r[...] for r in (r0, r1, r2, r3)], axis=1)
+        for k in range(parts):
+            part = pl.ds(k * part_rows, part_rows)
+            copies[k].wait()
+            rot_ref[part, :] = nn(rows_ref[part, :], matrix).astype(BF)
+        kept().start()
+
+    slot = (slot_ref[...] - step * count).astype(I16)
+    digit = lax.broadcasted_iota(I32, (count, ROWS), 0).astype(I16)
+    hot = jnp.where(slot == digit, jnp.ones((), BF), jnp.zeros((), BF))
+    sent = nn(hot, rot_ref[...]).astype(BF)
+    line = lax.broadcasted_iota(I32, (ID_ROWS, CAP), 0)
+    for j in range(step_owners):
+        ids = ids_ref[pl.ds(step * step_owners + j, 1), :]
+        high = jnp.where(ids < 0, -1, ids // 128)
+        low = ids % 128
+        tail = jnp.where(line == 0, high, jnp.where(line == 1, low, 0))
+        tail = tail.astype(F32).astype(BF)
+        for g in range(GROUPS):
+            low_ref[g, j, :HALF, :] = sent[j * HALF : (j + 1) * HALF, g * 128 : (g + 1) * 128]
+            low_ref[g, j, HALF:, :] = tail
+
+    @pl.when(step == pl.num_programs(0) - 1)
+    def _():
+        kept().wait()
+
+
+def first_route(owner, lists, embeddings, matrix):
+    step_owners = 16
+    parts = 4
+    depth = HALF + ID_ROWS
     return pl.pallas_call(
-        rank_kernel,
+        functools.partial(first_route_kernel, parts, step_owners),
+        grid=(OWNERS // step_owners,),
+        in_specs=[
+            pl.BlockSpec((1, ROWS), lambda i: (0, 0)),
+            pl.BlockSpec((1, ROWS), lambda i: (0, 0)),
+            pl.BlockSpec(memory_space=pl.ANY),
+            *matrix_columns(0),
+        ],
+        out_specs=[
+            pl.BlockSpec((GROUPS, step_owners, depth, 128), lambda i: (0, i, 0, 0)),
+            pl.BlockSpec(memory_space=pl.ANY),
+            pl.BlockSpec((1, ROWS), lambda i: (0, 0)),
+            pl.BlockSpec((OWNERS, 128), lambda i: (0, 0)),
+        ],
         out_shape=[
+            jax.ShapeDtypeStruct((GROUPS, OWNERS, depth, 128), BF),
+            jax.ShapeDtypeStruct((ROWS, GROUPS * 128), BF),
             jax.ShapeDtypeStruct((1, ROWS), I32),
             jax.ShapeDtypeStruct((OWNERS, 128), I32),
-            jax.ShapeDtypeStruct((OWNERS, CAP), I32),
-        ],
-        compiler_params=pltpu.CompilerParams(vmem_limit_bytes=56 * MIB),
-        cost_estimate=cost(1e9, 100000),
-    )(owner, lists)
-
-
-ORDERED = ROWS + 16 * OWNERS
-ID_ROWS = 16
-HALF = CAP // 2
-HALF_SLOTS = SOURCES * HALF
-
-
-def order_rows(step, rot_steps, row_steps, place_ref, rows_ref, columns, rot_ref, run_ref):
+        ],
+        scratch_shapes=[
+            pltpu.VMEM((1, ROWS), I32),
+            pltpu.VMEM((OWNERS, CAP), I32),
+            pltpu.VMEM((ROWS, WIDTH), BF),
+            pltpu.VMEM((ROWS, GROUPS * 128), BF),
+            pltpu.SemaphoreType.DMA((parts,)),
+            pltpu.SemaphoreType.DMA,
+        ],
+        compiler_params=params(60),
+        cost_estimate=cost(8e9, 10 * MIB),
+    )(owner, lists, embeddings, matrix, matrix, matrix, matrix)
+
+
+def second_route_kernel(rot_steps, row_steps, step_owners, start_ref, place_ref, rot0_ref, rows_ref,
+                        r0, r1, r2, r3, both_ref, high_ref, rot_ref, run_ref):
+    step = pl.program_id(0)
     rot_rows = ROWS // rot_steps
     run_rows = ORDERED // row_steps
+    wide = GROUPS * 128
 
     @pl.when(step < rot_steps)
     def _():
-        matrix = jnp.concatenate([r[...] for r in columns], axis=1)
+        matrix = jnp.concatenate([r[...] for r in (r0, r1, r2, r3)], axis=1)
         at = pl.multiple_of(step * rot_rows, rot_rows)
         rot_ref[pl.ds(at, rot_rows), :] = nn(rows_ref[...], matrix).astype(BF)
 
     @pl.when(step == 0)
     def _():
-        run_ref[ORDERED:, :] = jnp.zeros((CAP, GROUPS * 128), BF)
+        run_ref[ORDERED:, :] = jnp.zeros((CAP, 2 * wide), BF)
 
     @pl.when(step == rot_steps)
     def _():
@@ -119,36 +205,9 @@
         for k in range(row_steps):
             place = (place_ref[...] - k * run_rows).astype(I16)
             hot = jnp.where(place == digit, one, zero)
-            run_ref[k * run_rows : (k + 1) * run_rows, :] = nn(hot, rot_ref[...]).astype(BF)
-
-
-def first_route_kernel(rot_steps, row_steps, step_owners, start_ref, place_ref, ids_ref, rows_ref,
-                       r0, r1, r2, r3, low_ref, high_ref, rot_ref, run_ref):
-    step = pl.program_id(0)
-    order_rows(step, rot_steps, row_steps, place_ref, rows_ref, (r0, r1, r2, r3), rot_ref, run_ref)
-
-    @pl.when(step >= rot_steps)
-    def _():
-        line = lax.broadcasted_iota(I32, (ID_ROWS, CAP), 0)
-        for j in range(step_owners):
-            owner = (step - rot_steps) * step_owners + j
-            begin = pl.multiple_of(start_ref[owner, 0] * 16, 16)
-            run = run_ref[pl.ds(begin, CAP), :]
-            ids = ids_ref[pl.ds(owner, 1), :]
-            high = jnp.where(ids < 0, -1, ids // 128)
-            low = ids % 128
-            tail = jnp.where(line == 0, high, jnp.where(line == 1, low, 0))
-            tail = tail.astype(F32).astype(BF)
-            for g in range(GROUPS):
-                low_ref[g, j, :HALF, :] = run[:HALF, g * 128 : (g + 1) * 128]
-                low_ref[g, j, HALF:, :] = tail
-                high_ref[g, j] = run[HALF:, g * 128 : (g + 1) * 128]
-
-
-def second_route_kernel(rot_steps, row_steps, step_owners, start_ref, place_ref, rest_ref, rows_ref,
-                        r0, r1, r2, r3, both_ref, high_ref, rot_ref, run_ref):
-    step = pl.program_id(0)
-    order_rows(step, rot_steps, row_steps, place_ref, rows_ref, (r0, r1, r2, r3), rot_ref, run_ref)
+            part = slice(k * run_rows, (k + 1) * run_rows)
+            run_ref[part, :wide] = nn(hot, rot0_ref[...]).astype(BF)
+            run_ref[part, wide:] = nn(hot, rot_ref[...]).astype(BF)
 
     @pl.when(step >= rot_steps)
     def _():
@@ -157,48 +216,39 @@
             begin = pl.multiple_of(start_ref[owner, 0] * 16, 16)
             run = run_ref[pl.ds(begin, CAP), :]
             for g in range(GROUPS):
-                both_ref[g, j, :HALF, :] = rest_ref[g, j]
-                both_ref[g, j, HALF:, :] = run[:HALF, g * 128 : (g + 1) * 128]
-                high_ref[g, j] = run[HALF:, g * 128 : (g + 1) * 128]
-
-
-def route(half, start, place, extra, embeddings, matrix):
+                mine = slice(g * 128, (g + 1) * 128)
+                both_ref[g, j, :HALF, :] = run[HALF:, mine]
+                both_ref[g, j, HALF:, :] = run[:HALF, wide + g * 128 : wide + (g + 1) * 128]
+                high_ref[g, j] = run[HALF:, wide + g * 128 : wide + (g + 1) * 128]
+
+
+def second_route(start, place, rot0, embeddings, matrix):
     step_owners = 8
     rot_steps = 2
     row_steps = 5
-    depths = (HALF + ID_ROWS, HALF) if half == 0 else (CAP, HALF)
-    columns = [
-        pl.BlockSpec((WIDTH, 128), functools.partial(lambda col, i: (0, col), 2 * g + half))
-        for g in range(GROUPS)
-    ]
 
     def by_owner(i):
         return (0, jnp.maximum(i - rot_steps, 0), 0, 0)
 
-    if half == 0:
-        extra_spec = pl.BlockSpec((OWNERS, CAP), lambda i: (0, 0))
-    else:
-        extra_spec = pl.BlockSpec((GROUPS, step_owners, HALF, 128), by_owner)
-    kernel = first_route_kernel if half == 0 else second_route_kernel
     return pl.pallas_call(
-        functools.partial(kernel, rot_steps, row_steps, step_owners),
+        functools.partial(second_route_kernel, rot_steps, row_steps, step_owners),
         grid=(rot_steps + OWNERS // step_owners,),
         in_specs=[
             pl.BlockSpec(memory_space=pltpu.SMEM),
             pl.BlockSpec((1, ROWS), lambda i: (0, 0)),
-            extra_spec,
+            pl.BlockSpec((ROWS, GROUPS * 128), lambda i: (0, 0)),
             pl.BlockSpec((ROWS // rot_steps, WIDTH), lambda i: (jnp.minimum(i, rot_steps - 1), 0)),
-            *columns,
-        ],
-        out_specs=[pl.BlockSpec((GROUPS, step_owners, d, 128), by_owner) for d in depths],
-        out_shape=[jax.ShapeDtypeStruct((GROUPS, OWNERS, d, 128), BF) for d in depths],
+            *matrix_columns(1),
+        ],
+        out_specs=[pl.BlockSpec((GROUPS, step_owners, d, 128), by_owner) for d in (CAP, HALF)],
+        out_shape=[jax.ShapeDtypeStruct((GROUPS, OWNERS, d, 128), BF) for d in (CAP, HALF)],
         scratch_shapes=[
             pltpu.VMEM((ROWS, GROUPS * 128), BF),
-            pltpu.VMEM((ORDERED + CAP, GROUPS * 128), BF),
-        ],
-        compiler_params=params(56),
-        cost_estimate=cost(8e9, 10 * MIB),
-    )(start, place, extra, embeddings, matrix, matrix, matrix, matrix)
+            pltpu.VMEM((ORDERED + CAP, 2 * GROUPS * 128), BF),
+        ],
+        compiler_params=params(60),
+        cost_estimate=cost(13e9, 12 * MIB),
+    )(start, place, rot0, embeddings, matrix, matrix, matrix, matrix)
 
 
 def pick_kernel(step_sources, tail_ref, centroid_ref, target_ref, out_ref, lower_ref, upper_ref, count_ref, acc_ref):
@@ -215,7 +265,7 @@
     numbers = []
     hots = []
     for j in range(step_sources):
-        tail = tail_ref[j].astype(F32)
+        tail = tail_ref[j, HALF:, :].astype(F32)
         number = tail[0:1, :] * 128.0 + tail[1:2, :]
         numbers.append(number)
         column = jnp.broadcast_to(number, (128, CAP)).T.astype(I32).astype(I16)
@@ -266,7 +316,7 @@
         functools.partial(pick_kernel, step_sources),
         grid=(SOURCES // step_sources,),
         in_specs=[
-            pl.BlockSpec((step_sources, ID_ROWS, CAP), lambda i: (i, HALF // ID_ROWS, 0)),
+            pl.BlockSpec((step_sources, HALF + ID_ROWS, CAP), lambda i: (i, 0, 0)),
             pl.BlockSpec((LISTS, 256), lambda i: (0, 0)),
             pl.BlockSpec((16, slots), lambda i: (0, i)),
         ],
@@ -283,7 +333,7 @@
             jax.ShapeDtypeStruct((16, 16, 16), F32),
         ],
         scratch_shapes=[pltpu.VMEM((256, 256), F32)],
-        compiler_params=params(56),
+        compiler_params=params(60),
         cost_estimate=cost(20e9, 12 * MIB),
     )(rows0, centroids, targets)
 
@@ -311,7 +361,7 @@
         in_specs=[pl.BlockSpec((128, CODES), lambda i: (i, 0))],
         out_specs=pl.BlockSpec((8 * CODES, 256), lambda i: (i, 0)),
         out_shape=jax.ShapeDtypeStruct((16 * CODES, 256), BF),
-        compiler_params=params(56),
+        compiler_params=params(60),
         cost_estimate=cost(1e9, 3 * MIB),
     )(codebook.reshape(256, CODES))
 
@@ -405,7 +455,7 @@
             jax.ShapeDtypeStruct((8, 16, CODES), F32),
         ],
         scratch_shapes=[pltpu.VMEM((2, 256, 256), F32)],
-        compiler_params=params(56),
+        compiler_params=params(60),
         cost_estimate=cost(11e9, 5 * MIB),
     )(rows, picked, ids, targets, book)
 
@@ -433,7 +483,7 @@
 
 
 def last_sums(rows, picked, ids, targets, s00, s01, s10, counts):
-    step_sources = 32
+    step_sources = 64
     slots = step_sources * HALF
     whole = [pl.BlockSpec((8, 16, CODES), lambda i: (0, 0, 0))] * 3
     return pl.pallas_call(
@@ -447,7 +497,7 @@
         out_specs=pl.BlockSpec((OWNERS, 24, 128), lambda i: (0, 0, 0)),
         out_shape=jax.ShapeDtypeStruct((OWNERS, 24, 128), F32),
         scratch_shapes=[pltpu.VMEM((2, 256, 256), F32)],
-        compiler_params=params(56),
+        compiler_params=params(60),
         cost_estimate=cost(2e9, 5 * MIB),
     )(rows, picked, ids, targets, s00, s01, s10, counts)
 
@@ -471,7 +521,7 @@
 
 
 def last_errors(begin, end, rows, picked, ids, targets, book, e00, e01, e10, before):
-    step_sources = 16
+    step_sources = 32
     slots = step_sources * HALF
     block = [pl.BlockSpec((8, slots), lambda i: (0, i + begin))] * 3
     earlier = [] if before is None else [before]
@@ -486,27 +536,17 @@
         out_specs=pl.BlockSpec((16, 2 * slots), lambda i: (0, i + begin)),
         out_shape=jax.ShapeDtypeStruct((16, SLOTS), F32),
         input_output_aliases={} if before is None else {8: 0},
-        compiler_params=params(56),
-        cost_estimate=cost(1.1e9 * (end - begin), (end - begin) * MIB),
+        compiler_params=params(60),
+        cost_estimate=cost(2.2e9 * (end - begin), (end - begin) * 2 * MIB),
     )(rows, picked, ids, targets, book, e00, e01, e10, *earlier)
 
 
-def piece_kernel(got_ref, code_ref, out_ref):
-    total = jnp.sum(got_ref[...], axis=0)
-    codes = code_ref[...]
+def new_piece(got, codes):
+    total = jnp.sum(got, axis=0)
     low = (codes[:, :128] + total[:8]) / (1.0 + total[16:17])
     high = (codes[:, 128:] + total[8:16]) / (1.0 + total[17:18])
     piece = jnp.concatenate([low, high], axis=1)
-    out_ref[...] = jnp.broadcast_to(piece[None], (OWNERS, 8, CODES))
-
-
-def new_piece(got, codes):
-    return pl.pallas_call(
-        piece_kernel,
-        out_shape=jax.ShapeDtypeStruct((OWNERS, 8, CODES), F32),
-        compiler_params=pltpu.CompilerParams(vmem_limit_bytes=56 * MIB),
-        cost_estimate=cost(1e6, MIB),
-    )(got, codes)
+    return jnp.broadcast_to(piece[None], (OWNERS, 8, CODES))
 
 
 def exchange(x, axes):
@@ -517,10 +557,11 @@
     embeddings, owner_of_row, list_in_owner, opq_matrix, centroids, codebook, code_targets
 ):
     every = ("sub", "lists")
-    place, start, ids = rank_rows(owner_of_row.reshape(1, ROWS), list_in_owner.reshape(1, ROWS))
-    send_a, rest = route(0, start, place, ids, embeddings, opq_matrix)
+    owner = owner_of_row.reshape(1, ROWS)
+    lists = list_in_owner.reshape(1, ROWS)
+    send_a, rot0, place, start = first_route(owner, lists, embeddings, opq_matrix)
     rows_a = exchange(send_a.reshape(SOURCES, HALF + ID_ROWS, 128), every)
-    send_b, send_c = route(1, start, place, rest, embeddings, opq_matrix)
+    send_b, send_c = second_route(start, place, rot0, embeddings, opq_matrix)
     book = make_book(codebook)
     targets = code_targets.reshape(16, SOURCES, 2, HALF).transpose(2, 0, 1, 3)
     targets = targets.reshape(2, 16, HALF_SLOTS)
@@ -543,7 +584,7 @@
     piece, quant_error = lax.optimization_barrier((new_piece(got, codes), quant_error))
     spread = exchange(piece, "lists")
     quant_error = last_errors(
-        2, 8, rows_c, picked, upper, targets, book, e00, e01, e10, quant_error
+        2, 4, rows_c, picked, upper, targets, book, e00, e01, e10, quant_error
     )
     return quant_error, spread.reshape(16, 16, CODES)
 

time: 199 us -> 190 us (0.955)
  waiting for transfers between devices: 29.6 us -> 21.2 us
    all_to_all x5, waiting for transfers between devices: 29.6 us -> 21.2 us  [exchange(): return lax.all_to_all(x, axes, split_axis=0, concat_axis=0, tiled=True)]
    pallas_call x4 -> x2, Pallas kernels: 30.8 us -> 30.7 us  [the longest x1 19.4 us: second_route(): pl.pallas_call(functools.partial(second_route_kernel, rot_steps, row_step...]
  transfers between devices with their start and end apart: 5 -> 5, of which waited for: 4 -> 5; matrix products, arithmetic and copies ran while one was open for 5% -> 5% of each run, Pallas kernels for 51% -> 55%
where the time goes in v3:
time: 190 us
  Pallas kernels  122 us (64%)
  starting transfers between devices  34.5 us (18%)
  waiting for transfers between devices  21.2 us (11%)
  local copies, waits for them, and re-layouts  10.8 us (6%)
    pallas_call x3, Pallas kernels, quarter(): pl.pallas_call(functools.partial(quarter_kernel, slots), grid=(SOURCES //...  43.5 us
    all_to_all x5, starting transfers between devices, exchange(): return lax.all_to_all(x, axes, split_axis=0, concat_axis=0, tiled=True)  34.5 us
    pallas_call x1, Pallas kernels, pick(): pl.pallas_call(functools.partial(pick_kernel, step_sources), grid=(SOURCE...  24.4 us
    all_to_all x5, waiting for transfers between devices, exchange(): return lax.all_to_all(x, axes, split_axis=0, concat_axis=0, tiled=True)  21.2 us
    pallas_call x1, Pallas kernels, second_route(): pl.pallas_call(functools.partial(second_route_kernel, rot_steps, row_step...  19.4 us
    pallas_call x2, Pallas kernels, last_errors(): pl.pallas_call(functools.partial(last_errors_kernel, slots), grid=(end -...  14.8 us
    pallas_call x1, Pallas kernels, first_route(): pl.pallas_call(functools.partial(first_route_kernel, parts, step_owners),...  11.3 us
    pallas_call x1, Pallas kernels, last_sums(): pl.pallas_call(functools.partial(last_sums_kernel, slots), grid=(SOURCES...  5.23 us
  transfers between devices with their start and end apart: 5, of which 5 were waited for; matrix products, arithmetic and copies ran while one was open for 5% of the time, Pallas kernels for 55%

profile of v3, /device:TPU:1, one launch (start us, length us, event | category | flops | bytes accessed | tf_op | source)
XLA Modules:
  0.0 189.5 jit_solution(4239315706870020228)
XLA Ops:
  0.6 11.3 %shard_map.86 = (bf16[4,32,72,128]{3,2,1,0:T(8,128)(2,1)}, bf16[2048,512]{1,0:T(8,128)(2,1)}, s32[1,2048]{1,0:T(1,128)}, s32[32,128]{1,0:T(8,128)}) custom-call(s32[1,2048]{1,0:T(1,128)} %bitcast.25, s32[1,2048]{1,0:T(1,128)} %bitcast.26, bf16[2048,1024]{1,0:T(8,128)(2,1)} %rows_ref.1, bf16[1024,1024]{1,0:T(8,128)(2,1)} %r3.3, bf16[1024,1024]{1,0:T(8,128)(2,1)} %r3.3, ...), custom_call_target="tpu_custom_call" | custom-call | flops 8000000000 | bytes 10485760 | tf_op jit(solution)/shard_map/pallas_call | solution.py:149
  11.9 11.9 %all-to-all-start = ((bf16[128,72,128]{2,1,0:T(8,128)(2,1)}), bf16[128,72,128]{2,1,0:T(8,128)(2,1)}, u32[]{:S(2)}, u32[]{:S(2)}) async-start(bf16[128,72,128]{2,1,0:T(8,128)(2,1)} %bitcast.20), calls=%async_computation | async-start | bytes 4718592 | tf_op jit(solution)/shard_map/all_to_all | solution.py:553
  23.9 2.9 %reshape.45 = s32[16,128,2,64]{3,2,1,0:T(2,128)} reshape(s32[16,16384]{1,0:T(8,128)S(1)} %copy-done.1) | data formatting | bytes 2097152 | tf_op jit(solution)/shard_map/reshape | solution.py:566
  26.8 1.8 copy.11
  28.6 1.6 reshape.46.target_ref
  30.2 2.9 %shard_map.89.book_ref = bf16[4096,256]{1,0:T(8,128)(2,1)} custom-call(bf16[256,256]{1,0:T(8,128)(2,1)} %bitcast.23), custom_call_target="tpu_custom_call" | custom-call | flops 1000000000 | bytes 3145728 | tf_op jit(solution)/shard_map/pallas_call | solution.py:358
  33.8 19.4 %shard_map.87 = (bf16[4,32,128,128]{3,2,1,0:T(8,128)(2,1)}, bf16[4,32,64,128]{3,2,1,0:T(8,128)(2,1)}) custom-call(s32[32,128]{1,0:T(8,128)} %get-tuple-element.30.start_ref, s32[1,2048]{1,0:T(1,128)} %get-tuple-element.31.place_ref, bf16[2048,512]{1,0:T(8,128)(2,1)} %get-tuple-element.32.rot0_ref, bf16[2048,1024]{1,0:T(8,128)(2,1)} %rows_ref.1, ...), custom_call_target="tpu_custom_call" | custom-call | flops 12999999488 | bytes 12582912 | tf_op jit(solution)/shard_map/pallas_call | solution.py:233
  53.3 3.3 %all-to-all-done.tail_ref.rows_ref = bf16[128,72,128]{2,1,0:T(8,128)(2,1)} async-done(((bf16[128,72,128]{2,1,0:T(8,128)(2,1)}), bf16[128,72,128]{2,1,0:T(8,128)(2,1)}, u32[]{:S(2)}, u32[]{:S(2)}) %all-to-all-start) | async-done | bytes 2359328 | tf_op jit(solution)/shard_map/all_to_all | solution.py:553
  56.5 7.0 %all-to-all-start.2 = ((bf16[128,128,128]{2,1,0:T(8,128)(2,1)}), bf16[128,128,128]{2,1,0:T(8,128)(2,1)}, u32[]{:S(2)}, u32[]{:S(2)}) async-start(bf16[128,128,128]{2,1,0:T(8,128)(2,1)} %bitcast.19), calls=%async_computation.2 | async-start | bytes 8388608 | tf_op jit(solution)/shard_map/all_to_all | solution.py:553
  63.5 24.4 %shard_map.88 = (bf16[128,128,256]{2,1,0:T(8,128)(2,1)}, f32[1,8192]{1,0:T(1,128)}, f32[1,8192]{1,0:T(1,128)}, f32[16,16,16]{2,1,0:T(8,128)}) custom-call(bf16[128,72,128]{2,1,0:T(8,128)(2,1)} %all-to-all-done.tail_ref.rows_ref, bf16[2048,256]{1,0:T(8,128)(2,1)} %centroid_ref.1, s32[16,16384]{1,0:T(8,128)} %target_ref.1), custom_call_target="tpu_custom_call" | custom-call | flops 20000000000 | bytes 12582912 | tf_op jit(solution)/shard_map/pallas_call | solution.py:315
  87.9 1.6 reshape.49.count_ref
  89.5 14.5 %shard_map.90 = (f32[8,8192]{1,0:T(8,128)}, f32[8,16,256]{2,1,0:T(8,128)}) custom-call(bf16[128,72,128]{2,1,0:T(8,128)(2,1)} %all-to-all-done.tail_ref.rows_ref, bf16[128,128,256]{2,1,0:T(8,128)(2,1)} %get-tuple-element.35.pick_ref, f32[1,8192]{1,0:T(1,128)} %get-tuple-element.36.ids_ref, s32[2,16,8192]{2,1,0:T(8,128)} %reshape.46.target_ref, ...), custom_call_target="tpu_custom_call" | custom-call | flops 11000000512 | bytes 5242880 | tf_op jit(solution)/shard_map/pallas_call | solution.py:445
  104.0 12.1 %all-to-all-done.2.rows_ref = bf16[128,128,128]{2,1,0:T(8,128)(2,1)} async-done(((bf16[128,128,128]{2,1,0:T(8,128)(2,1)}), bf16[128,128,128]{2,1,0:T(8,128)(2,1)}, u32[]{:S(2)}, u32[]{:S(2)}) %all-to-all-start.2) | async-done | bytes 4194336 | tf_op jit(solution)/shard_map/all_to_all | solution.py:553
  116.1 4.5 %all-to-all-start.1 = ((bf16[128,64,128]{2,1,0:T(8,128)(2,1)}), bf16[128,64,128]{2,1,0:T(8,128)(2,1)S(1)}, u32[]{:S(2)}, u32[]{:S(2)}) async-start(bf16[128,64,128]{2,1,0:T(8,128)(2,1)} %bitcast.21), calls=%async_computation.1 | async-start | bytes 4194304 | tf_op jit(solution)/shard_map/all_to_all | solution.py:553
  120.6 14.5 %shard_map.92 = (f32[8,8192]{1,0:T(8,128)}, f32[8,16,256]{2,1,0:T(8,128)}) custom-call(bf16[128,128,128]{2,1,0:T(8,128)(2,1)} %all-to-all-done.2.rows_ref, bf16[128,128,256]{2,1,0:T(8,128)(2,1)} %get-tuple-element.35.pick_ref, f32[1,8192]{1,0:T(1,128)} %get-tuple-element.36.ids_ref, s32[2,16,8192]{2,1,0:T(8,128)} %reshape.46.target_ref, ...), custom_call_target="tpu_custom_call" | custom-call | flops 11000000512 | bytes 5242880 | tf_op jit(solution)/shard_map/pallas_call | solution.py:445
  135.2 14.5 %shard_map.91 = (f32[8,8192]{1,0:T(8,128)}, f32[8,16,256]{2,1,0:T(8,128)}) custom-call(bf16[128,128,128]{2,1,0:T(8,128)(2,1)} %all-to-all-done.2.rows_ref, bf16[128,128,256]{2,1,0:T(8,128)(2,1)} %get-tuple-element.35.pick_ref, f32[1,8192]{1,0:T(1,128)} %get-tuple-element.44.ids_ref, s32[2,16,8192]{2,1,0:T(8,128)} %reshape.46.target_ref, ...), custom_call_target="tpu_custom_call" | custom-call | flops 11000000512 | bytes 5242880 | tf_op jit(solution)/shard_map/pallas_call | solution.py:445
  151.0 1.4 copy-done
  152.4 5.2 %shard_map.93 = f32[32,24,128]{2,1,0:T(8,128)} custom-call(bf16[128,64,128]{2,1,0:T(8,128)(2,1)} %copy-done, bf16[128,128,256]{2,1,0:T(8,128)(2,1)} %get-tuple-element.35.pick_ref, f32[1,8192]{1,0:T(1,128)} %get-tuple-element.44.ids_ref, s32[2,16,8192]{2,1,0:T(8,128)} %reshape.46.target_ref, f32[8,16,256]{2,1,0:T(8,128)} %get-tuple-element.52.s00, ...), custom_call_target="tpu_custom_call" | custom-call | flops 2000000000 | bytes 5242880 | tf_op jit(solution)/shard_map/pallas_call | solution.py:489
  157.6 6.6 %all-to-all-start.3 = ((f32[32,24,128]{2,1,0:T(8,128)}), f32[32,24,128]{2,1,0:T(8,128)S(1)}, u32[]{:S(2)}, u32[]{:S(2)}) async-start(f32[32,24,128]{2,1,0:T(8,128)} %shard_map.93), calls=%async_computation.3 | async-start | bytes 786432 | tf_op jit(solution)/shard_map/all_to_all | solution.py:553
  164.2 7.4 %shard_map.94.rest_0_ = f32[16,16384]{1,0:T(8,128)} custom-call(bf16[128,64,128]{2,1,0:T(8,128)(2,1)} %copy-done, bf16[128,128,256]{2,1,0:T(8,128)(2,1)} %get-tuple-element.35.pick_ref, f32[1,8192]{1,0:T(1,128)} %get-tuple-element.44.ids_ref, s32[2,16,8192]{2,1,0:T(8,128)} %reshape.46.target_ref, bf16[4096,256]{1,0:T(8,128)(2,1)} %shard_map.89.book_ref, ...), custom_call_target="tpu_custom_call" | custom-call | flops 4400000000 | bytes 4194304 | tf_op jit(solution)/shard_map/pallas_call | solution.py:528
  171.6 2.9 %all-to-all-done.3 = f32[32,24,128]{2,1,0:T(8,128)S(1)} async-done(((f32[32,24,128]{2,1,0:T(8,128)}), f32[32,24,128]{2,1,0:T(8,128)S(1)}, u32[]{:S(2)}, u32[]{:S(2)}) %all-to-all-start.3) | async-done | bytes 393248 | tf_op jit(solution)/shard_map/all_to_all | solution.py:553
  175.3 4.5 %all-to-all-start.4 = ((f32[32,8,256]{2,1,0:T(8,128)}), f32[32,8,256]{2,1,0:T(8,128)S(1)}, u32[]{:S(2)}, u32[]{:S(2)}) async-start(f32[32,8,256]{2,1,0:T(8,128)} %broadcast_in_dim.2), calls=%async_computation.4 | async-start | bytes 524288 | tf_op jit(solution)/shard_map/all_to_all | solution.py:553
  179.8 7.4 %shard_map.95 = f32[16,16384]{1,0:T(8,128)} custom-call(bf16[128,64,128]{2,1,0:T(8,128)(2,1)} %copy-done, bf16[128,128,256]{2,1,0:T(8,128)(2,1)} %get-tuple-element.35.pick_ref, f32[1,8192]{1,0:T(1,128)} %get-tuple-element.44.ids_ref, s32[2,16,8192]{2,1,0:T(8,128)} %reshape.46.target_ref, ...), custom_call_target="tpu_custom_call", output_to_operand_aliasing={{}: (8, {})} | custom-call | flops 4400000000 | bytes 4194304 | tf_op jit(solution)/shard_map/pallas_call | solution.py:528
  187.2 1.6 all-to-all-done.4
  (11 shorter events, 3.5 us)
Async XLA Ops:
  11.9 11.9 %copy-start.1 = (s32[16,16384]{1,0:T(8,128)S(1)}, s32[16,16384]{1,0:T(8,128)}, u32[]{:S(2)}) copy-start(s32[16,16384]{1,0:T(8,128)} %target_ref.1) | copy-start | bytes 3145732
  11.9 44.6 %all-to-all-start = ((bf16[128,72,128]{2,1,0:T(8,128)(2,1)}), bf16[128,72,128]{2,1,0:T(8,128)(2,1)}, u32[]{:S(2)}, u32[]{:S(2)}) async-start(bf16[128,72,128]{2,1,0:T(8,128)(2,1)} %bitcast.20), calls=%async_computation | async-start | bytes 4718592 | tf_op jit(solution)/shard_map/all_to_all | solution.py:553
  56.5 59.6 %all-to-all-start.2 = ((bf16[128,128,128]{2,1,0:T(8,128)(2,1)}), bf16[128,128,128]{2,1,0:T(8,128)(2,1)}, u32[]{:S(2)}, u32[]{:S(2)}) async-start(bf16[128,128,128]{2,1,0:T(8,128)(2,1)} %bitcast.19), calls=%async_computation.2 | async-start | bytes 8388608 | tf_op jit(solution)/shard_map/all_to_all | solution.py:553
  116.1 34.9 %all-to-all-start.1 = ((bf16[128,64,128]{2,1,0:T(8,128)(2,1)}), bf16[128,64,128]{2,1,0:T(8,128)(2,1)S(1)}, u32[]{:S(2)}, u32[]{:S(2)}) async-start(bf16[128,64,128]{2,1,0:T(8,128)(2,1)} %bitcast.21), calls=%async_computation.1 | async-start | bytes 4194304 | tf_op jit(solution)/shard_map/all_to_all | solution.py:553
  151.0 1.4 copy-start
  157.6 16.9 %all-to-all-start.3 = ((f32[32,24,128]{2,1,0:T(8,128)}), f32[32,24,128]{2,1,0:T(8,128)S(1)}, u32[]{:S(2)}, u32[]{:S(2)}) async-start(f32[32,24,128]{2,1,0:T(8,128)} %shard_map.93), calls=%async_computation.3 | async-start | bytes 786432 | tf_op jit(solution)/shard_map/all_to_all | solution.py:553
  175.3 13.5 %all-to-all-start.4 = ((f32[32,8,256]{2,1,0:T(8,128)}), f32[32,8,256]{2,1,0:T(8,128)S(1)}, u32[]{:S(2)}, u32[]{:S(2)}) async-start(f32[32,8,256]{2,1,0:T(8,128)} %broadcast_in_dim.2), calls=%async_computation.4 | async-start | bytes 524288 | tf_op jit(solution)/shard_map/all_to_all | solution.py:553

commit v4 on v3

v4 whole, which is shorter than its diff:
```python
import functools

import jax
import jax.numpy as jnp
from jax import lax
from jax.experimental import pallas as pl
from jax.experimental.pallas import tpu as pltpu
from jax.sharding import PartitionSpec as P

BF = jnp.bfloat16
F32 = jnp.float32
I32 = jnp.int32
I16 = jnp.int16
OWNERS = 32
GROUPS = 4
CAP = 128
ROWS = 2048
WIDTH = 1024
SOURCES = OWNERS * GROUPS
SLOTS = SOURCES * CAP
LISTS = 2048
CODES = 256
MIB = 2**20


def nn(a, b):
    return jnp.dot(a, b, preferred_element_type=F32)


def nt(a, b):
    return lax.dot_general(a, b, (((1,), (1,)), ((), ())), preferred_element_type=F32)


def params(mib):
    return pltpu.CompilerParams(
        vmem_limit_bytes=mib * MIB, dimension_semantics=("arbitrary",)
    )


def cost(flops, bytes_accessed):
    return pl.CostEstimate(
        flops=int(flops), bytes_accessed=int(bytes_accessed), transcendentals=0
    )


ORDERED = ROWS + 16 * OWNERS
ID_ROWS = 8


def rank_rows(owner, lists):
    owner_hot = (owner == lax.broadcasted_iota(I32, (OWNERS, ROWS), 0)).astype(F32)
    before = (
        lax.broadcasted_iota(I32, (128, 128), 0) < lax.broadcasted_iota(I32, (128, 128), 1)
    ).astype(F32)
    blocks = ROWS // 128
    stacked = jnp.concatenate(
        [owner_hot[:, b * 128 : (b + 1) * 128] for b in range(blocks)], axis=0
    ).astype(BF)
    inside = nn(stacked, before.astype(BF))
    ranks = []
    carry = jnp.zeros((OWNERS, 1), F32)
    for b in range(blocks):
        hot = owner_hot[:, b * 128 : (b + 1) * 128]
        earlier = inside[b * OWNERS : (b + 1) * OWNERS] + carry
        ranks.append(jnp.sum(hot * earlier, axis=0, keepdims=True))
        carry = carry + jnp.sum(hot, axis=1, keepdims=True)
    rank = jnp.concatenate(ranks, axis=1)
    pages = ((carry.astype(I32) + 15) // 16).astype(F32).astype(BF)
    after = before[:OWNERS, :OWNERS].T.astype(BF)
    first = nn(after, jnp.broadcast_to(pages, (OWNERS, 128)))
    begin = jnp.sum(owner_hot * first[:, :1], axis=0, keepdims=True) * 16.0
    place = (begin + rank).astype(I32)
    rank = rank.astype(I32)
    rank_hot = (rank == lax.broadcasted_iota(I32, (CAP, ROWS), 0)).astype(F32).astype(BF)
    high = (lists // 128).astype(F32)
    low = (lists % 128).astype(F32)
    left = jnp.concatenate([owner_hot * high, owner_hot * low, owner_hot], axis=0).astype(BF)
    found = nt(left, rank_hot)
    number = found[:OWNERS] * 128.0 + found[OWNERS : 2 * OWNERS]
    ids = (number + found[2 * OWNERS :] - 1.0).astype(I32)
    return place, first.astype(I32), ids


def matrix_columns(half):
    return [
        pl.BlockSpec((WIDTH, 128), functools.partial(lambda col, i: (0, col), 2 * g + half))
        for g in range(GROUPS)
    ]


def order_rows(place, rot_ref, run_ref, row_steps):
    run_rows = ORDERED // row_steps
    one = jnp.ones((), BF)
    zero = jnp.zeros((), BF)
    digit = lax.broadcasted_iota(I32, (run_rows, ROWS), 0).astype(I16)
    for k in range(row_steps):
        hot = jnp.where((place - k * run_rows).astype(I16) == digit, one, zero)
        run_ref[k * run_rows : (k + 1) * run_rows, :] = nn(hot, rot_ref[...]).astype(BF)
    run_ref[ORDERED:, :] = jnp.zeros((CAP, GROUPS * 128), BF)


def route_kernel(half, parts, row_steps, step_owners, *refs):
    if half == 0:
        owner_ref, list_ref, rows_hbm, r0, r1, r2, r3, out_ref, place_ref, first_ref = refs[:10]
        start_ref, ids_ref, rows_ref, rot_ref, run_ref, in_sem, start_sem = refs[10:]
    else:
        start_ref, place_ref, rows_hbm, r0, r1, r2, r3, out_ref = refs[:8]
        rows_ref, rot_ref, run_ref, in_sem = refs[8:]
    step = pl.program_id(0)
    part_rows = ROWS // parts

    @pl.when(step == 0)
    def _():
        copies = []
        for k in range(parts):
            part = pl.ds(k * part_rows, part_rows)
            copies.append(
                pltpu.make_async_copy(rows_hbm.at[part], rows_ref.at[part], in_sem.at[k])
            )
            copies[k].start()
        if half == 0:
            place, first, ids = rank_rows(owner_ref[...], list_ref[...])
            place_ref[...] = place
            first_ref[...] = first
            ids_ref[...] = ids
            starts = pltpu.make_async_copy(first_ref, start_ref, start_sem)
            starts.start()
        matrix = jnp.concatenate([r[...] for r in (r0, r1, r2, r3)], axis=1)
        for k in range(parts):
            part = pl.ds(k * part_rows, part_rows)
            copies[k].wait()
            rot_ref[part, :] = nn(rows_ref[part, :], matrix).astype(BF)
        order_rows(place_ref[...], rot_ref, run_ref, row_steps)
        if half == 0:
            starts.wait()

    line = lax.broadcasted_iota(I32, (ID_ROWS, CAP), 0)
    for j in range(step_owners):
        owner = step * step_owners + j
        begin = pl.multiple_of(start_ref[owner, 0] * 16, 16)
        run = run_ref[pl.ds(begin, CAP), :]
        for g in range(GROUPS):
            out_ref[g, j, :CAP, :] = run[:, g * 128 : (g + 1) * 128]
        if half == 0:
            ids = ids_ref[pl.ds(owner, 1), :]
            high = jnp.where(ids < 0, -1, ids // 128)
            low = ids % 128
            tail = jnp.where(line == 0, high, jnp.where(line == 1, low, 0))
            tail = tail.astype(F32).astype(BF)
            for g in range(GROUPS):
                out_ref[g, j, CAP:, :] = tail


def route(half, first_arg, second_arg, embeddings, matrix):
    step_owners = 8
    parts = 4
    row_steps = 5
    depth = CAP + (ID_ROWS if half == 0 else 0)
    line = pl.BlockSpec((1, ROWS), lambda i: (0, 0))
    out_specs = [pl.BlockSpec((GROUPS, step_owners, depth, 128), lambda i: (0, i, 0, 0))]
    out_shape = [jax.ShapeDtypeStruct((GROUPS, OWNERS, depth, 128), BF)]
    scratch = [
        pltpu.VMEM((ROWS, WIDTH), BF),
        pltpu.VMEM((ROWS, GROUPS * 128), BF),
        pltpu.VMEM((ORDERED + CAP, GROUPS * 128), BF),
        pltpu.SemaphoreType.DMA((parts,)),
    ]
    if half == 0:
        inputs = [line, line]
        out_specs += [line, pl.BlockSpec((OWNERS, 128), lambda i: (0, 0))]
        out_shape += [
            jax.ShapeDtypeStruct((1, ROWS), I32),
            jax.ShapeDtypeStruct((OWNERS, 128), I32),
        ]
        scratch = [
            pltpu.SMEM((OWNERS, 128), I32),
            pltpu.VMEM((OWNERS, CAP), I32),
            *scratch,
            pltpu.SemaphoreType.DMA,
        ]
    else:
        inputs = [pl.BlockSpec(memory_space=pltpu.SMEM), line]
    return pl.pallas_call(
        functools.partial(route_kernel, half, parts, row_steps, step_owners),
        grid=(OWNERS // step_owners,),
        in_specs=[*inputs, pl.BlockSpec(memory_space=pl.ANY), *matrix_columns(half)],
        out_specs=out_specs,
        out_shape=out_shape,
        scratch_shapes=scratch,
        compiler_params=params(60),
        cost_estimate=cost(8e9, 10 * MIB),
    )(first_arg, second_arg, embeddings, matrix, matrix, matrix, matrix)


def pick_kernel(step_sources, tail_ref, centroid_ref, out_ref, ids_ref):
    one = jnp.ones((), BF)
    zero = jnp.zeros((), BF)
    lane = lax.broadcasted_iota(I32, (CAP, 128), 1).astype(I16)
    numbers = []
    hots = []
    for j in range(step_sources):
        tail = tail_ref[j, CAP:, :].astype(F32)
        number = tail[0:1, :] * 128.0 + tail[1:2, :]
        numbers.append(number)
        column = jnp.broadcast_to(number, (128, CAP)).T.astype(I32).astype(I16)
        hots.append(
            jnp.concatenate(
                [
                    jnp.where(column == lane + jnp.int16(128 * b), one, zero)
                    for b in range(LISTS // 128)
                ],
                axis=1,
            )
        )
    found = nn(jnp.concatenate(hots, axis=0), centroid_ref[...]).astype(BF)
    out_ref[...] = found.reshape(step_sources, CAP, 256)
    ids_ref[...] = jnp.concatenate(numbers, axis=1)


def pick(rows0, centroids):
    step_sources = 16
    slots = step_sources * CAP
    return pl.pallas_call(
        functools.partial(pick_kernel, step_sources),
        grid=(SOURCES // step_sources,),
        in_specs=[
            pl.BlockSpec((step_sources, CAP + ID_ROWS, CAP), lambda i: (i, 0, 0)),
            pl.BlockSpec((LISTS, 256), lambda i: (0, 0)),
        ],
        out_specs=[
            pl.BlockSpec((step_sources, CAP, 256), lambda i: (i, 0, 0)),
            pl.BlockSpec((1, slots), lambda i: (0, i)),
        ],
        out_shape=[
            jax.ShapeDtypeStruct((SOURCES, CAP, 256), BF),
            jax.ShapeDtypeStruct((1, SLOTS), F32),
        ],
        compiler_params=params(60),
        cost_estimate=cost(18e9, 14 * MIB),
    )(rows0, centroids)


def book_kernel(code_ref, out_ref):
    codes = code_ref[...].astype(F32).T
    lane = lax.broadcasted_iota(I32, (CODES, 128), 1)
    for m in range(8):
        mine = jnp.where(lane // 16 == m, codes, 0.0)
        square = jnp.sum(mine * mine, axis=1, keepdims=True)
        high = square.astype(BF).astype(F32)
        middle = (square - high).astype(BF).astype(F32)
        low = square - high - middle
        tail = jnp.where(
            lane == 0, high, jnp.where(lane == 1, middle, jnp.where(lane == 2, low, 0.0))
        )
        out_ref[m * CODES : (m + 1) * CODES, :128] = (-2.0 * mine).astype(BF)
        out_ref[m * CODES : (m + 1) * CODES, 128:] = tail.astype(BF)


def make_book(codebook):
    return pl.pallas_call(
        book_kernel,
        grid=(2,),
        in_specs=[pl.BlockSpec((128, CODES), lambda i: (i, 0))],
        out_specs=pl.BlockSpec((8 * CODES, 256), lambda i: (i, 0)),
        out_shape=jax.ShapeDtypeStruct((16 * CODES, 256), BF),
        compiler_params=params(60),
        cost_estimate=cost(1e9, 3 * MIB),
    )(codebook.reshape(256, CODES))


def residual(rows_ref, pick_ref, slots):
    rows = rows_ref[...].reshape(slots, 128).astype(F32)
    centre = pick_ref[...].reshape(slots, 128).astype(F32)
    return (rows - centre).astype(BF)


def add_sums(slots, flipped, live, target, acc_ref):
    high = jnp.where(live, target // 64, -1).astype(I16)
    low = (target % 64).astype(I16)
    digit = lax.broadcasted_iota(I32, (64, slots), 0).astype(I16)
    line = lax.broadcasted_iota(I32, (16, slots), 0)
    nth = (line // 4).astype(I16)
    quarter = (line % 4).astype(I16)
    one = jnp.ones((), BF)
    zero = jnp.zeros((), BF)
    for t in range(2):
        left = []
        right = []
        mixed = jnp.zeros((16, slots), I16)
        for m in range(4 * t, 4 * t + 4):
            mine = flipped[m * 16 : (m + 1) * 16]
            row = jnp.broadcast_to(high[m : m + 1], (16, slots))
            mixed = jnp.where(nth == jnp.int16(m % 4), row, mixed)
            for h in range(4):
                left.append(jnp.where(row == jnp.int16(h), mine, zero))
            right.append(jnp.where(low[m : m + 1] == digit, one, zero))
        left.append(jnp.where(mixed == quarter, one, zero))
        acc_ref[t] += nt(jnp.concatenate(left, axis=0), jnp.concatenate(right, axis=0))


def sum_of(acc_ref, m):
    base = (m % 4) * 64
    part = acc_ref[m // 4][:, base : base + 64]
    return jnp.concatenate([part[base + h * 16 : base + (h + 1) * 16] for h in range(4)], axis=1)


def count_of(acc_ref, m):
    base = (m % 4) * 64
    part = acc_ref[m // 4][256:, base : base + 64]
    at = (m % 4) * 4
    return jnp.concatenate([part[at + h : at + h + 1] for h in range(4)], axis=1)


def least_errors(slots, resid, flipped, live, book_ref):
    wide = jnp.concatenate([resid, jnp.ones((slots, 128), BF)], axis=1)
    lines = []
    for m in range(8):
        mine = flipped[m * 16 : (m + 1) * 16]
        row_sq = jnp.sum(mine * mine, axis=0, keepdims=True)
        dist = nt(book_ref[m * CODES : (m + 1) * CODES], wide)
        least = jnp.min(dist, axis=0, keepdims=True)
        lines.append(jnp.where(live, row_sq + least, 0.0))
    return lines


def half_specs(step_sources, half, begin=0):
    slots = step_sources * CAP
    return [
        pl.BlockSpec((step_sources, CAP, 128), lambda i: (i + begin, 0, 0)),
        pl.BlockSpec((step_sources, CAP, 128), lambda i: (i + begin, 0, half)),
        pl.BlockSpec((1, slots), lambda i: (0, i + begin)),
        pl.BlockSpec((8, slots), lambda i: (half, i + begin)),
        pl.BlockSpec((8 * CODES, 256), lambda i: (half, 0)),
    ]


def first_half_kernel(slots, rows_ref, pick_ref, ids_ref, target_ref, book_ref,
                      error_ref, sum_ref, count_ref, acc_ref):
    step = pl.program_id(0)

    @pl.when(step == 0)
    def _():
        acc_ref[...] = jnp.zeros_like(acc_ref)

    resid = residual(rows_ref, pick_ref, slots)
    flipped = resid.astype(F32).T
    live = ids_ref[...] >= 0
    add_sums(slots, flipped.astype(BF), live, target_ref[...], acc_ref)
    for m, line in enumerate(least_errors(slots, resid, flipped, live, book_ref)):
        error_ref[m : m + 1, :] = line

    @pl.when(step == pl.num_programs(0) - 1)
    def _():
        for m in range(8):
            sum_ref[m] = sum_of(acc_ref, m)
            count_ref[m : m + 1, :] = count_of(acc_ref, m)


def first_half(rows, picked, ids, targets, book):
    step_sources = 32
    slots = step_sources * CAP
    return pl.pallas_call(
        functools.partial(first_half_kernel, slots),
        grid=(SOURCES // step_sources,),
        in_specs=half_specs(step_sources, 0),
        out_specs=[
            pl.BlockSpec((8, slots), lambda i: (0, i)),
            pl.BlockSpec((8, 16, CODES), lambda i: (0, 0, 0)),
            pl.BlockSpec((8, CODES), lambda i: (0, 0)),
        ],
        out_shape=[
            jax.ShapeDtypeStruct((16, SLOTS), F32),
            jax.ShapeDtypeStruct((8, 16, CODES), F32),
            jax.ShapeDtypeStruct((8, CODES), F32),
        ],
        scratch_shapes=[pltpu.VMEM((2, 272, 256), F32)],
        compiler_params=params(60),
        cost_estimate=cost(22e9, 10 * MIB),
    )(rows, picked, ids, targets, book)


def last_sums_kernel(slots, rows_ref, pick_ref, ids_ref, target_ref, sum_ref, count_ref, out_ref, acc_ref):
    step = pl.program_id(0)

    @pl.when(step == 0)
    def _():
        acc_ref[...] = jnp.zeros_like(acc_ref)
        out_ref[:, 16:, :] = jnp.zeros((OWNERS, 8, 128), F32)

    resid = residual(rows_ref, pick_ref, slots)
    flipped = resid.astype(F32).T.astype(BF)
    add_sums(slots, flipped, ids_ref[...] >= 0, target_ref[...], acc_ref)

    @pl.when(step == pl.num_programs(0) - 1)
    def _():
        for m in range(16):
            total = sum_ref[m] if m < 8 else sum_of(acc_ref, m - 8)
            count = count_ref[m : m + 1, :] if m < 8 else count_of(acc_ref, m - 8)
            for h in range(2):
                out_ref[2 * m + h, :8, :] = total[8 * h : 8 * h + 8, :128]
                out_ref[2 * m + h, 8:16, :] = total[8 * h : 8 * h + 8, 128:]
                out_ref[2 * m + h, 16:17, :] = count[:, :128]
                out_ref[2 * m + h, 17:18, :] = count[:, 128:]


def last_sums(rows, picked, ids, targets, sums, counts):
    step_sources = 32
    slots = step_sources * CAP
    return pl.pallas_call(
        functools.partial(last_sums_kernel, slots),
        grid=(SOURCES // step_sources,),
        in_specs=[
            *half_specs(step_sources, 1)[:4],
            pl.BlockSpec((8, 16, CODES), lambda i: (0, 0, 0)),
            pl.BlockSpec((8, CODES), lambda i: (0, 0)),
        ],
        out_specs=pl.BlockSpec((OWNERS, 24, 128), lambda i: (0, 0, 0)),
        out_shape=jax.ShapeDtypeStruct((OWNERS, 24, 128), F32),
        scratch_shapes=[pltpu.VMEM((2, 272, 256), F32)],
        compiler_params=params(60),
        cost_estimate=cost(4e9, 9 * MIB),
    )(rows, picked, ids, targets, sums, counts)


def last_errors_kernel(slots, rows_ref, pick_ref, ids_ref, book_ref, before_ref, out_ref):
    del before_ref
    resid = residual(rows_ref, pick_ref, slots)
    flipped = resid.astype(F32).T
    for m, line in enumerate(least_errors(slots, resid, flipped, ids_ref[...] >= 0, book_ref)):
        out_ref[m : m + 1, :] = line


def last_errors(begin, end, rows, picked, ids, book, before):
    step_sources = 32
    slots = step_sources * CAP
    specs = half_specs(step_sources, 1, begin)
    return pl.pallas_call(
        functools.partial(last_errors_kernel, slots),
        grid=(end - begin,),
        in_specs=[*specs[:3], specs[4], pl.BlockSpec(memory_space=pl.ANY)],
        out_specs=pl.BlockSpec((8, slots), lambda i: (1, i + begin)),
        out_shape=jax.ShapeDtypeStruct((16, SLOTS), F32),
        input_output_aliases={4: 0},
        compiler_params=params(60),
        cost_estimate=cost(4.4e9 * (end - begin), (end - begin) * 3 * MIB),
    )(rows, picked, ids, book, before)


def new_piece(got, codes):
    total = jnp.sum(got, axis=0)
    low = (codes[:, :128] + total[:8]) / (1.0 + total[16:17])
    high = (codes[:, 128:] + total[8:16]) / (1.0 + total[17:18])
    piece = jnp.concatenate([low, high], axis=1)
    return jnp.broadcast_to(piece[None], (OWNERS, 8, CODES))


def exchange(x, axes):
    return lax.all_to_all(x, axes, split_axis=0, concat_axis=0, tiled=True)


def per_device(
    embeddings, owner_of_row, list_in_owner, opq_matrix, centroids, codebook, code_targets
):
    every = ("sub", "lists")
    owner = owner_of_row.reshape(1, ROWS)
    lists = list_in_owner.reshape(1, ROWS)
    send0, place, start = route(0, owner, lists, embeddings, opq_matrix)
    rows0 = exchange(send0.reshape(SOURCES, CAP + ID_ROWS, 128), every)
    (send1,) = route(1, start, place, embeddings, opq_matrix)
    book = make_book(codebook)
    me = lax.axis_index("lists")
    codes = codebook.astype(F32).reshape(OWNERS, 8, CODES)
    codes = lax.dynamic_slice(codes, (me, 0, 0), (1, 8, CODES))[0]
    send1, book, codes = lax.optimization_barrier((send1, book, codes))
    rows1 = exchange(send1.reshape(SOURCES, CAP, 128), every)
    picked, ids = pick(rows0, centroids)
    quant_error, sums, counts = first_half(rows0, picked, ids, code_targets, book)
    rows1, quant_error, sums = lax.optimization_barrier((rows1, quant_error, sums))
    pieces = last_sums(rows1, picked, ids, code_targets, sums, counts)
    quant_error = last_errors(0, 2, rows1, picked, ids, book, quant_error)
    got = exchange(pieces, "lists")
    piece, quant_error = lax.optimization_barrier((new_piece(got, codes), quant_error))
    spread = exchange(piece, "lists")
    quant_error = last_errors(2, 4, rows1, picked, ids, book, quant_error)
    return quant_error, spread.reshape(16, 16, CODES)


def solution(mesh):
    placed = (
        P(("lists", "sub"), None),
        P(("lists", "sub"), None),
        P(("lists", "sub")),
        P(),
        P("lists", "sub"),
        P("sub", None, None),
        P("sub", "lists"),
    )
    return jax.shard_map(
        per_device,
        mesh=mesh,
        in_specs=placed,
        out_specs=(P("sub", "lists"), P("sub", None, None)),
        check_vma=False,
    )
```

time: 190 us -> 188 us (0.989)
  waiting for transfers between devices: 21.2 us -> 43.3 us
  Pallas kernels: 122 us -> 112 us
  local copies, waits for them, and re-layouts: 10.8 us -> 1.42 us
  starting transfers between devices: 34.5 us -> 29.6 us
    all_to_all x5 -> x4, waiting for transfers between devices: 21.2 us -> 43.3 us  [exchange(): return lax.all_to_all(x, axes, split_axis=0, concat_axis=0, tiled=True)]
    pallas_call x5 -> x3, Pallas kernels: 74.2 us -> 53.2 us  [the longest x2 27 us: route(): pl.pallas_call(functools.partial(route_kernel, half, parts, row_steps, st...]
    pallas_call x2, Pallas kernels: 14.8 us -> 25.1 us  [last_errors(): pl.pallas_call(functools.partial(last_errors_kernel, slots), grid=(end -...]
    reshape x3 -> x0, local copies, waits for them, and re-layouts: 6.13 us -> none  [the longest x1 2.91 us: per_device(): targets = code_targets.reshape(16, SOURCES, 2, HALF).transpose(2, 0, 1, 3)]
    all_to_all x5 -> x4, starting transfers between devices: 34.5 us -> 29.6 us  [exchange(): return lax.all_to_all(x, axes, split_axis=0, concat_axis=0, tiled=True)]
    pallas_call x1, Pallas kernels: 5.23 us -> 8.58 us  [last_sums(): pl.pallas_call(functools.partial(last_sums_kernel, slots), grid=(SOURCES...]
    pallas_call x1, Pallas kernels: 24.4 us -> 21.8 us  [pick(): pl.pallas_call(functools.partial(pick_kernel, step_sources), grid=(SOURCE...]
  transfers between devices with their start and end apart: 5 -> 4, of which waited for: 5 -> 2; matrix products, arithmetic and copies ran while one was open for 5% -> 0% of each run, Pallas kernels for 55% -> 48%
where the time goes in v4:
time: 188 us; the launch traced here: 187 us
  Pallas kernels  112 us (60%)
  waiting for transfers between devices  43.3 us (23%)
  starting transfers between devices  29.6 us (16%)
    all_to_all x4, waiting for transfers between devices, exchange(): return lax.all_to_all(x, axes, split_axis=0, concat_axis=0, tiled=True)  43.3 us
    all_to_all x4, starting transfers between devices, exchange(): return lax.all_to_all(x, axes, split_axis=0, concat_axis=0, tiled=True)  29.6 us
    pallas_call x2, Pallas kernels, route(): pl.pallas_call(functools.partial(route_kernel, half, parts, row_steps, st...  27 us
    pallas_call x1, Pallas kernels, first_half(): pl.pallas_call(functools.partial(first_half_kernel, slots), grid=(SOURCES...  26.2 us
    pallas_call x2, Pallas kernels, last_errors(): pl.pallas_call(functools.partial(last_errors_kernel, slots), grid=(end -...  25.1 us
    pallas_call x1, Pallas kernels, pick(): pl.pallas_call(functools.partial(pick_kernel, step_sources), grid=(SOURCE...  21.8 us
    pallas_call x1, Pallas kernels, last_sums(): pl.pallas_call(functools.partial(last_sums_kernel, slots), grid=(SOURCES...  8.58 us
  transfers between devices with their start and end apart: 4, of which 2 were waited for; matrix products, arithmetic and copies ran while one was open for 0% of the time, Pallas kernels for 48%

profile of v4, /device:TPU:1, one launch (start us, length us, event | category | flops | bytes accessed | tf_op | source)
XLA Modules:
  0.0 187.4 jit_solution(12040765846210246707)
XLA Ops:
  0.6 13.7 %shard_map.86 = (bf16[4,32,136,128]{3,2,1,0:T(8,128)(2,1)}, s32[1,2048]{1,0:T(1,128)}, s32[32,128]{1,0:T(8,128)}) custom-call(s32[1,2048]{1,0:T(1,128)} %bitcast.19, s32[1,2048]{1,0:T(1,128)} %bitcast.20, bf16[2048,1024]{1,0:T(8,128)(2,1)} %refs_2_.3, bf16[1024,1024]{1,0:T(8,128)(2,1)} %refs_6_.3, bf16[1024,1024]{1,0:T(8,128)(2,1)} %refs_6_.3, ...), custom_call_target="tpu_custom_call" | custom-call | flops 8000000000 | bytes 10485760 | tf_op jit(solution)/shard_map/pallas_call | solution.py:183
  14.3 11.9 %all-to-all-start.1 = ((bf16[128,136,128]{2,1,0:T(8,128)(2,1)}), bf16[128,136,128]{2,1,0:T(8,128)(2,1)}, u32[]{:S(2)}, u32[]{:S(2)}) async-start(bf16[128,136,128]{2,1,0:T(8,128)(2,1)} %bitcast.14), calls=%async_computation.1 | async-start | bytes 8912896 | tf_op jit(solution)/shard_map/all_to_all | solution.py:458
  26.2 2.9 %shard_map.88.book_ref = bf16[4096,256]{1,0:T(8,128)(2,1)} custom-call(bf16[256,256]{1,0:T(8,128)(2,1)} %bitcast.17), custom_call_target="tpu_custom_call" | custom-call | flops 1000000000 | bytes 3145728 | tf_op jit(solution)/shard_map/pallas_call | solution.py:260
  29.1 0.7 convert_bitcast_fusion
  29.8 13.3 %shard_map.87 = bf16[4,32,128,128]{3,2,1,0:T(8,128)(2,1)} custom-call(s32[32,128]{1,0:T(8,128)} %get-tuple-element.18.refs_0_, s32[1,2048]{1,0:T(1,128)} %get-tuple-element.19.refs_1_, bf16[2048,1024]{1,0:T(8,128)(2,1)} %refs_2_.3, bf16[1024,1024]{1,0:T(8,128)(2,1)} %refs_6_.3, bf16[1024,1024]{1,0:T(8,128)(2,1)} %refs_6_.3, bf16[1024,1024]{1,0:T(8,128)(2,1)} %refs_6_.3, ...), custom_call_target="tpu_custom_call" | custom-call | flops 8000000000 | bytes 10485760 | tf_op jit(solution)/shard_map/pallas_call | solution.py:183
  43.2 38.5 %all-to-all-done.1.tail_ref.rows_ref = bf16[128,136,128]{2,1,0:T(8,128)(2,1)} async-done(((bf16[128,136,128]{2,1,0:T(8,128)(2,1)}), bf16[128,136,128]{2,1,0:T(8,128)(2,1)}, u32[]{:S(2)}, u32[]{:S(2)}) %all-to-all-start.1) | async-done | bytes 4456480 | tf_op jit(solution)/shard_map/all_to_all | solution.py:458
  81.7 5.6 %all-to-all-start = ((bf16[128,128,128]{2,1,0:T(8,128)(2,1)}), bf16[128,128,128]{2,1,0:T(8,128)(2,1)}, u32[]{:S(2)}, u32[]{:S(2)}) async-start(bf16[128,128,128]{2,1,0:T(8,128)(2,1)} %bitcast.15), calls=%async_computation | async-start | bytes 8388608 | tf_op jit(solution)/shard_map/all_to_all | solution.py:458
  87.3 21.8 %shard_map.89 = (bf16[128,128,256]{2,1,0:T(8,128)(2,1)}, f32[1,16384]{1,0:T(1,128)}) custom-call(bf16[128,136,128]{2,1,0:T(8,128)(2,1)} %all-to-all-done.1.tail_ref.rows_ref, bf16[2048,256]{1,0:T(8,128)(2,1)} %centroid_ref.1), custom_call_target="tpu_custom_call" | custom-call | flops 17999998976 | bytes 14680064 | tf_op jit(solution)/shard_map/pallas_call | solution.py:223
  109.1 26.2 %shard_map.90 = (f32[16,16384]{1,0:T(8,128)}, f32[8,16,256]{2,1,0:T(8,128)}, f32[8,256]{1,0:T(8,128)}) custom-call(bf16[128,136,128]{2,1,0:T(8,128)(2,1)} %all-to-all-done.1.tail_ref.rows_ref, bf16[128,128,256]{2,1,0:T(8,128)(2,1)} %get-tuple-element.22.pick_ref, f32[1,16384]{1,0:T(1,128)} %get-tuple-element.23.ids_ref, s32[16,16384]{1,0:T(8,128)} %target_ref.3, ...), custom_call_target="tpu_custom_call" | custom-call | flops 22000001024 | bytes 10485760 | tf_op jit(solution)/shard_map/pallas_call | solution.py:362
  135.3 4.7 %all-to-all-done.rows_ref = bf16[128,128,128]{2,1,0:T(8,128)(2,1)} async-done(((bf16[128,128,128]{2,1,0:T(8,128)(2,1)}), bf16[128,128,128]{2,1,0:T(8,128)(2,1)}, u32[]{:S(2)}, u32[]{:S(2)}) %all-to-all-start) | async-done | bytes 4194336 | tf_op jit(solution)/shard_map/all_to_all | solution.py:458
  140.1 8.6 %shard_map.91 = f32[32,24,128]{2,1,0:T(8,128)} custom-call(bf16[128,128,128]{2,1,0:T(8,128)(2,1)} %all-to-all-done.rows_ref, bf16[128,128,256]{2,1,0:T(8,128)(2,1)} %get-tuple-element.22.pick_ref, f32[1,16384]{1,0:T(1,128)} %get-tuple-element.23.ids_ref, s32[16,16384]{1,0:T(8,128)} %target_ref.3, f32[8,16,256]{2,1,0:T(8,128)} %get-tuple-element.29.sum_ref, ...), custom_call_target="tpu_custom_call" | custom-call | flops 4000000000 | bytes 9437184 | tf_op jit(solution)/shard_map/pallas_call | solution.py:409
  148.6 4.6 %all-to-all-start.2 = ((f32[32,24,128]{2,1,0:T(8,128)}), f32[32,24,128]{2,1,0:T(8,128)S(1)}, u32[]{:S(2)}, u32[]{:S(2)}) async-start(f32[32,24,128]{2,1,0:T(8,128)} %shard_map.91), calls=%async_computation.2 | async-start | bytes 786432 | tf_op jit(solution)/shard_map/all_to_all | solution.py:458
  153.2 12.6 %shard_map.92.before_ref = f32[16,16384]{1,0:T(8,128)} custom-call(bf16[128,128,128]{2,1,0:T(8,128)(2,1)} %all-to-all-done.rows_ref, bf16[128,128,256]{2,1,0:T(8,128)(2,1)} %get-tuple-element.22.pick_ref, f32[1,16384]{1,0:T(1,128)} %get-tuple-element.23.ids_ref, bf16[4096,256]{1,0:T(8,128)(2,1)} %shard_map.88.book_ref, ...), custom_call_target="tpu_custom_call", output_to_operand_aliasing={{}: (4, {})} | custom-call | flops 8800000000 | bytes 6291456 | tf_op jit(solution)/shard_map/pallas_call | solution.py:437
  165.8 0.0 all-to-all-done.2
  165.9 0.7 broadcast_in_dim.2
  166.6 7.5 %all-to-all-start.3 = ((f32[32,8,256]{2,1,0:T(8,128)}), f32[32,8,256]{2,1,0:T(8,128)S(1)}, u32[]{:S(2)}, u32[]{:S(2)}) async-start(f32[32,8,256]{2,1,0:T(8,128)} %broadcast_in_dim.2), calls=%async_computation.3 | async-start | bytes 524288 | tf_op jit(solution)/shard_map/all_to_all | solution.py:458
  174.1 12.6 %shard_map.93 = f32[16,16384]{1,0:T(8,128)} custom-call(bf16[128,128,128]{2,1,0:T(8,128)(2,1)} %all-to-all-done.rows_ref, bf16[128,128,256]{2,1,0:T(8,128)(2,1)} %get-tuple-element.22.pick_ref, f32[1,16384]{1,0:T(1,128)} %get-tuple-element.23.ids_ref, bf16[4096,256]{1,0:T(8,128)(2,1)} %shard_map.88.book_ref, ...), custom_call_target="tpu_custom_call", output_to_operand_aliasing={{}: (4, {})} | custom-call | flops 8800000000 | bytes 6291456 | tf_op jit(solution)/shard_map/pallas_call | solution.py:437
  186.7 0.0 all-to-all-done.3
  186.7 0.7 copy.14
  (4 shorter events, 0.1 us)
Async XLA Ops:
  14.3 67.4 %all-to-all-start.1 = ((bf16[128,136,128]{2,1,0:T(8,128)(2,1)}), bf16[128,136,128]{2,1,0:T(8,128)(2,1)}, u32[]{:S(2)}, u32[]{:S(2)}) async-start(bf16[128,136,128]{2,1,0:T(8,128)(2,1)} %bitcast.14), calls=%async_computation.1 | async-start | bytes 8912896 | tf_op jit(solution)/shard_map/all_to_all | solution.py:458
  81.7 58.3 %all-to-all-start = ((bf16[128,128,128]{2,1,0:T(8,128)(2,1)}), bf16[128,128,128]{2,1,0:T(8,128)(2,1)}, u32[]{:S(2)}, u32[]{:S(2)}) async-start(bf16[128,128,128]{2,1,0:T(8,128)(2,1)} %bitcast.15), calls=%async_computation | async-start | bytes 8388608 | tf_op jit(solution)/shard_map/all_to_all | solution.py:458
  148.6 17.1 %all-to-all-start.2 = ((f32[32,24,128]{2,1,0:T(8,128)}), f32[32,24,128]{2,1,0:T(8,128)S(1)}, u32[]{:S(2)}, u32[]{:S(2)}) async-start(f32[32,24,128]{2,1,0:T(8,128)} %shard_map.91), calls=%async_computation.2 | async-start | bytes 786432 | tf_op jit(solution)/shard_map/all_to_all | solution.py:458
  166.6 20.1 %all-to-all-start.3 = ((f32[32,8,256]{2,1,0:T(8,128)}), f32[32,8,256]{2,1,0:T(8,128)S(1)}, u32[]{:S(2)}, u32[]{:S(2)}) async-start(f32[32,8,256]{2,1,0:T(8,128)} %broadcast_in_dim.2), calls=%async_computation.3 | async-start | bytes 524288 | tf_op jit(solution)/shard_map/all_to_all | solution.py:458

commit v5 on v4

--- a/solution.py
+++ b/solution.py
@@ -315,7 +315,7 @@
     wide = jnp.concatenate([resid, jnp.ones((slots, 128), BF)], axis=1)
     lines = []
     for m in range(8):
-        mine = flipped[m * 16 : (m + 1) * 16]
+        mine = flipped[m * 16 : (m + 1) * 16].astype(F32)
         row_sq = jnp.sum(mine * mine, axis=0, keepdims=True)
         dist = nt(book_ref[m * CODES : (m + 1) * CODES], wide)
         least = jnp.min(dist, axis=0, keepdims=True)
@@ -343,9 +343,9 @@
         acc_ref[...] = jnp.zeros_like(acc_ref)
 
     resid = residual(rows_ref, pick_ref, slots)
-    flipped = resid.astype(F32).T
+    flipped = resid.T
     live = ids_ref[...] >= 0
-    add_sums(slots, flipped.astype(BF), live, target_ref[...], acc_ref)
+    add_sums(slots, flipped, live, target_ref[...], acc_ref)
     for m, line in enumerate(least_errors(slots, resid, flipped, live, book_ref)):
         error_ref[m : m + 1, :] = line
 
@@ -388,7 +388,7 @@
         out_ref[:, 16:, :] = jnp.zeros((OWNERS, 8, 128), F32)
 
     resid = residual(rows_ref, pick_ref, slots)
-    flipped = resid.astype(F32).T.astype(BF)
+    flipped = resid.T
     add_sums(slots, flipped, ids_ref[...] >= 0, target_ref[...], acc_ref)
 
     @pl.when(step == pl.num_programs(0) - 1)
@@ -424,10 +424,15 @@
 
 def last_errors_kernel(slots, rows_ref, pick_ref, ids_ref, book_ref, before_ref, out_ref):
     del before_ref
-    resid = residual(rows_ref, pick_ref, slots)
-    flipped = resid.astype(F32).T
-    for m, line in enumerate(least_errors(slots, resid, flipped, ids_ref[...] >= 0, book_ref)):
-        out_ref[m : m + 1, :] = line
+    blocks = 4
+    part = slots // blocks
+    for b in range(blocks):
+        sources = slice(b * part // CAP, (b + 1) * part // CAP)
+        at = slice(b * part, (b + 1) * part)
+        resid = residual(rows_ref.at[sources], pick_ref.at[sources], part)
+        live = ids_ref[:, at] >= 0
+        for m, line in enumerate(least_errors(part, resid, resid.T, live, book_ref)):
+            out_ref[m : m + 1, at] = line
 
 
 def last_errors(begin, end, rows, picked, ids, book, before):

time: 188 us -> 187 us (level)
  Pallas kernels: 112 us -> 110 us
  transfers between devices with their start and end apart: 4 -> 4, of which waited for: 2 -> 2; matrix products, arithmetic and copies ran while one was open for 0% -> 0% of each run, Pallas kernels for 48% -> 47%
where the time goes in v5:
time: 187 us; the launch traced here: 186 us
  Pallas kernels  110 us (59%)
  waiting for transfers between devices  43.6 us (23%)
  starting transfers between devices  29.6 us (16%)
    all_to_all x4, waiting for transfers between devices, exchange(): return lax.all_to_all(x, axes, split_axis=0, concat_axis=0, tiled=True)  43.6 us
    all_to_all x4, starting transfers between devices, exchange(): return lax.all_to_all(x, axes, split_axis=0, concat_axis=0, tiled=True)  29.6 us
    pallas_call x2, Pallas kernels, route(): pl.pallas_call(functools.partial(route_kernel, half, parts, row_steps, st...  27 us
    pallas_call x1, Pallas kernels, first_half(): pl.pallas_call(functools.partial(first_half_kernel, slots), grid=(SOURCES...  25.9 us
    pallas_call x2, Pallas kernels, last_errors(): pl.pallas_call(functools.partial(last_errors_kernel, slots), grid=(end -...  24.1 us
    pallas_call x1, Pallas kernels, pick(): pl.pallas_call(functools.partial(pick_kernel, step_sources), grid=(SOURCE...  21.8 us
    pallas_call x1, Pallas kernels, last_sums(): pl.pallas_call(functools.partial(last_sums_kernel, slots), grid=(SOURCES...  8.6 us
  transfers between devices with their start and end apart: 4, of which 2 were waited for; matrix products, arithmetic and copies ran while one was open for 0% of the time, Pallas kernels for 47%

profile of v5, /device:TPU:1, one launch (start us, length us, event | category | flops | bytes accessed | tf_op | source)
XLA Modules:
  0.0 186.4 jit_solution(3800847759106486326)
XLA Ops:
  0.6 13.7 %shard_map.86 = (bf16[4,32,136,128]{3,2,1,0:T(8,128)(2,1)}, s32[1,2048]{1,0:T(1,128)}, s32[32,128]{1,0:T(8,128)}) custom-call(s32[1,2048]{1,0:T(1,128)} %bitcast.19, s32[1,2048]{1,0:T(1,128)} %bitcast.20, bf16[2048,1024]{1,0:T(8,128)(2,1)} %refs_2_.3, bf16[1024,1024]{1,0:T(8,128)(2,1)} %refs_6_.3, bf16[1024,1024]{1,0:T(8,128)(2,1)} %refs_6_.3, ...), custom_call_target="tpu_custom_call" | custom-call | flops 8000000000 | bytes 10485760 | tf_op jit(solution)/shard_map/pallas_call | solution.py:183
  14.3 11.9 %all-to-all-start.1 = ((bf16[128,136,128]{2,1,0:T(8,128)(2,1)}), bf16[128,136,128]{2,1,0:T(8,128)(2,1)}, u32[]{:S(2)}, u32[]{:S(2)}) async-start(bf16[128,136,128]{2,1,0:T(8,128)(2,1)} %bitcast.14), calls=%async_computation.1 | async-start | bytes 8912896 | tf_op jit(solution)/shard_map/all_to_all | solution.py:463
  26.2 2.9 %shard_map.88.book_ref = bf16[4096,256]{1,0:T(8,128)(2,1)} custom-call(bf16[256,256]{1,0:T(8,128)(2,1)} %bitcast.17), custom_call_target="tpu_custom_call" | custom-call | flops 1000000000 | bytes 3145728 | tf_op jit(solution)/shard_map/pallas_call | solution.py:260
  29.1 0.7 convert_bitcast_fusion
  29.8 13.3 %shard_map.87 = bf16[4,32,128,128]{3,2,1,0:T(8,128)(2,1)} custom-call(s32[32,128]{1,0:T(8,128)} %get-tuple-element.18.refs_0_, s32[1,2048]{1,0:T(1,128)} %get-tuple-element.19.refs_1_, bf16[2048,1024]{1,0:T(8,128)(2,1)} %refs_2_.3, bf16[1024,1024]{1,0:T(8,128)(2,1)} %refs_6_.3, bf16[1024,1024]{1,0:T(8,128)(2,1)} %refs_6_.3, bf16[1024,1024]{1,0:T(8,128)(2,1)} %refs_6_.3, ...), custom_call_target="tpu_custom_call" | custom-call | flops 8000000000 | bytes 10485760 | tf_op jit(solution)/shard_map/pallas_call | solution.py:183
  43.2 38.5 %all-to-all-done.1.tail_ref.rows_ref = bf16[128,136,128]{2,1,0:T(8,128)(2,1)} async-done(((bf16[128,136,128]{2,1,0:T(8,128)(2,1)}), bf16[128,136,128]{2,1,0:T(8,128)(2,1)}, u32[]{:S(2)}, u32[]{:S(2)}) %all-to-all-start.1) | async-done | bytes 4456480 | tf_op jit(solution)/shard_map/all_to_all | solution.py:463
  81.7 5.6 %all-to-all-start = ((bf16[128,128,128]{2,1,0:T(8,128)(2,1)}), bf16[128,128,128]{2,1,0:T(8,128)(2,1)}, u32[]{:S(2)}, u32[]{:S(2)}) async-start(bf16[128,128,128]{2,1,0:T(8,128)(2,1)} %bitcast.15), calls=%async_computation | async-start | bytes 8388608 | tf_op jit(solution)/shard_map/all_to_all | solution.py:463
  87.3 21.8 %shard_map.89 = (bf16[128,128,256]{2,1,0:T(8,128)(2,1)}, f32[1,16384]{1,0:T(1,128)}) custom-call(bf16[128,136,128]{2,1,0:T(8,128)(2,1)} %all-to-all-done.1.tail_ref.rows_ref, bf16[2048,256]{1,0:T(8,128)(2,1)} %centroid_ref.1), custom_call_target="tpu_custom_call" | custom-call | flops 17999998976 | bytes 14680064 | tf_op jit(solution)/shard_map/pallas_call | solution.py:223
  109.1 25.9 %shard_map.90 = (f32[16,16384]{1,0:T(8,128)}, f32[8,16,256]{2,1,0:T(8,128)}, f32[8,256]{1,0:T(8,128)}) custom-call(bf16[128,136,128]{2,1,0:T(8,128)(2,1)} %all-to-all-done.1.tail_ref.rows_ref, bf16[128,128,256]{2,1,0:T(8,128)(2,1)} %get-tuple-element.22.pick_ref, f32[1,16384]{1,0:T(1,128)} %get-tuple-element.23.ids_ref, s32[16,16384]{1,0:T(8,128)} %target_ref.3, ...), custom_call_target="tpu_custom_call" | custom-call | flops 22000001024 | bytes 10485760 | tf_op jit(solution)/shard_map/pallas_call | solution.py:362
  135.0 5.0 %all-to-all-done.rows_ref = bf16[128,128,128]{2,1,0:T(8,128)(2,1)} async-done(((bf16[128,128,128]{2,1,0:T(8,128)(2,1)}), bf16[128,128,128]{2,1,0:T(8,128)(2,1)}, u32[]{:S(2)}, u32[]{:S(2)}) %all-to-all-start) | async-done | bytes 4194336 | tf_op jit(solution)/shard_map/all_to_all | solution.py:463
  140.1 8.6 %shard_map.91 = f32[32,24,128]{2,1,0:T(8,128)} custom-call(bf16[128,128,128]{2,1,0:T(8,128)(2,1)} %all-to-all-done.rows_ref, bf16[128,128,256]{2,1,0:T(8,128)(2,1)} %get-tuple-element.22.pick_ref, f32[1,16384]{1,0:T(1,128)} %get-tuple-element.23.ids_ref, s32[16,16384]{1,0:T(8,128)} %target_ref.3, f32[8,16,256]{2,1,0:T(8,128)} %get-tuple-element.29.sum_ref, ...), custom_call_target="tpu_custom_call" | custom-call | flops 4000000000 | bytes 9437184 | tf_op jit(solution)/shard_map/pallas_call | solution.py:409
  148.7 4.6 %all-to-all-start.2 = ((f32[32,24,128]{2,1,0:T(8,128)}), f32[32,24,128]{2,1,0:T(8,128)S(1)}, u32[]{:S(2)}, u32[]{:S(2)}) async-start(f32[32,24,128]{2,1,0:T(8,128)} %shard_map.91), calls=%async_computation.2 | async-start | bytes 786432 | tf_op jit(solution)/shard_map/all_to_all | solution.py:463
  153.2 12.1 %shard_map.92.before_ref = f32[16,16384]{1,0:T(8,128)} custom-call(bf16[128,128,128]{2,1,0:T(8,128)(2,1)} %all-to-all-done.rows_ref, bf16[128,128,256]{2,1,0:T(8,128)(2,1)} %get-tuple-element.22.pick_ref, f32[1,16384]{1,0:T(1,128)} %get-tuple-element.23.ids_ref, bf16[4096,256]{1,0:T(8,128)(2,1)} %shard_map.88.book_ref, ...), custom_call_target="tpu_custom_call", output_to_operand_aliasing={{}: (4, {})} | custom-call | flops 8800000000 | bytes 6291456 | tf_op jit(solution)/shard_map/pallas_call | solution.py:442
  165.3 0.0 all-to-all-done.2
  165.4 0.7 broadcast_in_dim.2
  166.1 7.5 %all-to-all-start.3 = ((f32[32,8,256]{2,1,0:T(8,128)}), f32[32,8,256]{2,1,0:T(8,128)S(1)}, u32[]{:S(2)}, u32[]{:S(2)}) async-start(f32[32,8,256]{2,1,0:T(8,128)} %broadcast_in_dim.2), calls=%async_computation.3 | async-start | bytes 524288 | tf_op jit(solution)/shard_map/all_to_all | solution.py:463
  173.6 12.1 %shard_map.93 = f32[16,16384]{1,0:T(8,128)} custom-call(bf16[128,128,128]{2,1,0:T(8,128)(2,1)} %all-to-all-done.rows_ref, bf16[128,128,256]{2,1,0:T(8,128)(2,1)} %get-tuple-element.22.pick_ref, f32[1,16384]{1,0:T(1,128)} %get-tuple-element.23.ids_ref, bf16[4096,256]{1,0:T(8,128)(2,1)} %shard_map.88.book_ref, ...), custom_call_target="tpu_custom_call", output_to_operand_aliasing={{}: (4, {})} | custom-call | flops 8800000000 | bytes 6291456 | tf_op jit(solution)/shard_map/pallas_call | solution.py:442
  185.7 0.0 all-to-all-done.3
  185.7 0.7 copy.14
  (4 shorter events, 0.1 us)
Async XLA Ops:
  14.3 67.4 %all-to-all-start.1 = ((bf16[128,136,128]{2,1,0:T(8,128)(2,1)}), bf16[128,136,128]{2,1,0:T(8,128)(2,1)}, u32[]{:S(2)}, u32[]{:S(2)}) async-start(bf16[128,136,128]{2,1,0:T(8,128)(2,1)} %bitcast.14), calls=%async_computation.1 | async-start | bytes 8912896 | tf_op jit(solution)/shard_map/all_to_all | solution.py:463
  81.7 58.3 %all-to-all-start = ((bf16[128,128,128]{2,1,0:T(8,128)(2,1)}), bf16[128,128,128]{2,1,0:T(8,128)(2,1)}, u32[]{:S(2)}, u32[]{:S(2)}) async-start(bf16[128,128,128]{2,1,0:T(8,128)(2,1)} %bitcast.15), calls=%async_computation | async-start | bytes 8388608 | tf_op jit(solution)/shard_map/all_to_all | solution.py:463
  148.7 16.7 %all-to-all-start.2 = ((f32[32,24,128]{2,1,0:T(8,128)}), f32[32,24,128]{2,1,0:T(8,128)S(1)}, u32[]{:S(2)}, u32[]{:S(2)}) async-start(f32[32,24,128]{2,1,0:T(8,128)} %shard_map.91), calls=%async_computation.2 | async-start | bytes 786432 | tf_op jit(solution)/shard_map/all_to_all | solution.py:463
  166.1 19.6 %all-to-all-start.3 = ((f32[32,8,256]{2,1,0:T(8,128)}), f32[32,8,256]{2,1,0:T(8,128)S(1)}, u32[]{:S(2)}, u32[]{:S(2)}) async-start(f32[32,8,256]{2,1,0:T(8,128)} %broadcast_in_dim.2), calls=%async_computation.3 | async-start | bytes 524288 | tf_op jit(solution)/shard_map/all_to_all | solution.py:463

commit v6 on v5

--- a/solution.py
+++ b/solution.py
@@ -44,7 +44,7 @@
 
 
 ORDERED = ROWS + 16 * OWNERS
-ID_ROWS = 8
+ID_ROWS = 16
 
 
 def rank_rows(owner, lists):
@@ -152,7 +152,7 @@
 
 
 def route(half, first_arg, second_arg, embeddings, matrix):
-    step_owners = 8
+    step_owners = 16
     parts = 4
     row_steps = 5
     depth = CAP + (ID_ROWS if half == 0 else 0)

time: 187 us -> 190 us (1.016)
  waiting for transfers between devices: 43.6 us -> 46.5 us
    all_to_all x4, waiting for transfers between devices: 43.6 us -> 46.5 us  [exchange(): return lax.all_to_all(x, axes, split_axis=0, concat_axis=0, tiled=True)]
  transfers between devices with their start and end apart: 4 -> 4, of which waited for: 2 -> 2; matrix products, arithmetic and copies ran while one was open for 0% -> 0% of each run, Pallas kernels for 47% -> 46%
where the time goes in v6:
time: 190 us; the launch traced here: 189 us
  Pallas kernels  110 us (58%)
  waiting for transfers between devices  46.5 us (24%)
  starting transfers between devices  29.7 us (16%)
    all_to_all x4, waiting for transfers between devices, exchange(): return lax.all_to_all(x, axes, split_axis=0, concat_axis=0, tiled=True)  46.5 us
    all_to_all x4, starting transfers between devices, exchange(): return lax.all_to_all(x, axes, split_axis=0, concat_axis=0, tiled=True)  29.7 us
    pallas_call x2, Pallas kernels, route(): pl.pallas_call(functools.partial(route_kernel, half, parts, row_steps, st...  26.5 us
    pallas_call x1, Pallas kernels, first_half(): pl.pallas_call(functools.partial(first_half_kernel, slots), grid=(SOURCES...  25.9 us
    pallas_call x2, Pallas kernels, last_errors(): pl.pallas_call(functools.partial(last_errors_kernel, slots), grid=(end -...  24.1 us
    pallas_call x1, Pallas kernels, pick(): pl.pallas_call(functools.partial(pick_kernel, step_sources), grid=(SOURCE...  21.8 us
    pallas_call x1, Pallas kernels, last_sums(): pl.pallas_call(functools.partial(last_sums_kernel, slots), grid=(SOURCES...  8.6 us
  transfers between devices with their start and end apart: 4, of which 2 were waited for; matrix products, arithmetic and copies ran while one was open for 0% of the time, Pallas kernels for 46%

profile of v6, /device:TPU:1, one launch (start us, length us, event | category | flops | bytes accessed | tf_op | source)
XLA Modules:
  0.0 189.0 jit_solution(9235049595142993579)
XLA Ops:
  0.6 13.4 %shard_map.86 = (bf16[4,32,144,128]{3,2,1,0:T(8,128)(2,1)}, s32[1,2048]{1,0:T(1,128)}, s32[32,128]{1,0:T(8,128)}) custom-call(s32[1,2048]{1,0:T(1,128)} %bitcast.19, s32[1,2048]{1,0:T(1,128)} %bitcast.20, bf16[2048,1024]{1,0:T(8,128)(2,1)} %refs_2_.3, bf16[1024,1024]{1,0:T(8,128)(2,1)} %refs_6_.3, bf16[1024,1024]{1,0:T(8,128)(2,1)} %refs_6_.3, ...), custom_call_target="tpu_custom_call" | custom-call | flops 8000000000 | bytes 10485760 | tf_op jit(solution)/shard_map/pallas_call | solution.py:183
  14.1 11.9 %all-to-all-start.1 = ((bf16[128,144,128]{2,1,0:T(8,128)(2,1)}), bf16[128,144,128]{2,1,0:T(8,128)(2,1)}, u32[]{:S(2)}, u32[]{:S(2)}) async-start(bf16[128,144,128]{2,1,0:T(8,128)(2,1)} %bitcast.14), calls=%async_computation.1 | async-start | bytes 9437184 | tf_op jit(solution)/shard_map/all_to_all | solution.py:463
  26.0 2.9 %shard_map.88.book_ref = bf16[4096,256]{1,0:T(8,128)(2,1)} custom-call(bf16[256,256]{1,0:T(8,128)(2,1)} %bitcast.17), custom_call_target="tpu_custom_call" | custom-call | flops 1000000000 | bytes 3145728 | tf_op jit(solution)/shard_map/pallas_call | solution.py:260
  28.9 0.7 convert_bitcast_fusion
  29.6 13.0 %shard_map.87 = bf16[4,32,128,128]{3,2,1,0:T(8,128)(2,1)} custom-call(s32[32,128]{1,0:T(8,128)} %get-tuple-element.18.refs_0_, s32[1,2048]{1,0:T(1,128)} %get-tuple-element.19.refs_1_, bf16[2048,1024]{1,0:T(8,128)(2,1)} %refs_2_.3, bf16[1024,1024]{1,0:T(8,128)(2,1)} %refs_6_.3, bf16[1024,1024]{1,0:T(8,128)(2,1)} %refs_6_.3, bf16[1024,1024]{1,0:T(8,128)(2,1)} %refs_6_.3, ...), custom_call_target="tpu_custom_call" | custom-call | flops 8000000000 | bytes 10485760 | tf_op jit(solution)/shard_map/pallas_call | solution.py:183
  42.6 41.6 %all-to-all-done.1.tail_ref.rows_ref = bf16[128,144,128]{2,1,0:T(8,128)(2,1)} async-done(((bf16[128,144,128]{2,1,0:T(8,128)(2,1)}), bf16[128,144,128]{2,1,0:T(8,128)(2,1)}, u32[]{:S(2)}, u32[]{:S(2)}) %all-to-all-start.1) | async-done | bytes 4718624 | tf_op jit(solution)/shard_map/all_to_all | solution.py:463
  84.3 5.7 %all-to-all-start = ((bf16[128,128,128]{2,1,0:T(8,128)(2,1)}), bf16[128,128,128]{2,1,0:T(8,128)(2,1)}, u32[]{:S(2)}, u32[]{:S(2)}) async-start(bf16[128,128,128]{2,1,0:T(8,128)(2,1)} %bitcast.15), calls=%async_computation | async-start | bytes 8388608 | tf_op jit(solution)/shard_map/all_to_all | solution.py:463
  90.0 21.8 %shard_map.89 = (bf16[128,128,256]{2,1,0:T(8,128)(2,1)}, f32[1,16384]{1,0:T(1,128)}) custom-call(bf16[128,144,128]{2,1,0:T(8,128)(2,1)} %all-to-all-done.1.tail_ref.rows_ref, bf16[2048,256]{1,0:T(8,128)(2,1)} %centroid_ref.1), custom_call_target="tpu_custom_call" | custom-call | flops 17999998976 | bytes 14680064 | tf_op jit(solution)/shard_map/pallas_call | solution.py:223
  111.8 25.9 %shard_map.90 = (f32[16,16384]{1,0:T(8,128)}, f32[8,16,256]{2,1,0:T(8,128)}, f32[8,256]{1,0:T(8,128)}) custom-call(bf16[128,144,128]{2,1,0:T(8,128)(2,1)} %all-to-all-done.1.tail_ref.rows_ref, bf16[128,128,256]{2,1,0:T(8,128)(2,1)} %get-tuple-element.22.pick_ref, f32[1,16384]{1,0:T(1,128)} %get-tuple-element.23.ids_ref, s32[16,16384]{1,0:T(8,128)} %target_ref.3, ...), custom_call_target="tpu_custom_call" | custom-call | flops 22000001024 | bytes 10485760 | tf_op jit(solution)/shard_map/pallas_call | solution.py:362
  137.7 4.9 %all-to-all-done.rows_ref = bf16[128,128,128]{2,1,0:T(8,128)(2,1)} async-done(((bf16[128,128,128]{2,1,0:T(8,128)(2,1)}), bf16[128,128,128]{2,1,0:T(8,128)(2,1)}, u32[]{:S(2)}, u32[]{:S(2)}) %all-to-all-start) | async-done | bytes 4194336 | tf_op jit(solution)/shard_map/all_to_all | solution.py:463
  142.6 8.6 %shard_map.91 = f32[32,24,128]{2,1,0:T(8,128)} custom-call(bf16[128,128,128]{2,1,0:T(8,128)(2,1)} %all-to-all-done.rows_ref, bf16[128,128,256]{2,1,0:T(8,128)(2,1)} %get-tuple-element.22.pick_ref, f32[1,16384]{1,0:T(1,128)} %get-tuple-element.23.ids_ref, s32[16,16384]{1,0:T(8,128)} %target_ref.3, f32[8,16,256]{2,1,0:T(8,128)} %get-tuple-element.29.sum_ref, ...), custom_call_target="tpu_custom_call" | custom-call | flops 4000000000 | bytes 9437184 | tf_op jit(solution)/shard_map/pallas_call | solution.py:409
  151.2 4.6 %all-to-all-start.2 = ((f32[32,24,128]{2,1,0:T(8,128)}), f32[32,24,128]{2,1,0:T(8,128)S(1)}, u32[]{:S(2)}, u32[]{:S(2)}) async-start(f32[32,24,128]{2,1,0:T(8,128)} %shard_map.91), calls=%async_computation.2 | async-start | bytes 786432 | tf_op jit(solution)/shard_map/all_to_all | solution.py:463
  155.8 12.1 %shard_map.92.before_ref = f32[16,16384]{1,0:T(8,128)} custom-call(bf16[128,128,128]{2,1,0:T(8,128)(2,1)} %all-to-all-done.rows_ref, bf16[128,128,256]{2,1,0:T(8,128)(2,1)} %get-tuple-element.22.pick_ref, f32[1,16384]{1,0:T(1,128)} %get-tuple-element.23.ids_ref, bf16[4096,256]{1,0:T(8,128)(2,1)} %shard_map.88.book_ref, ...), custom_call_target="tpu_custom_call", output_to_operand_aliasing={{}: (4, {})} | custom-call | flops 8800000000 | bytes 6291456 | tf_op jit(solution)/shard_map/pallas_call | solution.py:442
  167.9 0.0 all-to-all-done.2
  167.9 0.7 broadcast_in_dim.2
  168.7 7.5 %all-to-all-start.3 = ((f32[32,8,256]{2,1,0:T(8,128)}), f32[32,8,256]{2,1,0:T(8,128)S(1)}, u32[]{:S(2)}, u32[]{:S(2)}) async-start(f32[32,8,256]{2,1,0:T(8,128)} %broadcast_in_dim.2), calls=%async_computation.3 | async-start | bytes 524288 | tf_op jit(solution)/shard_map/all_to_all | solution.py:463
  176.2 12.1 %shard_map.93 = f32[16,16384]{1,0:T(8,128)} custom-call(bf16[128,128,128]{2,1,0:T(8,128)(2,1)} %all-to-all-done.rows_ref, bf16[128,128,256]{2,1,0:T(8,128)(2,1)} %get-tuple-element.22.pick_ref, f32[1,16384]{1,0:T(1,128)} %get-tuple-element.23.ids_ref, bf16[4096,256]{1,0:T(8,128)(2,1)} %shard_map.88.book_ref, ...), custom_call_target="tpu_custom_call", output_to_operand_aliasing={{}: (4, {})} | custom-call | flops 8800000000 | bytes 6291456 | tf_op jit(solution)/shard_map/pallas_call | solution.py:442
  188.2 0.0 all-to-all-done.3
  188.3 0.7 copy.14
  (4 shorter events, 0.1 us)
Async XLA Ops:
  14.1 70.2 %all-to-all-start.1 = ((bf16[128,144,128]{2,1,0:T(8,128)(2,1)}), bf16[128,144,128]{2,1,0:T(8,128)(2,1)}, u32[]{:S(2)}, u32[]{:S(2)}) async-start(bf16[128,144,128]{2,1,0:T(8,128)(2,1)} %bitcast.14), calls=%async_computation.1 | async-start | bytes 9437184 | tf_op jit(solution)/shard_map/all_to_all | solution.py:463
  84.3 58.3 %all-to-all-start = ((bf16[128,128,128]{2,1,0:T(8,128)(2,1)}), bf16[128,128,128]{2,1,0:T(8,128)(2,1)}, u32[]{:S(2)}, u32[]{:S(2)}) async-start(bf16[128,128,128]{2,1,0:T(8,128)(2,1)} %bitcast.15), calls=%async_computation | async-start | bytes 8388608 | tf_op jit(solution)/shard_map/all_to_all | solution.py:463
  151.2 16.7 %all-to-all-start.2 = ((f32[32,24,128]{2,1,0:T(8,128)}), f32[32,24,128]{2,1,0:T(8,128)S(1)}, u32[]{:S(2)}, u32[]{:S(2)}) async-start(f32[32,24,128]{2,1,0:T(8,128)} %shard_map.91), calls=%async_computation.2 | async-start | bytes 786432 | tf_op jit(solution)/shard_map/all_to_all | solution.py:463
  168.7 19.6 %all-to-all-start.3 = ((f32[32,8,256]{2,1,0:T(8,128)}), f32[32,8,256]{2,1,0:T(8,128)S(1)}, u32[]{:S(2)}, u32[]{:S(2)}) async-start(f32[32,8,256]{2,1,0:T(8,128)} %broadcast_in_dim.2), calls=%async_computation.3 | async-start | bytes 524288 | tf_op jit(solution)/shard_map/all_to_all | solution.py:463

commit v7 on v5

--- a/solution.py
+++ b/solution.py
@@ -81,36 +81,38 @@
     return place, first.astype(I32), ids
 
 
-def matrix_columns(half):
-    return [
-        pl.BlockSpec((WIDTH, 128), functools.partial(lambda col, i: (0, col), 2 * g + half))
-        for g in range(GROUPS)
-    ]
-
-
-def order_rows(place, rot_ref, run_ref, row_steps):
+def order_rows(place, rot_ref, run_ref, row_steps, chunks):
     run_rows = ORDERED // row_steps
     one = jnp.ones((), BF)
     zero = jnp.zeros((), BF)
     digit = lax.broadcasted_iota(I32, (run_rows, ROWS), 0).astype(I16)
-    for k in range(row_steps):
+    for k in chunks:
         hot = jnp.where((place - k * run_rows).astype(I16) == digit, one, zero)
         run_ref[k * run_rows : (k + 1) * run_rows, :] = nn(hot, rot_ref[...]).astype(BF)
-    run_ref[ORDERED:, :] = jnp.zeros((CAP, GROUPS * 128), BF)
 
 
 def route_kernel(half, parts, row_steps, step_owners, *refs):
     if half == 0:
-        owner_ref, list_ref, rows_hbm, r0, r1, r2, r3, out_ref, place_ref, first_ref = refs[:10]
-        start_ref, ids_ref, rows_ref, rot_ref, run_ref, in_sem, start_sem = refs[10:]
+        owner_ref, list_ref, rows_hbm, matrix_hbm, out_ref, place_ref, first_ref = refs[:7]
+        start_ref, ids_ref, rows_ref, matrix_ref, rot_ref, run_ref, in_sem, matrix_sem, start_sem = refs[7:]
     else:
-        start_ref, place_ref, rows_hbm, r0, r1, r2, r3, out_ref = refs[:8]
-        rows_ref, rot_ref, run_ref, in_sem = refs[8:]
+        start_ref, place_ref, rows_hbm, matrix_hbm, out_ref = refs[:5]
+        rows_ref, matrix_ref, rot_ref, run_ref, in_sem, matrix_sem = refs[5:]
     step = pl.program_id(0)
     part_rows = ROWS // parts
 
     @pl.when(step == 0)
     def _():
+        columns = []
+        for g in range(GROUPS):
+            columns.append(
+                pltpu.make_async_copy(
+                    matrix_hbm.at[:, pl.ds((2 * g + half) * 128, 128)],
+                    matrix_ref.at[:, pl.ds(g * 128, 128)],
+                    matrix_sem.at[g],
+                )
+            )
+            columns[g].start()
         copies = []
         for k in range(parts):
             part = pl.ds(k * part_rows, part_rows)
@@ -125,14 +127,24 @@
             ids_ref[...] = ids
             starts = pltpu.make_async_copy(first_ref, start_ref, start_sem)
             starts.start()
-        matrix = jnp.concatenate([r[...] for r in (r0, r1, r2, r3)], axis=1)
+        rest = ORDERED + CAP - step_owners * CAP
+        run_ref[step_owners * CAP :, :] = jnp.zeros((rest, GROUPS * 128), BF)
+        for copy in columns:
+            copy.wait()
         for k in range(parts):
             part = pl.ds(k * part_rows, part_rows)
             copies[k].wait()
-            rot_ref[part, :] = nn(rows_ref[part, :], matrix).astype(BF)
-        order_rows(place_ref[...], rot_ref, run_ref, row_steps)
+            rot_ref[part, :] = nn(rows_ref[part, :], matrix_ref[...]).astype(BF)
         if half == 0:
             starts.wait()
+
+    needed = step_owners * CAP * row_steps // ORDERED
+    for k in range(-(-row_steps // needed)):
+        chunks = range(k * needed, min((k + 1) * needed, row_steps))
+
+        @pl.when(step == k)
+        def _(chunks=chunks):
+            order_rows(place_ref[...], rot_ref, run_ref, row_steps, chunks)
 
     line = lax.broadcasted_iota(I32, (ID_ROWS, CAP), 0)
     for j in range(step_owners):
@@ -153,7 +165,7 @@
 
 def route(half, first_arg, second_arg, embeddings, matrix):
     step_owners = 8
-    parts = 4
+    parts = 2
     row_steps = 5
     depth = CAP + (ID_ROWS if half == 0 else 0)
     line = pl.BlockSpec((1, ROWS), lambda i: (0, 0))
@@ -161,9 +173,11 @@
     out_shape = [jax.ShapeDtypeStruct((GROUPS, OWNERS, depth, 128), BF)]
     scratch = [
         pltpu.VMEM((ROWS, WIDTH), BF),
+        pltpu.VMEM((WIDTH, GROUPS * 128), BF),
         pltpu.VMEM((ROWS, GROUPS * 128), BF),
         pltpu.VMEM((ORDERED + CAP, GROUPS * 128), BF),
         pltpu.SemaphoreType.DMA((parts,)),
+        pltpu.SemaphoreType.DMA((GROUPS,)),
     ]
     if half == 0:
         inputs = [line, line]
@@ -183,13 +197,13 @@
     return pl.pallas_call(
         functools.partial(route_kernel, half, parts, row_steps, step_owners),
         grid=(OWNERS // step_owners,),
-        in_specs=[*inputs, pl.BlockSpec(memory_space=pl.ANY), *matrix_columns(half)],
+        in_specs=[*inputs, pl.BlockSpec(memory_space=pl.ANY), pl.BlockSpec(memory_space=pl.ANY)],
         out_specs=out_specs,
         out_shape=out_shape,
         scratch_shapes=scratch,
         compiler_params=params(60),
         cost_estimate=cost(8e9, 10 * MIB),
-    )(first_arg, second_arg, embeddings, matrix, matrix, matrix, matrix)
+    )(first_arg, second_arg, embeddings, matrix)
 
 
 def pick_kernel(step_sources, tail_ref, centroid_ref, out_ref, ids_ref):

time: 187 us -> 187 us (level)
  no operation moved by 1% of the time
where the time goes in v7:
time: 187 us; the launch traced here: 186 us
  Pallas kernels  109 us (58%)
  waiting for transfers between devices  44 us (24%)
  starting transfers between devices  29.6 us (16%)
    all_to_all x4, waiting for transfers between devices, exchange(): return lax.all_to_all(x, axes, split_axis=0, concat_axis=0, tiled=True)  44 us
    all_to_all x4, starting transfers between devices, exchange(): return lax.all_to_all(x, axes, split_axis=0, concat_axis=0, tiled=True)  29.6 us
    pallas_call x2, Pallas kernels, route(): pl.pallas_call(functools.partial(route_kernel, half, parts, row_steps, st...  26 us
    pallas_call x1, Pallas kernels, first_half(): pl.pallas_call(functools.partial(first_half_kernel, slots), grid=(SOURCES...  25.9 us
    pallas_call x2, Pallas kernels, last_errors(): pl.pallas_call(functools.partial(last_errors_kernel, slots), grid=(end -...  24.1 us
    pallas_call x1, Pallas kernels, pick(): pl.pallas_call(functools.partial(pick_kernel, step_sources), grid=(SOURCE...  21.8 us
    pallas_call x1, Pallas kernels, last_sums(): pl.pallas_call(functools.partial(last_sums_kernel, slots), grid=(SOURCES...  8.61 us
  transfers between devices with their start and end apart: 4, of which 2 were waited for; matrix products, arithmetic and copies ran while one was open for 0% of the time, Pallas kernels for 47%

profile of v7, /device:TPU:1, one launch (start us, length us, event | category | flops | bytes accessed | tf_op | source)
XLA Modules:
  0.0 185.9 jit_solution(13707358777428354668)
XLA Ops:
  0.6 13.2 %shard_map.86 = (bf16[4,32,136,128]{3,2,1,0:T(8,128)(2,1)}, s32[1,2048]{1,0:T(1,128)}, s32[32,128]{1,0:T(8,128)}) custom-call(s32[1,2048]{1,0:T(1,128)} %bitcast.19, s32[1,2048]{1,0:T(1,128)} %bitcast.20, bf16[2048,1024]{1,0:T(8,128)(2,1)} %refs_2_.3, bf16[1024,1024]{1,0:T(8,128)(2,1)} %refs_3_.3), custom_call_target="tpu_custom_call" | custom-call | flops 8000000000 | bytes 10485760 | tf_op jit(solution)/shard_map/pallas_call | solution.py:197
  13.8 11.9 %all-to-all-start.1 = ((bf16[128,136,128]{2,1,0:T(8,128)(2,1)}), bf16[128,136,128]{2,1,0:T(8,128)(2,1)}, u32[]{:S(2)}, u32[]{:S(2)}) async-start(bf16[128,136,128]{2,1,0:T(8,128)(2,1)} %bitcast.14), calls=%async_computation.1 | async-start | bytes 8912896 | tf_op jit(solution)/shard_map/all_to_all | solution.py:477
  25.7 2.9 %shard_map.88.book_ref = bf16[4096,256]{1,0:T(8,128)(2,1)} custom-call(bf16[256,256]{1,0:T(8,128)(2,1)} %bitcast.17), custom_call_target="tpu_custom_call" | custom-call | flops 1000000000 | bytes 3145728 | tf_op jit(solution)/shard_map/pallas_call | solution.py:274
  28.6 0.7 convert_bitcast_fusion
  29.3 12.9 %shard_map.87 = bf16[4,32,128,128]{3,2,1,0:T(8,128)(2,1)} custom-call(s32[32,128]{1,0:T(8,128)} %get-tuple-element.18.refs_0_, s32[1,2048]{1,0:T(1,128)} %get-tuple-element.19.refs_1_, bf16[2048,1024]{1,0:T(8,128)(2,1)} %refs_2_.3, bf16[1024,1024]{1,0:T(8,128)(2,1)} %refs_3_.3), custom_call_target="tpu_custom_call" | custom-call | flops 8000000000 | bytes 10485760 | tf_op jit(solution)/shard_map/pallas_call | solution.py:197
  42.2 39.0 %all-to-all-done.1.tail_ref.rows_ref = bf16[128,136,128]{2,1,0:T(8,128)(2,1)} async-done(((bf16[128,136,128]{2,1,0:T(8,128)(2,1)}), bf16[128,136,128]{2,1,0:T(8,128)(2,1)}, u32[]{:S(2)}, u32[]{:S(2)}) %all-to-all-start.1) | async-done | bytes 4456480 | tf_op jit(solution)/shard_map/all_to_all | solution.py:477
  81.2 5.6 %all-to-all-start = ((bf16[128,128,128]{2,1,0:T(8,128)(2,1)}), bf16[128,128,128]{2,1,0:T(8,128)(2,1)}, u32[]{:S(2)}, u32[]{:S(2)}) async-start(bf16[128,128,128]{2,1,0:T(8,128)(2,1)} %bitcast.15), calls=%async_computation | async-start | bytes 8388608 | tf_op jit(solution)/shard_map/all_to_all | solution.py:477
  86.8 21.8 %shard_map.89 = (bf16[128,128,256]{2,1,0:T(8,128)(2,1)}, f32[1,16384]{1,0:T(1,128)}) custom-call(bf16[128,136,128]{2,1,0:T(8,128)(2,1)} %all-to-all-done.1.tail_ref.rows_ref, bf16[2048,256]{1,0:T(8,128)(2,1)} %centroid_ref.1), custom_call_target="tpu_custom_call" | custom-call | flops 17999998976 | bytes 14680064 | tf_op jit(solution)/shard_map/pallas_call | solution.py:237
  108.6 25.9 %shard_map.90 = (f32[16,16384]{1,0:T(8,128)}, f32[8,16,256]{2,1,0:T(8,128)}, f32[8,256]{1,0:T(8,128)}) custom-call(bf16[128,136,128]{2,1,0:T(8,128)(2,1)} %all-to-all-done.1.tail_ref.rows_ref, bf16[128,128,256]{2,1,0:T(8,128)(2,1)} %get-tuple-element.22.pick_ref, f32[1,16384]{1,0:T(1,128)} %get-tuple-element.23.ids_ref, s32[16,16384]{1,0:T(8,128)} %target_ref.3, ...), custom_call_target="tpu_custom_call" | custom-call | flops 22000001024 | bytes 10485760 | tf_op jit(solution)/shard_map/pallas_call | solution.py:376
  134.5 5.0 %all-to-all-done.rows_ref = bf16[128,128,128]{2,1,0:T(8,128)(2,1)} async-done(((bf16[128,128,128]{2,1,0:T(8,128)(2,1)}), bf16[128,128,128]{2,1,0:T(8,128)(2,1)}, u32[]{:S(2)}, u32[]{:S(2)}) %all-to-all-start) | async-done | bytes 4194336 | tf_op jit(solution)/shard_map/all_to_all | solution.py:477
  139.5 8.6 %shard_map.91 = f32[32,24,128]{2,1,0:T(8,128)} custom-call(bf16[128,128,128]{2,1,0:T(8,128)(2,1)} %all-to-all-done.rows_ref, bf16[128,128,256]{2,1,0:T(8,128)(2,1)} %get-tuple-element.22.pick_ref, f32[1,16384]{1,0:T(1,128)} %get-tuple-element.23.ids_ref, s32[16,16384]{1,0:T(8,128)} %target_ref.3, f32[8,16,256]{2,1,0:T(8,128)} %get-tuple-element.29.sum_ref, ...), custom_call_target="tpu_custom_call" | custom-call | flops 4000000000 | bytes 9437184 | tf_op jit(solution)/shard_map/pallas_call | solution.py:423
  148.1 4.6 %all-to-all-start.2 = ((f32[32,24,128]{2,1,0:T(8,128)}), f32[32,24,128]{2,1,0:T(8,128)S(1)}, u32[]{:S(2)}, u32[]{:S(2)}) async-start(f32[32,24,128]{2,1,0:T(8,128)} %shard_map.91), calls=%async_computation.2 | async-start | bytes 786432 | tf_op jit(solution)/shard_map/all_to_all | solution.py:477
  152.7 12.1 %shard_map.92.before_ref = f32[16,16384]{1,0:T(8,128)} custom-call(bf16[128,128,128]{2,1,0:T(8,128)(2,1)} %all-to-all-done.rows_ref, bf16[128,128,256]{2,1,0:T(8,128)(2,1)} %get-tuple-element.22.pick_ref, f32[1,16384]{1,0:T(1,128)} %get-tuple-element.23.ids_ref, bf16[4096,256]{1,0:T(8,128)(2,1)} %shard_map.88.book_ref, ...), custom_call_target="tpu_custom_call", output_to_operand_aliasing={{}: (4, {})} | custom-call | flops 8800000000 | bytes 6291456 | tf_op jit(solution)/shard_map/pallas_call | solution.py:456
  164.8 0.0 all-to-all-done.2
  164.9 0.7 broadcast_in_dim.2
  165.6 7.5 %all-to-all-start.3 = ((f32[32,8,256]{2,1,0:T(8,128)}), f32[32,8,256]{2,1,0:T(8,128)S(1)}, u32[]{:S(2)}, u32[]{:S(2)}) async-start(f32[32,8,256]{2,1,0:T(8,128)} %broadcast_in_dim.2), calls=%async_computation.3 | async-start | bytes 524288 | tf_op jit(solution)/shard_map/all_to_all | solution.py:477
  173.1 12.1 %shard_map.93 = f32[16,16384]{1,0:T(8,128)} custom-call(bf16[128,128,128]{2,1,0:T(8,128)(2,1)} %all-to-all-done.rows_ref, bf16[128,128,256]{2,1,0:T(8,128)(2,1)} %get-tuple-element.22.pick_ref, f32[1,16384]{1,0:T(1,128)} %get-tuple-element.23.ids_ref, bf16[4096,256]{1,0:T(8,128)(2,1)} %shard_map.88.book_ref, ...), custom_call_target="tpu_custom_call", output_to_operand_aliasing={{}: (4, {})} | custom-call | flops 8800000000 | bytes 6291456 | tf_op jit(solution)/shard_map/pallas_call | solution.py:456
  185.2 0.0 all-to-all-done.3
  185.2 0.7 copy.14
  (4 shorter events, 0.1 us)
Async XLA Ops:
  13.8 67.4 %all-to-all-start.1 = ((bf16[128,136,128]{2,1,0:T(8,128)(2,1)}), bf16[128,136,128]{2,1,0:T(8,128)(2,1)}, u32[]{:S(2)}, u32[]{:S(2)}) async-start(bf16[128,136,128]{2,1,0:T(8,128)(2,1)} %bitcast.14), calls=%async_computation.1 | async-start | bytes 8912896 | tf_op jit(solution)/shard_map/all_to_all | solution.py:477
  81.2 58.3 %all-to-all-start = ((bf16[128,128,128]{2,1,0:T(8,128)(2,1)}), bf16[128,128,128]{2,1,0:T(8,128)(2,1)}, u32[]{:S(2)}, u32[]{:S(2)}) async-start(bf16[128,128,128]{2,1,0:T(8,128)(2,1)} %bitcast.15), calls=%async_computation | async-start | bytes 8388608 | tf_op jit(solution)/shard_map/all_to_all | solution.py:477
  148.1 16.7 %all-to-all-start.2 = ((f32[32,24,128]{2,1,0:T(8,128)}), f32[32,24,128]{2,1,0:T(8,128)S(1)}, u32[]{:S(2)}, u32[]{:S(2)}) async-start(f32[32,24,128]{2,1,0:T(8,128)} %shard_map.91), calls=%async_computation.2 | async-start | bytes 786432 | tf_op jit(solution)/shard_map/all_to_all | solution.py:477
  165.6 19.6 %all-to-all-start.3 = ((f32[32,8,256]{2,1,0:T(8,128)}), f32[32,8,256]{2,1,0:T(8,128)S(1)}, u32[]{:S(2)}, u32[]{:S(2)}) async-start(f32[32,8,256]{2,1,0:T(8,128)} %broadcast_in_dim.2), calls=%async_computation.3 | async-start | bytes 524288 | tf_op jit(solution)/shard_map/all_to_all | solution.py:477

commit v8 on v7

--- a/solution.py
+++ b/solution.py
@@ -166,7 +166,7 @@
 def route(half, first_arg, second_arg, embeddings, matrix):
     step_owners = 8
     parts = 2
-    row_steps = 5
+    row_steps = 10
     depth = CAP + (ID_ROWS if half == 0 else 0)
     line = pl.BlockSpec((1, ROWS), lambda i: (0, 0))
     out_specs = [pl.BlockSpec((GROUPS, step_owners, depth, 128), lambda i: (0, i, 0, 0))]
@@ -438,7 +438,7 @@
 
 def last_errors_kernel(slots, rows_ref, pick_ref, ids_ref, book_ref, before_ref, out_ref):
     del before_ref
-    blocks = 4
+    blocks = 2
     part = slots // blocks
     for b in range(blocks):
         sources = slice(b * part // CAP, (b + 1) * part // CAP)
@@ -450,7 +450,7 @@
 
 
 def last_errors(begin, end, rows, picked, ids, book, before):
-    step_sources = 32
+    step_sources = 16
     slots = step_sources * CAP
     specs = half_specs(step_sources, 1, begin)
     return pl.pallas_call(
@@ -461,7 +461,7 @@
         out_shape=jax.ShapeDtypeStruct((16, SLOTS), F32),
         input_output_aliases={4: 0},
         compiler_params=params(60),
-        cost_estimate=cost(4.4e9 * (end - begin), (end - begin) * 3 * MIB),
+        cost_estimate=cost(2.2e9 * (end - begin), (end - begin) * 1.5 * MIB),
     )(rows, picked, ids, book, before)
 
 
@@ -496,11 +496,11 @@
     quant_error, sums, counts = first_half(rows0, picked, ids, code_targets, book)
     rows1, quant_error, sums = lax.optimization_barrier((rows1, quant_error, sums))
     pieces = last_sums(rows1, picked, ids, code_targets, sums, counts)
-    quant_error = last_errors(0, 2, rows1, picked, ids, book, quant_error)
+    quant_error = last_errors(0, 4, rows1, picked, ids, book, quant_error)
     got = exchange(pieces, "lists")
     piece, quant_error = lax.optimization_barrier((new_piece(got, codes), quant_error))
     spread = exchange(piece, "lists")
-    quant_error = last_errors(2, 4, rows1, picked, ids, book, quant_error)
+    quant_error = last_errors(4, 8, rows1, picked, ids, book, quant_error)
     return quant_error, spread.reshape(16, 16, CODES)
 
 

time: 187 us -> 187 us (level)
  no operation moved by 1% of the time
where the time goes in v8:
time: 187 us; the launch traced here: 186 us
  Pallas kernels  109 us (58%)
  waiting for transfers between devices  44 us (24%)
  starting transfers between devices  29.7 us (16%)
    all_to_all x4, waiting for transfers between devices, exchange(): return lax.all_to_all(x, axes, split_axis=0, concat_axis=0, tiled=True)  44 us
    all_to_all x4, starting transfers between devices, exchange(): return lax.all_to_all(x, axes, split_axis=0, concat_axis=0, tiled=True)  29.7 us
    pallas_call x2, Pallas kernels, route(): pl.pallas_call(functools.partial(route_kernel, half, parts, row_steps, st...  26 us
    pallas_call x1, Pallas kernels, first_half(): pl.pallas_call(functools.partial(first_half_kernel, slots), grid=(SOURCES...  25.9 us
    pallas_call x2, Pallas kernels, last_errors(): pl.pallas_call(functools.partial(last_errors_kernel, slots), grid=(end -...  24.1 us
    pallas_call x1, Pallas kernels, pick(): pl.pallas_call(functools.partial(pick_kernel, step_sources), grid=(SOURCE...  21.8 us
    pallas_call x1, Pallas kernels, last_sums(): pl.pallas_call(functools.partial(last_sums_kernel, slots), grid=(SOURCES...  8.6 us
  transfers between devices with their start and end apart: 4, of which 2 were waited for; matrix products, arithmetic and copies ran while one was open for 0% of the time, Pallas kernels for 47%

profile of v8, /device:TPU:1, one launch (start us, length us, event | category | flops | bytes accessed | tf_op | source)
XLA Modules:
  0.0 186.0 jit_solution(9563757639545101519)
XLA Ops:
  0.6 13.2 %shard_map.86 = (bf16[4,32,136,128]{3,2,1,0:T(8,128)(2,1)}, s32[1,2048]{1,0:T(1,128)}, s32[32,128]{1,0:T(8,128)}) custom-call(s32[1,2048]{1,0:T(1,128)} %bitcast.19, s32[1,2048]{1,0:T(1,128)} %bitcast.20, bf16[2048,1024]{1,0:T(8,128)(2,1)} %refs_2_.3, bf16[1024,1024]{1,0:T(8,128)(2,1)} %refs_3_.3), custom_call_target="tpu_custom_call" | custom-call | flops 8000000000 | bytes 10485760 | tf_op jit(solution)/shard_map/pallas_call | solution.py:197
  13.8 11.9 %all-to-all-start.1 = ((bf16[128,136,128]{2,1,0:T(8,128)(2,1)}), bf16[128,136,128]{2,1,0:T(8,128)(2,1)}, u32[]{:S(2)}, u32[]{:S(2)}) async-start(bf16[128,136,128]{2,1,0:T(8,128)(2,1)} %bitcast.14), calls=%async_computation.1 | async-start | bytes 8912896 | tf_op jit(solution)/shard_map/all_to_all | solution.py:477
  25.7 2.9 %shard_map.88.book_ref = bf16[4096,256]{1,0:T(8,128)(2,1)} custom-call(bf16[256,256]{1,0:T(8,128)(2,1)} %bitcast.17), custom_call_target="tpu_custom_call" | custom-call | flops 1000000000 | bytes 3145728 | tf_op jit(solution)/shard_map/pallas_call | solution.py:274
  28.6 0.7 convert_bitcast_fusion
  29.3 12.9 %shard_map.87 = bf16[4,32,128,128]{3,2,1,0:T(8,128)(2,1)} custom-call(s32[32,128]{1,0:T(8,128)} %get-tuple-element.18.refs_0_, s32[1,2048]{1,0:T(1,128)} %get-tuple-element.19.refs_1_, bf16[2048,1024]{1,0:T(8,128)(2,1)} %refs_2_.3, bf16[1024,1024]{1,0:T(8,128)(2,1)} %refs_3_.3), custom_call_target="tpu_custom_call" | custom-call | flops 8000000000 | bytes 10485760 | tf_op jit(solution)/shard_map/pallas_call | solution.py:197
  42.2 39.0 %all-to-all-done.1.tail_ref.rows_ref = bf16[128,136,128]{2,1,0:T(8,128)(2,1)} async-done(((bf16[128,136,128]{2,1,0:T(8,128)(2,1)}), bf16[128,136,128]{2,1,0:T(8,128)(2,1)}, u32[]{:S(2)}, u32[]{:S(2)}) %all-to-all-start.1) | async-done | bytes 4456480 | tf_op jit(solution)/shard_map/all_to_all | solution.py:477
  81.2 5.8 %all-to-all-start = ((bf16[128,128,128]{2,1,0:T(8,128)(2,1)}), bf16[128,128,128]{2,1,0:T(8,128)(2,1)}, u32[]{:S(2)}, u32[]{:S(2)}) async-start(bf16[128,128,128]{2,1,0:T(8,128)(2,1)} %bitcast.15), calls=%async_computation | async-start | bytes 8388608 | tf_op jit(solution)/shard_map/all_to_all | solution.py:477
  87.0 21.8 %shard_map.89 = (bf16[128,128,256]{2,1,0:T(8,128)(2,1)}, f32[1,16384]{1,0:T(1,128)}) custom-call(bf16[128,136,128]{2,1,0:T(8,128)(2,1)} %all-to-all-done.1.tail_ref.rows_ref, bf16[2048,256]{1,0:T(8,128)(2,1)} %centroid_ref.1), custom_call_target="tpu_custom_call" | custom-call | flops 17999998976 | bytes 14680064 | tf_op jit(solution)/shard_map/pallas_call | solution.py:237
  108.7 25.9 %shard_map.90 = (f32[16,16384]{1,0:T(8,128)}, f32[8,16,256]{2,1,0:T(8,128)}, f32[8,256]{1,0:T(8,128)}) custom-call(bf16[128,136,128]{2,1,0:T(8,128)(2,1)} %all-to-all-done.1.tail_ref.rows_ref, bf16[128,128,256]{2,1,0:T(8,128)(2,1)} %get-tuple-element.22.pick_ref, f32[1,16384]{1,0:T(1,128)} %get-tuple-element.23.ids_ref, s32[16,16384]{1,0:T(8,128)} %target_ref.3, ...), custom_call_target="tpu_custom_call" | custom-call | flops 22000001024 | bytes 10485760 | tf_op jit(solution)/shard_map/pallas_call | solution.py:376
  134.7 5.0 %all-to-all-done.rows_ref = bf16[128,128,128]{2,1,0:T(8,128)(2,1)} async-done(((bf16[128,128,128]{2,1,0:T(8,128)(2,1)}), bf16[128,128,128]{2,1,0:T(8,128)(2,1)}, u32[]{:S(2)}, u32[]{:S(2)}) %all-to-all-start) | async-done | bytes 4194336 | tf_op jit(solution)/shard_map/all_to_all | solution.py:477
  139.7 8.6 %shard_map.91 = f32[32,24,128]{2,1,0:T(8,128)} custom-call(bf16[128,128,128]{2,1,0:T(8,128)(2,1)} %all-to-all-done.rows_ref, bf16[128,128,256]{2,1,0:T(8,128)(2,1)} %get-tuple-element.22.pick_ref, f32[1,16384]{1,0:T(1,128)} %get-tuple-element.23.ids_ref, s32[16,16384]{1,0:T(8,128)} %target_ref.3, f32[8,16,256]{2,1,0:T(8,128)} %get-tuple-element.29.sum_ref, ...), custom_call_target="tpu_custom_call" | custom-call | flops 4000000000 | bytes 9437184 | tf_op jit(solution)/shard_map/pallas_call | solution.py:423
  148.3 4.6 %all-to-all-start.2 = ((f32[32,24,128]{2,1,0:T(8,128)}), f32[32,24,128]{2,1,0:T(8,128)S(1)}, u32[]{:S(2)}, u32[]{:S(2)}) async-start(f32[32,24,128]{2,1,0:T(8,128)} %shard_map.91), calls=%async_computation.2 | async-start | bytes 786432 | tf_op jit(solution)/shard_map/all_to_all | solution.py:477
  152.9 12.1 %shard_map.92.before_ref = f32[16,16384]{1,0:T(8,128)} custom-call(bf16[128,128,128]{2,1,0:T(8,128)(2,1)} %all-to-all-done.rows_ref, bf16[128,128,256]{2,1,0:T(8,128)(2,1)} %get-tuple-element.22.pick_ref, f32[1,16384]{1,0:T(1,128)} %get-tuple-element.23.ids_ref, bf16[4096,256]{1,0:T(8,128)(2,1)} %shard_map.88.book_ref, ...), custom_call_target="tpu_custom_call", output_to_operand_aliasing={{}: (4, {})} | custom-call | flops 8800000000 | bytes 6291456 | tf_op jit(solution)/shard_map/pallas_call | solution.py:456
  164.9 0.0 all-to-all-done.2
  165.0 0.7 broadcast_in_dim.2
  165.8 7.5 %all-to-all-start.3 = ((f32[32,8,256]{2,1,0:T(8,128)}), f32[32,8,256]{2,1,0:T(8,128)S(1)}, u32[]{:S(2)}, u32[]{:S(2)}) async-start(f32[32,8,256]{2,1,0:T(8,128)} %broadcast_in_dim.2), calls=%async_computation.3 | async-start | bytes 524288 | tf_op jit(solution)/shard_map/all_to_all | solution.py:477
  173.3 12.1 %shard_map.93 = f32[16,16384]{1,0:T(8,128)} custom-call(bf16[128,128,128]{2,1,0:T(8,128)(2,1)} %all-to-all-done.rows_ref, bf16[128,128,256]{2,1,0:T(8,128)(2,1)} %get-tuple-element.22.pick_ref, f32[1,16384]{1,0:T(1,128)} %get-tuple-element.23.ids_ref, bf16[4096,256]{1,0:T(8,128)(2,1)} %shard_map.88.book_ref, ...), custom_call_target="tpu_custom_call", output_to_operand_aliasing={{}: (4, {})} | custom-call | flops 8800000000 | bytes 6291456 | tf_op jit(solution)/shard_map/pallas_call | solution.py:456
  185.3 0.0 all-to-all-done.3
  185.3 0.7 copy.14
  (4 shorter events, 0.1 us)
Async XLA Ops:
  13.8 67.4 %all-to-all-start.1 = ((bf16[128,136,128]{2,1,0:T(8,128)(2,1)}), bf16[128,136,128]{2,1,0:T(8,128)(2,1)}, u32[]{:S(2)}, u32[]{:S(2)}) async-start(bf16[128,136,128]{2,1,0:T(8,128)(2,1)} %bitcast.14), calls=%async_computation.1 | async-start | bytes 8912896 | tf_op jit(solution)/shard_map/all_to_all | solution.py:477
  81.2 58.5 %all-to-all-start = ((bf16[128,128,128]{2,1,0:T(8,128)(2,1)}), bf16[128,128,128]{2,1,0:T(8,128)(2,1)}, u32[]{:S(2)}, u32[]{:S(2)}) async-start(bf16[128,128,128]{2,1,0:T(8,128)(2,1)} %bitcast.15), calls=%async_computation | async-start | bytes 8388608 | tf_op jit(solution)/shard_map/all_to_all | solution.py:477
  148.3 16.6 %all-to-all-start.2 = ((f32[32,24,128]{2,1,0:T(8,128)}), f32[32,24,128]{2,1,0:T(8,128)S(1)}, u32[]{:S(2)}, u32[]{:S(2)}) async-start(f32[32,24,128]{2,1,0:T(8,128)} %shard_map.91), calls=%async_computation.2 | async-start | bytes 786432 | tf_op jit(solution)/shard_map/all_to_all | solution.py:477
  165.8 19.6 %all-to-all-start.3 = ((f32[32,8,256]{2,1,0:T(8,128)}), f32[32,8,256]{2,1,0:T(8,128)S(1)}, u32[]{:S(2)}, u32[]{:S(2)}) async-start(f32[32,8,256]{2,1,0:T(8,128)} %broadcast_in_dim.2), calls=%async_computation.3 | async-start | bytes 524288 | tf_op jit(solution)/shard_map/all_to_all | solution.py:477
